TPU v7x, 128 devices: a whole 4x4x4 slice. The times are simulated.
128 devices in a mesh: role: 2 (over core), shard: 64 (over z, x, y).
Axes of the slice: x: 4, y: 4, z: 4, core: 2. Of those that a mesh axis runs over, the one named last changes fastest.
Arguments:
- emb_table: float32 [262144, 512], P(('role', 'shard')), may hold values from -3 to 3
- row_accum: float32 [262144], P(('role', 'shard')), may hold values from 1e-05 to 0.001
- owners: int32 [16384, 4, 1], P(('role', 'shard')), may hold values from 0 to 127; in each aligned block of 512 rows (0 to 511, 512 to 1023, ..., all dimensions but the last counted through in order) at most 8 rows name the same one
- local_rows: int32 [16384, 4, 4], P(('role', 'shard')), may hold values from 0 to 2047
- lengths: int32 [16384, 4], P(('role', 'shard')), may hold values from 1 to 4
- labels: int32 [16384], P(('role', 'shard')), may hold values 0 or 1
- w_hidden: bfloat16 [2048, 2048], replicated, may hold values from -0.125 to 0.125
- hidden_bias: float32 [2048], replicated, may hold values from -3 to 3
- w_logit: float32 [2048], replicated, may hold values from -0.125 to 0.125
Outputs:
- new_table: float32 [262144, 512], P(('role', 'shard'))
- w_grad: float32 [2048, 2048], P(('role', 'shard'))
Inputs may be any that keep to these rules, and one draw needn't show every extreme that they name: `owners`: among the 512 bags of one device's samples, at most 8 name one owner, a bound that some block reaches.
All inputs are finite; a program needn't handle non-finite values. No bound on the sum of `labels` on one device may be relied on, other than what follows from the above.
Results may differ from a plain program's by a relative error of at most 0.00055.
The roundings to bfloat16 on the way count: a program that leaves them out, or rounds other values in their place, can miss the bound.
Values may be sent and summed in bfloat16 or wider, within the bound.
No kernel may reach another device: no remote copies, remote signals or barrier semaphores. Data moves between devices by JAX's collectives and lax.ppermute only.
A program may use at most 128 MiB of HBM per device.

v0:
```python
import jax
import jax.numpy as jnp
from jax import lax
from jax.sharding import PartitionSpec as P

learn_rate = 0.1


def per_device(
    emb_table, row_accum, owners, local_rows, lengths, labels, w_hidden, hidden_bias, w_logit
):
    devices = lax.axis_size(("role", "shard"))
    samples, features, bag_len = local_rows.shape
    rows_dev, width = emb_table.shape
    bags = samples * features
    capacity = 2 * bags // devices
    owner_flat = owners.reshape(bags)
    live = jnp.arange(bag_len, dtype=jnp.int32)[None, None, :] < lengths[:, :, None]
    wanted = jnp.where(live, local_rows, -1).reshape(bags, bag_len)
    chosen = (owner_flat[:, None] == jnp.arange(devices, dtype=jnp.int32)[None, :]).astype(
        jnp.int32
    )
    earlier = jnp.cumsum(chosen, axis=0) - chosen
    rank = jnp.sum(earlier * chosen, axis=1)
    target = owner_flat * capacity + rank
    outgoing = jnp.full((devices * capacity, bag_len), -1, jnp.int32).at[target].set(wanted)
    outgoing = outgoing.reshape(devices, capacity, bag_len)
    table_bf = emb_table.astype(jnp.bfloat16)
    incoming = lax.all_to_all(outgoing, ("role", "shard"), split_axis=0, concat_axis=0, tiled=True)
    valid = incoming >= 0
    fetched = table_bf[jnp.maximum(incoming, 0)]
    fetched = jnp.where(valid[..., None], fetched, jnp.zeros((), jnp.bfloat16))
    answer = lax.all_to_all(fetched, ("role", "shard"), split_axis=0, concat_axis=0, tiled=True)
    returned, incoming = (answer, incoming)
    pooled_slots = jnp.sum(returned, axis=2, dtype=jnp.float32).astype(jnp.bfloat16)
    pooled = pooled_slots.reshape(devices * capacity, width)[target].reshape(
        samples, features * width
    )
    pre = jnp.dot(pooled, w_hidden, preferred_element_type=jnp.float32) + hidden_bias
    act = jax.nn.silu(pre)
    logit = jnp.dot(act, w_logit, precision=lax.Precision.HIGHEST)
    dlogit = jax.nn.sigmoid(logit) - labels.astype(jnp.float32)
    sig = jax.nn.sigmoid(pre)
    dpre = (dlogit[:, None] * w_logit[None, :] * sig * (1.0 + pre * (1.0 - sig))).astype(
        jnp.bfloat16
    )
    dpooled = lax.dot_general(
        dpre, w_hidden, (((1,), (1,)), ((), ())), preferred_element_type=jnp.float32
    ).astype(jnp.bfloat16)
    sending = (
        jnp.zeros((devices * capacity, width), jnp.bfloat16)
        .at[target]
        .set(dpooled.reshape(bags, width))
    )
    received = lax.all_to_all(
        sending.reshape(devices, capacity, width),
        ("role", "shard"),
        split_axis=0,
        concat_axis=0,
        tiled=True,
    )
    w_grad = lax.psum_scatter(
        lax.dot_general(pooled, dpre, (((0,), (0,)), ((), ())), preferred_element_type=jnp.float32),
        ("role", "shard"),
        scatter_dimension=0,
        tiled=True,
    )
    slot_grads = received.reshape(devices * capacity, width)
    row_grad = jnp.zeros((rows_dev, width), jnp.float32)
    for slot in range(bag_len):
        slot_ids = incoming[:, :, slot].reshape(devices * capacity)
        slot_data = jnp.where(
            (slot_ids >= 0)[:, None], slot_grads.astype(jnp.float32), jnp.float32(0.0)
        )
        row_grad = row_grad.at[jnp.maximum(slot_ids, 0)].add(slot_data)
    new_accum = row_accum + jnp.mean(row_grad * row_grad, axis=1)
    new_table = emb_table - learn_rate * row_grad / jnp.sqrt(new_accum + 1e-06)[:, None]
    return (new_table, w_grad)


def solution(mesh):
    placed = (
        P(("role", "shard"), None),
        P(("role", "shard")),
        P(("role", "shard"), None, None),
        P(("role", "shard"), None, None),
        P(("role", "shard"), None),
        P(("role", "shard")),
        P(),
        P(),
        P(),
    )
    return jax.shard_map(
        per_device,
        mesh=mesh,
        in_specs=placed,
        out_specs=(P(("role", "shard"), None), P(("role", "shard"), None)),
        check_vma=False,
    )
```

profile of v0, /device:TPU:0, one launch (start us, length us, event | category | flops | bytes accessed | tf_op | source)
XLA Modules:
  0.0 834.2 jit_solution(2849887354016100633)
XLA Ops:
  10.6 1.8 scatter_custom_fusion
  14.0 11.1 %all-to-all-start = ((s32[128,8,4]{1,2,0:T(4,128)}), s32[128,8,4]{1,2,0:T(4,128)S(1)}, u32[]{:S(2)}, u32[]{:S(2)}) async-start(s32[128,8,4]{1,2,0:T(4,128)} %copy.48), calls=%async_computation | async-start | bytes 524288 | tf_op jit(solution)/shard_map/all_to_all | solution.py:29
  25.2 2.5 convert_element_type.32
  27.6 7.8 all-to-all-done
  36.4 17.3 %gather_fusion = bf16[4096,512]{1,0:T(8,128)(2,1)} fusion(bf16[2048,512]{1,0:T(8,128)(2,1)S(1)} %convert_element_type.32, s32[4096]{0:T(1024)S(1)} %broadcast_clamp_fusion), kind=kCustom, calls=%fused_computation | custom fusion | bytes 8404992 | tf_op jit(solution)/shard_map/gather | solution.py:31
  53.7 6.9 reshape.162
  60.6 5.8 broadcast_select_fusion
  66.4 5.8 all-to-all-start.1
  72.3 52.6 %all-to-all-done.1 = bf16[128,8,4,512]{3,2,1,0:T(4,128)(2,1)} async-done(((bf16[128,8,4,512]{3,2,1,0:T(4,128)(2,1)}), bf16[128,8,4,512]{3,2,1,0:T(4,128)(2,1)}, u32[]{:S(2)}, u32[]{:S(2)}) %all-to-all-start.1) | async-done | bytes 4194336 | tf_op jit(solution)/shard_map/all_to_all | solution.py:33
  125.0 7.5 reduce_sum.34
  132.5 2.2 gather_fusion.1
  135.0 4.6 convolution_add_fusion
  140.8 8.3 fusion.35
  149.1 6.3 convolution_convert_fusion
  155.7 3.5 scatter_custom_fusion.1
  159.2 7.3 all-to-all-start.2
  169.1 17.6 %all-to-all-done.2 = bf16[128,8,512]{2,1,0:T(8,128)(2,1)S(1)} async-done(((bf16[128,8,512]{2,1,0:T(8,128)(2,1)}), bf16[128,8,512]{2,1,0:T(8,128)(2,1)S(1)}, u32[]{:S(2)}, u32[]{:S(2)}) %all-to-all-start.2) | async-done | bytes 1048608 | tf_op jit(solution)/shard_map/all_to_all | solution.py:55
  186.8 9.4 %scatter_custom_fusion.2 = f32[2048,512]{1,0:T(8,128)} fusion(s32[1024]{0:T(1024)S(1)} %reshape.195, f32[]{:T(128)} %constant.11.clone.1, bf16[128,8,512]{2,1,0:T(8,128)(2,1)S(1)} %all-to-all-done.2, pred[1024]{0:T(1024)(128)(4,1)S(1)} %ge.44), kind=kCustom, calls=%fused_computation.17 | custom fusion | flops 1572864 | bytes 5244928 | tf_op jit(solution)/shard_map/scatter-add | solution.py:75
  196.2 11.4 %scatter_custom_fusion.3 = f32[2048,512]{1,0:T(8,128)} fusion(f32[2048,512]{1,0:T(8,128)} %scatter_custom_fusion.2, s32[1024]{0:T(1024)S(1)} %reshape.203, bf16[128,8,512]{2,1,0:T(8,128)(2,1)S(1)} %all-to-all-done.2, f32[]{:T(128)} %constant.11.clone.1, pred[1024]{0:T(1024)(128)(4,1)S(1)} %ge.47), kind=kCustom, calls=%fused_computation.18 | custom fusion | flops 1572864 | bytes 5244416 | tf_op jit(solution)/shard_map/scatter-add | solution.py:75
  207.6 11.4 %scatter_custom_fusion.4 = f32[2048,512]{1,0:T(8,128)} fusion(f32[2048,512]{1,0:T(8,128)} %scatter_custom_fusion.3, s32[1024]{0:T(1024)S(1)} %reshape.211, bf16[128,8,512]{2,1,0:T(8,128)(2,1)S(1)} %all-to-all-done.2, f32[]{:T(128)} %constant.11.clone.1, pred[1024]{0:T(1024)(128)(4,1)S(1)} %ge.49), kind=kCustom, calls=%fused_computation.19 | custom fusion | flops 1572864 | bytes 5244416 | tf_op jit(solution)/shard_map/scatter-add | solution.py:75
  219.0 11.8 %scatter_custom_fusion.5 = f32[2048,512]{1,0:T(8,128)} fusion(f32[2048,512]{1,0:T(8,128)} %scatter_custom_fusion.4, s32[1024]{0:T(1024)S(1)} %reshape.219, bf16[128,8,512]{2,1,0:T(8,128)(2,1)S(1)} %all-to-all-done.2, f32[]{:T(128)} %constant.11.clone.1, pred[1024]{0:T(1024)(128)(4,1)S(1)} %ge.51), kind=kCustom, calls=%fused_computation.20 | custom fusion | flops 1572864 | bytes 5244416 | tf_op jit(solution)/shard_map/scatter-add | solution.py:75
  230.8 2.7 multiply_reduce_fusion
  234.3 4.9 divide_subtract_fusion
  239.2 588.2 %reduce-scatter.2.cloned.1.call-done = f32[16,2048]{1,0:T(8,128)} async-done(((f32[2048,2048]{1,0:T(8,128)}), f32[16,2048]{1,0:T(8,128)}) %reduce-scatter.2.cloned.1.call-update) | async-done | bytes 131088 | tf_op jit(solution)/shard_map/reduce_scatter | solution.py:62
  (53 shorter events, 11.1 us)
Async XLA Ops:
  14.0 21.4 %all-to-all-start = ((s32[128,8,4]{1,2,0:T(4,128)}), s32[128,8,4]{1,2,0:T(4,128)S(1)}, u32[]{:S(2)}, u32[]{:S(2)}) async-start(s32[128,8,4]{1,2,0:T(4,128)} %copy.48), calls=%async_computation | async-start | bytes 524288 | tf_op jit(solution)/shard_map/all_to_all | solution.py:29
  66.4 58.5 %all-to-all-start.1 = ((bf16[128,8,4,512]{3,2,1,0:T(4,128)(2,1)}), bf16[128,8,4,512]{3,2,1,0:T(4,128)(2,1)}, u32[]{:S(2)}, u32[]{:S(2)}) async-start(bf16[128,8,4,512]{3,2,1,0:T(4,128)(2,1)} %broadcast_select_fusion), calls=%async_computation.1 | async-start | bytes 8388608 | tf_op jit(solution)/shard_map/all_to_all | solution.py:33
  72.3 755.1 %reduce-scatter.2.cloned.1.call-start = ((), (), s32[]{:S(2)}) async-start(), calls=%async_computation.4 | async-start | bytes 16908288 | tf_op jit(solution)/shard_map/reduce_scatter | solution.py:62
  132.5 2.5 copy-start.1
  135.0 4.7 copy-start.2
  135.0 4.7 copy-start.4
  159.2 27.6 %all-to-all-start.2 = ((bf16[128,8,512]{2,1,0:T(8,128)(2,1)}), bf16[128,8,512]{2,1,0:T(8,128)(2,1)S(1)}, u32[]{:S(2)}, u32[]{:S(2)}) async-start(bf16[128,8,512]{2,1,0:T(8,128)(2,1)} %bitcast.10), calls=%async_computation.2 | async-start | bytes 2097152 | tf_op jit(solution)/shard_map/all_to_all | solution.py:55
  219.0 14.5 %copy-start.3 = (f32[2048]{0:T(1024)S(1)}, f32[2048]{0:T(1024)}, u32[]{:S(2)}) copy-start(f32[2048]{0:T(1024)} %param.10) | copy-start | bytes 24580
  230.8 3.5 copy-start
Sparse Core Ops, SparseCore 0:
  149.2 678.1 reduce-scatter.1
where the time goes:
time: 836 us; the launch traced here: 834 us
  waiting for transfers between devices  666 us (80%)
  other arithmetic  71.2 us (9%)
  local copies, waits for them, and re-layouts  37.9 us (5%)
  starting transfers between devices  24.4 us (3%)
  matrix products  20.3 us (2%)
  between operations  14.3 us (2%)
    reduce_scatter x1, waiting for transfers between devices, per_device(): lax.psum_scatter(lax.dot_general(pooled, dpre, (((0,), (0,)), ((), ())),...  588 us
    all_to_all x1, waiting for transfers between devices, per_device(): lax.all_to_all(fetched, ('role', 'shard'), split_axis=0, concat_axis=0, t...  52.6 us
    scatter-add x4, other arithmetic, per_device(): row_grad = row_grad.at[jnp.maximum(slot_ids, 0)].add(slot_data)  44 us
    gather x2, local copies, waits for them, and re-layouts, per_device(): fetched = table_bf[jnp.maximum(incoming, 0)]  24.3 us
    all_to_all x1, waiting for transfers between devices, per_device(): lax.all_to_all(sending.reshape(devices, capacity, width), ('role', 'shard...  17.6 us
  transfers between devices with their start and end apart: 4, of which 4 were waited for; matrix products, arithmetic and copies ran while one was open for 8% of the time, Pallas kernels for 0%

commit v1 on v0

v1 whole, which is shorter than its diff:
```python
import jax
import jax.numpy as jnp
from jax import lax
from jax.experimental import pallas as pl
from jax.experimental.pallas import tpu as pltpu
from jax.sharding import Mesh, PartitionSpec as P

learn_rate = 0.1
AXES = ("role", "z", "x", "y")
BF = jnp.bfloat16
F32 = jnp.float32
I32 = jnp.int32


def iota(shape, dim):
    return lax.broadcasted_iota(I32, shape, dim)


def dot(a, b):
    return jnp.dot(a, b, preferred_element_type=F32)


def params(mib):
    return pltpu.CompilerParams(vmem_limit_bytes=mib << 20)


def split_int(v):
    return (v >> 6).astype(F32).astype(BF), (v & 63).astype(F32).astype(BF)


def route_kernel(own_c, own_r, rows, lens, out, tgt_c, tgt_r):
    samples, features = own_c.shape
    bag_len = rows.shape[1] // features
    devices, width = out.shape
    cap = width // bag_len
    bags = samples * features
    lane = iota((samples, devices), 1)
    sub = iota((devices, samples), 0)
    hot = jnp.concatenate(
        [(own_c[:, f : f + 1] == lane).astype(F32) for f in range(features)], axis=0
    )
    hot_t = jnp.concatenate(
        [(own_r[f : f + 1, :] == sub).astype(F32) for f in range(features)], axis=1
    )
    lower = (iota((bags, bags), 1) < iota((bags, bags), 0)).astype(F32).astype(BF)
    upper = (iota((bags, bags), 0) < iota((bags, bags), 1)).astype(F32).astype(BF)
    hot_t_bf = hot_t.astype(BF)
    rank_c = jnp.sum(dot(lower, hot.astype(BF)) * hot, axis=1, keepdims=True).astype(I32)
    rank_r = jnp.sum(dot(hot_t_bf, upper) * hot_t, axis=0, keepdims=True).astype(I32)
    column = iota((samples, width), 1)
    his, los = [], []
    for f in range(features):
        rank = rank_c[f * samples : (f + 1) * samples]
        wanted = jnp.zeros((samples, width), I32)
        for j in range(bag_len):
            k = f * bag_len + j
            live = j < lens[:, f : f + 1]
            value = jnp.where(live, rows[:, k : k + 1] + 1, 0)
            wanted = jnp.where(column == j * cap + rank, value, wanted)
        hi, lo = split_int(wanted)
        his.append(hi)
        los.append(lo)
        tgt_c[:, f : f + 1] = own_c[:, f : f + 1] * cap + rank
        tgt_r[f : f + 1, :] = (
            own_r[f : f + 1, :] * cap + rank_r[:, f * samples : (f + 1) * samples]
        )
    hi = dot(hot_t_bf, jnp.concatenate(his, axis=0)).astype(I32)
    lo = dot(hot_t_bf, jnp.concatenate(los, axis=0)).astype(I32)
    out[...] = hi * 64 + lo - 1


def route(own_c, own_r, rows, lens, devices, cap):
    samples, features = own_c.shape
    bag_len = rows.shape[1] // features
    return pl.pallas_call(
        route_kernel,
        out_shape=(
            jax.ShapeDtypeStruct((devices, bag_len * cap), I32),
            jax.ShapeDtypeStruct((samples, features), I32),
            jax.ShapeDtypeStruct((features, samples), I32),
        ),
        compiler_params=params(16),
    )(own_c, own_r, rows, lens)


def lookup_kernel(bag_len, ids, table, out):
    sources, width = ids.shape
    cap = width // bag_len
    slots = sources * cap
    depth = table.shape[0]
    hi, lo = split_int(ids[...] + 1)
    rep = (iota((slots, sources), 0) // cap == iota((slots, sources), 1)).astype(F32).astype(BF)
    mine = (iota((slots, width), 1) % cap == iota((slots, width), 0) % cap).astype(F32)
    spread = iota((width, bag_len * 128), 0) // cap == iota((width, bag_len * 128), 1) // 128
    spread = spread.astype(F32).astype(BF)
    hi = dot((dot(rep, hi) * mine).astype(BF), spread)
    lo = dot((dot(rep, lo) * mine).astype(BF), spread)
    wanted = hi * 64.0 + lo - 1.0
    lane = iota((slots, 128), 1).astype(F32)
    pieces = []
    for k in range(depth // 128):
        count = jnp.zeros((slots, 128), F32)
        for j in range(bag_len):
            count += (wanted[:, j * 128 : (j + 1) * 128] == lane + (128.0 * k)).astype(F32)
        pieces.append(count.astype(BF))
    out[...] = dot(jnp.concatenate(pieces, axis=1), table[...]).astype(BF)


def lookup(ids, table, bag_len):
    sources, width = ids.shape
    depth, wide = table.shape
    cap = width // bag_len
    block = 32
    return pl.pallas_call(
        lambda *refs: lookup_kernel(bag_len, *refs),
        grid=(sources // block,),
        in_specs=[
            pl.BlockSpec((block, width), lambda i: (i, 0)),
            pl.BlockSpec((depth, wide), lambda i: (0, 0)),
        ],
        out_specs=pl.BlockSpec((block * cap, wide), lambda i: (i, 0)),
        out_shape=jax.ShapeDtypeStruct((sources * cap, wide), BF),
        compiler_params=params(32),
        cost_estimate=pl.CostEstimate(
            flops=2 * sources * cap * depth * wide, bytes_accessed=4 << 20, transcendentals=0
        ),
    )(ids, table)


def dense_kernel(
    slots, tgt_c, tgt_r, labels, bias, head, w_hbm, pooled, dpre_out, sending, w, sems
):
    samples, features = tgt_c.shape
    total, wide = slots.shape
    copies = []
    for f in range(features):
        part = pl.ds(f * wide, wide)
        copies.append(pltpu.make_async_copy(w_hbm.at[part], w.at[part], sems.at[f]))
        copies[-1].start()
    lane = iota((samples, total), 1)
    pre = bias[...]
    for f in range(features):
        pick = (tgt_c[:, f : f + 1] == lane).astype(F32).astype(BF)
        bag = dot(pick, slots[...]).astype(BF)
        pooled[:, f * wide : (f + 1) * wide] = bag
        copies[f].wait()
        pre = pre + dot(bag, w[f * wide : (f + 1) * wide, :])
    sig = jax.nn.sigmoid(pre)
    logit = jnp.sum(pre * sig * head[...], axis=1, keepdims=True)
    dlogit = jax.nn.sigmoid(logit) - labels[...].astype(F32)
    dpre = (dlogit * head[...] * sig * (1.0 + pre * (1.0 - sig))).astype(BF)
    dpre_out[...] = dpre
    sub = iota((total, samples), 0)
    acc = jnp.zeros((total, wide), F32)
    for f in range(features):
        grad = lax.dot_general(
            dpre,
            w[f * wide : (f + 1) * wide, :],
            (((1,), (1,)), ((), ())),
            preferred_element_type=F32,
        ).astype(BF)
        put = (tgt_r[f : f + 1, :] == sub).astype(F32).astype(BF)
        acc += dot(put, grad)
    sending[...] = acc.astype(BF)


def dense(slots, tgt_c, tgt_r, labels, bias, head, w):
    samples, features = tgt_c.shape
    total, wide = slots.shape
    hidden = w.shape[1]
    vmem = pl.BlockSpec(memory_space=pltpu.VMEM)
    return pl.pallas_call(
        dense_kernel,
        in_specs=[vmem] * 6 + [pl.BlockSpec(memory_space=pl.ANY)],
        out_specs=[vmem] * 3,
        out_shape=(
            jax.ShapeDtypeStruct((samples, features * wide), BF),
            jax.ShapeDtypeStruct((samples, hidden), BF),
            jax.ShapeDtypeStruct((total, wide), BF),
        ),
        scratch_shapes=[
            pltpu.VMEM(w.shape, BF),
            pltpu.SemaphoreType.DMA((features,)),
        ],
        compiler_params=params(40),
        cost_estimate=pl.CostEstimate(
            flops=6 * samples * w.size, bytes_accessed=12 << 20, transcendentals=0
        ),
    )(slots, tgt_c, tgt_r, labels, bias, head, w)


def counts_kernel(ids, out):
    block, slots = out.shape
    bag_len = ids.shape[0]
    row = iota((block, slots), 0) + pl.program_id(0) * block
    count = jnp.zeros((block, slots), F32)
    for j in range(bag_len):
        count += (ids[j : j + 1, :] == row).astype(F32)
    out[...] = count.astype(BF)


def counts(ids, rows):
    bag_len, slots = ids.shape
    block = 256
    return pl.pallas_call(
        counts_kernel,
        grid=(rows // block,),
        in_specs=[pl.BlockSpec((bag_len, slots), lambda i: (0, 0))],
        out_specs=pl.BlockSpec((block, slots), lambda i: (i, 0)),
        out_shape=jax.ShapeDtypeStruct((rows, slots), BF),
        compiler_params=params(16),
        cost_estimate=pl.CostEstimate(
            flops=8 * rows * slots, bytes_accessed=2 * rows * slots, transcendentals=0
        ),
    )(ids)


def update_kernel(count, grads, table, accum, out):
    row_grad = dot(count[...], grads[...])
    square = jnp.sum(row_grad * row_grad, axis=1, keepdims=True)
    new_accum = accum[:, 0:1] + square * (1.0 / row_grad.shape[1])
    out[...] = table[...] - learn_rate * row_grad / jnp.sqrt(new_accum + 1e-6)


def update(count, grads, table, accum):
    rows, wide = table.shape
    slots = grads.shape[0]
    block = 256
    return pl.pallas_call(
        update_kernel,
        grid=(rows // block,),
        in_specs=[
            pl.BlockSpec((block, slots), lambda i: (i, 0)),
            pl.BlockSpec((slots, wide), lambda i: (0, 0)),
            pl.BlockSpec((block, wide), lambda i: (i, 0)),
            pl.BlockSpec((block, 128), lambda i: (i, 0)),
        ],
        out_specs=pl.BlockSpec((block, wide), lambda i: (i, 0)),
        out_shape=jax.ShapeDtypeStruct((rows, wide), F32),
        compiler_params=params(32),
        cost_estimate=pl.CostEstimate(
            flops=2 * rows * slots * wide, bytes_accessed=13 << 20, transcendentals=0
        ),
    )(count, grads, table, accum)


def per_device(
    emb_table, row_accum, owners, local_rows, lengths, labels, w_hidden, hidden_bias, w_logit
):
    devices = lax.axis_size(AXES)
    samples, features, bag_len = local_rows.shape
    rows_dev, width = emb_table.shape
    cap = 2 * samples * features // devices
    own_c = owners.reshape(samples, features)
    outgoing, tgt_c, tgt_r = route(
        own_c, own_c.T, local_rows.reshape(samples, features * bag_len), lengths, devices, cap
    )
    table_bf = emb_table.astype(BF)
    incoming = lax.all_to_all(outgoing, AXES, split_axis=0, concat_axis=0, tiled=True)
    found = lookup(incoming, table_bf, bag_len)
    slots = lax.all_to_all(
        found.reshape(devices, cap, width), AXES, split_axis=0, concat_axis=0, tiled=True
    )
    ids_r = incoming.reshape(devices, bag_len, cap).transpose(1, 0, 2).reshape(bag_len, -1)
    count = counts(ids_r, rows_dev)
    accum = jnp.broadcast_to(row_accum[:, None], (rows_dev, 128))
    pooled, dpre, sending = dense(
        slots.reshape(devices * cap, width),
        tgt_c,
        tgt_r,
        labels.reshape(samples, 1),
        hidden_bias[None, :],
        w_logit[None, :],
        w_hidden,
    )
    received = lax.all_to_all(
        sending.reshape(devices, cap, width), AXES, split_axis=0, concat_axis=0, tiled=True
    )
    w_grad = lax.dot_general(
        pooled, dpre, (((0,), (0,)), ((), ())), preferred_element_type=F32
    )
    for axis in AXES:
        w_grad = lax.psum_scatter(w_grad, axis, scatter_dimension=0, tiled=True)
    new_table = update(count, received.reshape(devices * cap, width), emb_table, accum)
    return (new_table, w_grad)


def solution(mesh):
    split = Mesh(mesh.devices.reshape(2, 4, 4, 4), AXES)
    placed = (
        P(AXES, None),
        P(AXES),
        P(AXES, None, None),
        P(AXES, None, None),
        P(AXES, None),
        P(AXES),
        P(),
        P(),
        P(),
    )
    return jax.shard_map(
        per_device,
        mesh=split,
        in_specs=placed,
        out_specs=(P(AXES, None), P(AXES, None)),
        check_vma=False,
    )
```

time: 836 us -> 267 us (0.32)
  waiting for transfers between devices: 666 us -> 174 us
  other arithmetic: 71.2 us -> 2.46 us
  Pallas kernels: 0 us -> 29.6 us
  local copies, waits for them, and re-layouts: 37.9 us -> 13.6 us
  matrix products: 20.3 us -> 8.12 us
    reduce_scatter x1 -> x4, waiting for transfers between devices: 588 us -> 150 us  [per_device(): w_grad = lax.psum_scatter(w_grad, axis, scatter_dimension=0, tiled=True)]
    all_to_all x3, waiting for transfers between devices: 78 us -> 24.2 us  [the longest x1 17.6 us: per_device(): lax.all_to_all(found.reshape(devices, cap, width), AXES, split_axis=0, co...]
    scatter-add x4 -> x0, other arithmetic: 44 us -> none  [per_device(): row_grad = row_grad.at[jnp.maximum(slot_ids, 0)].add(slot_data)]
    pallas_call x0 -> x5, Pallas kernels: none -> 29.6 us  [the longest x1 8.89 us: dense(): pl.pallas_call(dense_kernel, in_specs=[vmem] * 6 + [pl.BlockSpec(memory_s...]
    gather x3 -> x0, local copies, waits for them, and re-layouts: 26.4 us -> none  [the longest x2 24.3 us: per_device(): fetched = table_bf[jnp.maximum(incoming, 0)]]
    dot_general x3 -> x0, matrix products: 12 us -> none  [the longest x1 6.3 us: per_device(): lax.dot_general(dpre, w_hidden, (((1,), (1,)), ((), ())), preferred_eleme...]
    reduce_sum x3 -> x0, other arithmetic: 10.5 us -> none  [the longest x1 7.55 us: per_device(): jnp.sum(returned, axis=2, dtype=jnp.float32).astype(jnp.bfloat16)]
    unnamed x12 -> x19, local copies, waits for them, and re-layouts: 1.58 us -> 11.2 us
  transfers between devices with their start and end apart: 4 -> 7, of which waited for: 4 -> 6; matrix products, arithmetic and copies ran while one was open for 8% -> 1% of each run, Pallas kernels for 0% -> 4%
where the time goes in v1:
time: 267 us; the launch traced here: 266 us
  waiting for transfers between devices  174 us (65%)
  Pallas kernels  29.6 us (11%)
  starting transfers between devices  24.4 us (9%)
  between operations  13.9 us (5%)
  local copies, waits for them, and re-layouts  13.6 us (5%)
  matrix products  8.12 us (3%)
    reduce_scatter x4, waiting for transfers between devices, per_device(): w_grad = lax.psum_scatter(w_grad, axis, scatter_dimension=0, tiled=True)  150 us
    all_to_all x1, waiting for transfers between devices, per_device(): lax.all_to_all(found.reshape(devices, cap, width), AXES, split_axis=0, co...  17.6 us
    unnamed x19, local copies, waits for them, and re-layouts  11.2 us
    all_to_all x1, starting transfers between devices, per_device(): lax.all_to_all(outgoing, AXES, split_axis=0, concat_axis=0, tiled=True)  11.1 us
    pallas_call x1, Pallas kernels, dense(): pl.pallas_call(dense_kernel, in_specs=[vmem] * 6 + [pl.BlockSpec(memory_s...  8.89 us
    pallas_call x1, Pallas kernels, lookup(): pl.pallas_call(lambda *refs: lookup_kernel(bag_len, *refs), grid=(sources...  8.34 us
    all_to_all x1, starting transfers between devices, per_device(): lax.all_to_all(sending.reshape(devices, cap, width), AXES, split_axis=0,...  8.26 us
    dot_general x1, matrix products, per_device(): lax.dot_general(pooled, dpre, (((0,), (0,)), ((), ())), preferred_element...  8.12 us
  transfers between devices with their start and end apart: 7, of which 6 were waited for; matrix products, arithmetic and copies ran while one was open for 1% of the time, Pallas kernels for 4%

profile of v1, /device:TPU:0, one launch (start us, length us, event | category | flops | bytes accessed | tf_op | source)
XLA Modules:
  0.0 266.0 jit_solution(1953885434033426711)
XLA Ops:
  7.2 0.8 copy.22.own_c
  8.0 0.8 copy.23.rows
  8.7 0.8 copy.24.lens
  9.5 0.7 copy-done.3
  10.2 2.8 %shard_map.104 = (s32[128,32]{1,0:T(8,128)}, s32[128,4]{1,0:T(8,128)S(1)}, s32[4,128]{1,0:T(4,128)S(1)}) custom-call(s32[128,4]{1,0:T(8,128)S(1)} %copy.22.own_c, s32[4,128]{1,0:T(4,128)S(1)} %bitcast.24, s32[128,16]{1,0:T(8,128)S(1)} %copy.23.rows, s32[128,4]{1,0:T(8,128)S(1)} %copy.24.lens), custom_call_target="tpu_custom_call" | custom-call | tf_op jit(solution)/shard_map/pallas_call | solution.py:75
  13.0 11.1 %all-to-all-start = ((s32[128,1,32]{2,1,0:T(1,128)}), s32[128,1,32]{2,1,0:T(1,128)S(1)}, u32[]{:S(2)}, u32[]{:S(2)}) async-start(s32[128,1,32]{2,1,0:T(1,128)} %bitcast.4), calls=%async_computation | async-start | bytes 131072 | tf_op jit(solution)/shard_map/all_to_all | solution.py:259
  24.1 2.5 convert_element_type.3.refs_1_
  26.6 6.6 %all-to-all-done = s32[128,1,32]{2,1,0:T(1,128)S(1)} async-done(((s32[128,1,32]{2,1,0:T(1,128)}), s32[128,1,32]{2,1,0:T(1,128)S(1)}, u32[]{:S(2)}, u32[]{:S(2)}) %all-to-all-start) | async-done | bytes 16416 | tf_op jit(solution)/shard_map/all_to_all | solution.py:259
  33.2 8.3 %shard_map.106 = bf16[1024,512]{1,0:T(8,128)(2,1)} custom-call(s32[128,32]{1,0:T(8,128)S(1)} %bitcast.22, bf16[2048,512]{1,0:T(8,128)(2,1)S(1)} %convert_element_type.3.refs_1_), custom_call_target="tpu_custom_call" | custom-call | flops 2147483648 | bytes 4194304 | tf_op jit(solution)/shard_map/pallas_call | solution.py:114
  41.5 4.6 %all-to-all-start.1 = ((bf16[128,8,512]{2,1,0:T(8,128)(2,1)}), bf16[128,8,512]{2,1,0:T(8,128)(2,1)S(1)}, u32[]{:S(2)}, u32[]{:S(2)}) async-start(bf16[128,8,512]{2,1,0:T(8,128)(2,1)} %bitcast.8), calls=%async_computation.1 | async-start | bytes 2097152 | tf_op jit(solution)/shard_map/all_to_all | solution.py:261
  46.5 17.6 %all-to-all-done.1 = bf16[128,8,512]{2,1,0:T(8,128)(2,1)S(1)} async-done(((bf16[128,8,512]{2,1,0:T(8,128)(2,1)}), bf16[128,8,512]{2,1,0:T(8,128)(2,1)S(1)}, u32[]{:S(2)}, u32[]{:S(2)}) %all-to-all-start.1) | async-done | bytes 1048608 | tf_op jit(solution)/shard_map/all_to_all | solution.py:261
  64.2 3.4 %copy-done.4 = bf16[2048,2048]{1,0:T(8,128)(2,1)S(1)} copy-done((bf16[2048,2048]{1,0:T(8,128)(2,1)S(1)}, bf16[2048,2048]{1,0:T(8,128)(2,1)}, u32[]{:S(2)}) %copy-start.4) | copy-done | bytes 8388632
  67.6 8.9 %shard_map.107 = (bf16[128,2048]{1,0:T(8,128)(2,1)S(1)}, bf16[128,2048]{1,0:T(8,128)(2,1)S(1)}, bf16[1024,512]{1,0:T(8,128)(2,1)}) custom-call(bf16[1024,512]{1,0:T(8,128)(2,1)S(1)} %bitcast.21, s32[128,4]{1,0:T(8,128)S(1)} %get-tuple-element.9.tgt_c, s32[4,128]{1,0:T(4,128)S(1)} %get-tuple-element.10.tgt_r, s32[128,1]{1,0:T(8,128)S(1)} %copy.28.labels, ...), custom_call_target="tpu_custom_call" | custom-call | flops 3221225472 | bytes 12582912 | tf_op jit(solution)/shard_map/pallas_call | solution.py:172
  76.5 8.1 %fusion = f32[2048,2048]{1,0:T(8,128)} fusion(bf16[128,2048]{1,0:T(8,128)(2,1)S(1)} %get-tuple-element.12, bf16[128,2048]{1,0:T(8,128)(2,1)S(1)} %get-tuple-element.13), kind=kOutput, calls=%fused_computation | convolution fusion | flops 1073741824 | bytes 17825792 | tf_op jit(solution)/shard_map/dot_general | solution.py:279
  84.7 25.8 %reduce-scatter.5.cloned.1.call-done = f32[1024,2048]{1,0:T(8,128)} async-done(((f32[2048,2048]{1,0:T(8,128)}), f32[1024,2048]{1,0:T(8,128)}) %reduce-scatter.5.cloned.1.call-update) | async-done | bytes 8388624 | tf_op jit(solution)/shard_map/reduce_scatter | solution.py:283
  110.5 84.6 %reduce-scatter.7.cloned.1.call-done = f32[256,2048]{1,0:T(8,128)} async-done(((f32[1024,2048]{1,0:T(8,128)}), f32[256,2048]{1,0:T(8,128)}) %reduce-scatter.7.cloned.1.call-update) | async-done | bytes 2097168 | tf_op jit(solution)/shard_map/reduce_scatter | solution.py:283
  195.2 8.3 %all-to-all-start.2 = ((bf16[128,8,512]{2,1,0:T(8,128)(2,1)}), bf16[128,8,512]{2,1,0:T(8,128)(2,1)S(1)}, u32[]{:S(2)}, u32[]{:S(2)}) async-start(bf16[128,8,512]{2,1,0:T(8,128)(2,1)} %bitcast.13), calls=%async_computation.2 | async-start | bytes 2097152 | tf_op jit(solution)/shard_map/all_to_all | solution.py:276
  203.5 31.6 %reduce-scatter.9.cloned.1.call-done = f32[64,2048]{1,0:T(8,128)} async-done(((f32[256,2048]{1,0:T(8,128)}), f32[64,2048]{1,0:T(8,128)}) %reduce-scatter.9.cloned.1.call-update) | async-done | bytes 524304 | tf_op jit(solution)/shard_map/reduce_scatter | solution.py:283
  235.5 3.3 %shard_map.105.count = bf16[2048,1024]{1,0:T(8,128)(2,1)S(1)} custom-call(s32[4,1024]{1,0:T(4,128)S(1)} %reshape.38.ids), custom_call_target="tpu_custom_call" | custom-call | flops 16777216 | bytes 4194304 | tf_op jit(solution)/shard_map/pallas_call | solution.py:205
  238.9 2.0 copy-done.1
  241.2 2.2 copy-done
  243.4 2.2 copy-done.2
  245.6 6.3 %shard_map.108 = f32[2048,512]{1,0:T(8,128)} custom-call(bf16[2048,1024]{1,0:T(8,128)(2,1)S(1)} %copy-done.2, bf16[1024,512]{1,0:T(8,128)(2,1)S(1)} %bitcast.20, f32[2048,512]{1,0:T(8,128)S(1)} %copy-done, f32[2048,128]{1,0:T(8,128)S(1)} %broadcast_in_dim.14.accum), custom_call_target="tpu_custom_call" | custom-call | flops 2147483648 | bytes 13631488 | tf_op jit(solution)/shard_map/pallas_call | solution.py:229
  251.9 7.6 %reduce-scatter.11.cloned.1.call-done = f32[16,2048]{1,0:T(8,128)} async-done(((f32[64,2048]{1,0:T(8,128)}), f32[16,2048]{1,0:T(8,128)}) %reduce-scatter.11.cloned.1.call-update) | async-done | bytes 131088 | tf_op jit(solution)/shard_map/reduce_scatter | solution.py:283
  (27 shorter events, 1.2 us)
Async XLA Ops:
  9.5 0.7 copy-start.3
  13.0 20.2 %all-to-all-start = ((s32[128,1,32]{2,1,0:T(1,128)}), s32[128,1,32]{2,1,0:T(1,128)S(1)}, u32[]{:S(2)}, u32[]{:S(2)}) async-start(s32[128,1,32]{2,1,0:T(1,128)} %bitcast.4), calls=%async_computation | async-start | bytes 131072 | tf_op jit(solution)/shard_map/all_to_all | solution.py:259
  33.2 13.2 %copy-start.8 = (s32[128]{0:T(128)S(1)}, s32[128]{0:T(128)}, u32[]{:S(2)}) copy-start(s32[128]{0:T(128)} %param.14) | copy-start | bytes 1540
  33.2 31.0 %copy-start.5 = (f32[2048]{0:T(1024)S(1)}, f32[2048]{0:T(1024)}, u32[]{:S(2)}) copy-start(f32[2048]{0:T(1024)} %param.16) | copy-start | bytes 24580
  33.2 31.0 %copy-start.6 = (f32[2048]{0:T(1024)S(1)}, f32[2048]{0:T(1024)}, u32[]{:S(2)}) copy-start(f32[2048]{0:T(1024)} %param.17) | copy-start | bytes 24580
  41.5 22.6 %all-to-all-start.1 = ((bf16[128,8,512]{2,1,0:T(8,128)(2,1)}), bf16[128,8,512]{2,1,0:T(8,128)(2,1)S(1)}, u32[]{:S(2)}, u32[]{:S(2)}) async-start(bf16[128,8,512]{2,1,0:T(8,128)(2,1)} %bitcast.8), calls=%async_computation.1 | async-start | bytes 2097152 | tf_op jit(solution)/shard_map/all_to_all | solution.py:261
  46.2 64.3 %reduce-scatter.5.cloned.1.call-start = ((), (), s32[]{:S(2)}) async-start(), calls=%async_computation.7 | async-start | bytes 25165824 | tf_op jit(solution)/shard_map/reduce_scatter | solution.py:283
  64.2 3.4 %copy-start.4 = (bf16[2048,2048]{1,0:T(8,128)(2,1)S(1)}, bf16[2048,2048]{1,0:T(8,128)(2,1)}, u32[]{:S(2)}) copy-start(bf16[2048,2048]{1,0:T(8,128)(2,1)} %w_hbm.1) | copy-start | bytes 25165828
  84.6 110.5 %reduce-scatter.7.cloned.1.call-start = ((), (), s32[]{:S(2)}) async-start(), calls=%async_computation.8 | async-start | bytes 10485760 | tf_op jit(solution)/shard_map/reduce_scatter | solution.py:283
  110.5 124.7 %reduce-scatter.9.cloned.1.call-start = ((), (), s32[]{:S(2)}) async-start(), calls=%async_computation.9 | async-start | bytes 2621440 | tf_op jit(solution)/shard_map/reduce_scatter | solution.py:283
  195.2 45.7 %copy-start.7 = (f32[2048]{0:T(1024)S(1)}, f32[2048]{0:T(1024)}, u32[]{:S(2)}) copy-start(f32[2048]{0:T(1024)} %param.10) | copy-start | bytes 24580
  195.2 45.7 %all-to-all-start.2 = ((bf16[128,8,512]{2,1,0:T(8,128)(2,1)}), bf16[128,8,512]{2,1,0:T(8,128)(2,1)S(1)}, u32[]{:S(2)}, u32[]{:S(2)}) async-start(bf16[128,8,512]{2,1,0:T(8,128)(2,1)} %bitcast.13), calls=%async_computation.2 | async-start | bytes 2097152 | tf_op jit(solution)/shard_map/all_to_all | solution.py:276
  203.4 56.1 %reduce-scatter.11.cloned.1.call-start = ((), (), s32[]{:S(2)}) async-start(), calls=%async_computation.10 | async-start | bytes 655360 | tf_op jit(solution)/shard_map/reduce_scatter | solution.py:283
  238.8 2.0 copy-start.1
  241.2 2.2 copy-start
  243.4 2.2 copy-start.2
Sparse Core Ops, SparseCore 0:
  84.7 25.6 reduce-scatter.4
  113.0 82.0 reduce-scatter.6
  197.7 37.4 reduce-scatter.8
  238.0 21.4 reduce-scatter.10

commit v2 on v1

--- a/solution.py
+++ b/solution.py
@@ -127,24 +127,44 @@
     )(ids, table)
 
 
-def dense_kernel(
-    slots, tgt_c, tgt_r, labels, bias, head, w_hbm, pooled, dpre_out, sending, w, sems
-):
+def pool_kernel(slots, tgt_c, pooled, blocks):
     samples, features = tgt_c.shape
     total, wide = slots.shape
+    part = blocks.shape[2]
+    lane = iota((samples, total), 1)
+    for f in range(features):
+        pick = (tgt_c[:, f : f + 1] == lane).astype(F32).astype(BF)
+        bag = dot(pick, slots[...]).astype(BF)
+        pooled[:, f * wide : (f + 1) * wide] = bag
+        for k in range(wide // part):
+            blocks[f * (wide // part) + k] = bag[:, k * part : (k + 1) * part]
+
+
+def pool(slots, tgt_c, groups):
+    samples, features = tgt_c.shape
+    full = features * slots.shape[1]
+    return pl.pallas_call(
+        pool_kernel,
+        out_shape=(
+            jax.ShapeDtypeStruct((samples, full), BF),
+            jax.ShapeDtypeStruct((groups, samples, full // groups), BF),
+        ),
+        compiler_params=params(16),
+    )(slots, tgt_c)
+
+
+def dense_kernel(pooled, tgt_r, labels, bias, head, w_hbm, dpre_out, sending, w, sems):
+    features, samples = tgt_r.shape
+    total, wide = sending.shape
     copies = []
     for f in range(features):
         part = pl.ds(f * wide, wide)
         copies.append(pltpu.make_async_copy(w_hbm.at[part], w.at[part], sems.at[f]))
         copies[-1].start()
-    lane = iota((samples, total), 1)
     pre = bias[...]
     for f in range(features):
-        pick = (tgt_c[:, f : f + 1] == lane).astype(F32).astype(BF)
-        bag = dot(pick, slots[...]).astype(BF)
-        pooled[:, f * wide : (f + 1) * wide] = bag
         copies[f].wait()
-        pre = pre + dot(bag, w[f * wide : (f + 1) * wide, :])
+        pre = pre + dot(pooled[:, f * wide : (f + 1) * wide], w[f * wide : (f + 1) * wide, :])
     sig = jax.nn.sigmoid(pre)
     logit = jnp.sum(pre * sig * head[...], axis=1, keepdims=True)
     dlogit = jax.nn.sigmoid(logit) - labels[...].astype(F32)
@@ -164,17 +184,16 @@
     sending[...] = acc.astype(BF)
 
 
-def dense(slots, tgt_c, tgt_r, labels, bias, head, w):
-    samples, features = tgt_c.shape
-    total, wide = slots.shape
+def dense(pooled, tgt_r, labels, bias, head, w, total):
+    features, samples = tgt_r.shape
     hidden = w.shape[1]
+    wide = w.shape[0] // features
     vmem = pl.BlockSpec(memory_space=pltpu.VMEM)
     return pl.pallas_call(
         dense_kernel,
-        in_specs=[vmem] * 6 + [pl.BlockSpec(memory_space=pl.ANY)],
-        out_specs=[vmem] * 3,
+        in_specs=[vmem] * 5 + [pl.BlockSpec(memory_space=pl.ANY)],
+        out_specs=[vmem] * 2,
         out_shape=(
-            jax.ShapeDtypeStruct((samples, features * wide), BF),
             jax.ShapeDtypeStruct((samples, hidden), BF),
             jax.ShapeDtypeStruct((total, wide), BF),
         ),
@@ -186,7 +205,36 @@
         cost_estimate=pl.CostEstimate(
             flops=6 * samples * w.size, bytes_accessed=12 << 20, transcendentals=0
         ),
-    )(slots, tgt_c, tgt_r, labels, bias, head, w)
+    )(pooled, tgt_r, labels, bias, head, w)
+
+
+def weight_kernel(order, blocks, *refs):
+    pieces, out = refs[:-1], refs[-1]
+    half = len(pieces) // 2
+    acc = None
+    for k in range(half):
+        left = jnp.concatenate([blocks[order[k]], blocks[order[half + k]]], axis=0)
+        right = jnp.concatenate([pieces[k][...], pieces[half + k][...]], axis=0)
+        term = lax.dot_general(
+            left, right, (((0,), (0,)), ((), ())), preferred_element_type=F32
+        )
+        acc = term if acc is None else acc + term
+    out[...] = acc
+
+
+def weight_part(order, blocks, pieces):
+    hidden = pieces[0].shape[1]
+    vmem = pl.BlockSpec(memory_space=pltpu.VMEM)
+    return pl.pallas_call(
+        weight_kernel,
+        in_specs=[pl.BlockSpec(memory_space=pltpu.SMEM)] + [vmem] * (1 + len(pieces)),
+        out_specs=vmem,
+        out_shape=jax.ShapeDtypeStruct((blocks.shape[2], hidden), F32),
+        compiler_params=params(32),
+        cost_estimate=pl.CostEstimate(
+            flops=2 * blocks.size * hidden, bytes_accessed=7 << 20, transcendentals=0
+        ),
+    )(order, blocks, *pieces)
 
 
 def counts_kernel(ids, out):
@@ -264,23 +312,36 @@
     ids_r = incoming.reshape(devices, bag_len, cap).transpose(1, 0, 2).reshape(bag_len, -1)
     count = counts(ids_r, rows_dev)
     accum = jnp.broadcast_to(row_accum[:, None], (rows_dev, 128))
-    pooled, dpre, sending = dense(
-        slots.reshape(devices * cap, width),
-        tgt_c,
+    group = lax.axis_size(("role", "z"))
+    ring = lax.axis_size("z")
+    pooled, blocks = pool(slots.reshape(devices * cap, width), tgt_c, group)
+    blocks = lax.all_to_all(blocks, ("role", "z"), split_axis=0, concat_axis=0, tiled=True)
+    dpre, sending = dense(
+        pooled,
         tgt_r,
         labels.reshape(samples, 1),
         hidden_bias[None, :],
         w_logit[None, :],
         w_hidden,
-    )
+        devices * cap,
+    )
+    mine = [dpre] + [
+        lax.ppermute(dpre, "z", [(i, (i + s) % ring) for i in range(ring)]) for s in range(1, ring)
+    ]
+    other = [lax.ppermute(v, "role", [(0, 1), (1, 0)]) for v in mine]
     received = lax.all_to_all(
         sending.reshape(devices, cap, width), AXES, split_axis=0, concat_axis=0, tiled=True
     )
-    w_grad = lax.dot_general(
-        pooled, dpre, (((0,), (0,)), ((), ())), preferred_element_type=F32
-    )
-    for axis in AXES:
-        w_grad = lax.psum_scatter(w_grad, axis, scatter_dimension=0, tiled=True)
+    role, z = lax.axis_index("role"), lax.axis_index("z")
+    order = jnp.stack(
+        [r * ring + (z - s) % ring for r in (role, 1 - role) for s in range(ring)]
+    ).astype(I32)
+    part = weight_part(order, blocks, mine + other)
+    plane = devices // group
+    part = lax.all_to_all(
+        part.reshape(plane, -1, part.shape[1]), ("x", "y"), split_axis=0, concat_axis=0, tiled=True
+    )
+    w_grad = jnp.sum(part, axis=0)
     new_table = update(count, received.reshape(devices * cap, width), emb_table, accum)
     return (new_table, w_grad)
 

time: 267 us -> 158 us (0.59)
  waiting for transfers between devices: 174 us -> 57.6 us
  blocking collectives: 0 us -> 22.2 us
  between operations: 13.9 us -> 0.8 us
  matrix products: 8.12 us -> 0 us
  starting transfers between devices: 24.4 us -> 31.2 us
  local copies, waits for them, and re-layouts: 13.6 us -> 7.33 us
  Pallas kernels: 29.6 us -> 33.4 us
    reduce_scatter x4 -> x0, waiting for transfers between devices: 150 us -> none  [per_device(): w_grad = lax.psum_scatter(w_grad, axis, scatter_dimension=0, tiled=True)]
    ppermute x0 -> x7, waiting for transfers between devices: none -> 30.7 us  [the longest x3 28.5 us: per_device(): lax.ppermute(dpre, 'z', [(i, (i + s) % ring) for i in range(ring)])]
    all_to_all x0 -> x1, blocking collectives: none -> 22.2 us  [per_device(): lax.all_to_all(found.reshape(devices, cap, width), AXES, split_axis=0, co...]
    dot_general x1 -> x0, matrix products: 8.12 us -> none  [per_device(): lax.dot_general(pooled, dpre, (((0,), (0,)), ((), ())), preferred_element...]
    unnamed x19 -> x15, local copies, waits for them, and re-layouts: 11.2 us -> 4.86 us
    ppermute x0 -> x7, starting transfers between devices: none -> 5.51 us  [the longest x3 4.91 us: per_device(): lax.ppermute(dpre, 'z', [(i, (i + s) % ring) for i in range(ring)])]
    pallas_call x1 -> x3, Pallas kernels: 8.89 us -> 13.4 us  [the longest x1 7.56 us: dense(): pl.pallas_call(dense_kernel, in_specs=[vmem] * 5 + [pl.BlockSpec(memory_s...]
    all_to_all x1 -> x2, starting transfers between devices: 4.63 us -> 8.07 us  [the longest x1 4.57 us: per_device(): lax.all_to_all(part.reshape(plane, -1, part.shape[1]), ('x', 'y'), split_...]
  transfers between devices with their start and end apart: 7 -> 11, of which waited for: 6 -> 5; matrix products, arithmetic and copies ran while one was open for 1% -> 2% of each run, Pallas kernels for 4% -> 14%
where the time goes in v2:
time: 158 us; the launch traced here: 157 us
  waiting for transfers between devices  57.6 us (36%)
  Pallas kernels  33.4 us (21%)
  starting transfers between devices  31.2 us (20%)
  blocking collectives  22.2 us (14%)
  local copies, waits for them, and re-layouts  7.33 us (5%)
  other arithmetic  4.81 us (3%)
    ppermute x3, waiting for transfers between devices, per_device(): lax.ppermute(dpre, 'z', [(i, (i + s) % ring) for i in range(ring)])  28.5 us
    all_to_all x1, blocking collectives, per_device(): lax.all_to_all(found.reshape(devices, cap, width), AXES, split_axis=0, co...  22.2 us
    all_to_all x1, waiting for transfers between devices, per_device(): lax.all_to_all(part.reshape(plane, -1, part.shape[1]), ('x', 'y'), split_...  20.3 us
    all_to_all x1, starting transfers between devices, per_device(): lax.all_to_all(outgoing, AXES, split_axis=0, concat_axis=0, tiled=True)  11.1 us
    pallas_call x1, Pallas kernels, lookup(): pl.pallas_call(lambda *refs: lookup_kernel(bag_len, *refs), grid=(sources...  7.61 us
    pallas_call x1, Pallas kernels, dense(): pl.pallas_call(dense_kernel, in_specs=[vmem] * 5 + [pl.BlockSpec(memory_s...  7.56 us
    all_to_all x1, waiting for transfers between devices, per_device(): lax.all_to_all(outgoing, AXES, split_axis=0, concat_axis=0, tiled=True)  6.59 us
    all_to_all x1, starting transfers between devices, per_device(): lax.all_to_all(sending.reshape(devices, cap, width), AXES, split_axis=0,...  6.49 us
  transfers between devices with their start and end apart: 11, of which 5 were waited for; matrix products, arithmetic and copies ran while one was open for 2% of the time, Pallas kernels for 14%

profile of v2, /device:TPU:0, one launch (start us, length us, event | category | flops | bytes accessed | tf_op | source)
XLA Modules:
  0.0 157.4 jit_solution(13283400457078734347)
XLA Ops:
  0.6 0.8 copy.23.rows
  3.7 2.8 %shard_map.104 = (s32[128,32]{1,0:T(8,128)}, s32[128,4]{1,0:T(8,128)S(1)}, s32[4,128]{1,0:T(4,128)S(1)}) custom-call(s32[128,4]{1,0:T(8,128)S(1)} %copy.22.own_c, s32[4,128]{1,0:T(4,128)S(1)} %bitcast.32, s32[128,16]{1,0:T(8,128)S(1)} %copy.23.rows, s32[128,4]{1,0:T(8,128)S(1)} %copy.24.lens), custom_call_target="tpu_custom_call" | custom-call | tf_op jit(solution)/shard_map/pallas_call | solution.py:75
  6.5 11.1 %all-to-all-start = ((s32[128,1,32]{2,1,0:T(1,128)}), s32[128,1,32]{2,1,0:T(1,128)S(1)}, u32[]{:S(2)}, u32[]{:S(2)}) async-start(s32[128,1,32]{2,1,0:T(1,128)} %bitcast.4), calls=%async_computation | async-start | bytes 131072 | tf_op jit(solution)/shard_map/all_to_all | solution.py:307
  17.6 2.5 %convert_element_type.3.refs_1_ = bf16[2048,512]{1,0:T(8,128)(2,1)S(1)} convert(f32[2048,512]{1,0:T(8,128)} %table.1) | non-fusion elementwise | flops 1048576 | bytes 6291456 | tf_op jit(solution)/shard_map/convert_element_type | solution.py:306
  20.1 6.6 %all-to-all-done = s32[128,1,32]{2,1,0:T(1,128)S(1)} async-done(((s32[128,1,32]{2,1,0:T(1,128)}), s32[128,1,32]{2,1,0:T(1,128)S(1)}, u32[]{:S(2)}, u32[]{:S(2)}) %all-to-all-start) | async-done | bytes 16416 | tf_op jit(solution)/shard_map/all_to_all | solution.py:307
  26.7 7.6 %shard_map.106 = bf16[1024,512]{1,0:T(8,128)(2,1)S(1)} custom-call(s32[128,32]{1,0:T(8,128)S(1)} %bitcast.30, bf16[2048,512]{1,0:T(8,128)(2,1)S(1)} %convert_element_type.3.refs_1_), custom_call_target="tpu_custom_call" | custom-call | flops 2147483648 | bytes 4194304 | tf_op jit(solution)/shard_map/pallas_call | solution.py:114
  34.3 22.2 %all_to_all.31 = bf16[128,8,512]{2,1,0:T(8,128)(2,1)S(1)} all-to-all(bf16[128,8,512]{2,1,0:T(8,128)(2,1)S(1)} %bitcast.29), channel_id=1, replica_groups=mesh['role'=2,'z'=4,'x'=4,'y'=4] {'role','z','x','y'}, dimensions={0} | all-to-all | bytes 2097152 | tf_op jit(solution)/shard_map/all_to_all | solution.py:309
  56.5 1.6 shard_map.107
  58.1 3.5 %all-to-all-start.3 = ((bf16[8,128,256]{2,1,0:T(8,128)(2,1)}), bf16[8,128,256]{2,1,0:T(8,128)(2,1)S(1)}, u32[]{:S(2)}, u32[]{:S(2)}) async-start(bf16[8,128,256]{2,1,0:T(8,128)(2,1)} %get-tuple-element.14), calls=%async_computation.3 | async-start | bytes 1048576 | tf_op jit(solution)/shard_map/all_to_all | solution.py:318
  61.7 3.4 %copy-done.2 = bf16[2048,2048]{1,0:T(8,128)(2,1)S(1)} copy-done((bf16[2048,2048]{1,0:T(8,128)(2,1)S(1)}, bf16[2048,2048]{1,0:T(8,128)(2,1)}, u32[]{:S(2)}) %copy-start.2) | copy-done | bytes 8388632
  65.1 7.6 %shard_map.108 = (bf16[128,2048]{1,0:T(8,128)(2,1)S(1)}, bf16[1024,512]{1,0:T(8,128)(2,1)}) custom-call(bf16[128,2048]{1,0:T(8,128)(2,1)S(1)} %get-tuple-element.11.pooled, s32[4,128]{1,0:T(4,128)S(1)} %get-tuple-element.12.tgt_r, s32[128,1]{1,0:T(8,128)S(1)} %copy.28.labels, f32[1,2048]{1,0:T(1,128)S(1)} %bitcast.33, f32[1,2048]{1,0:T(1,128)S(1)} %bitcast.34, ...), custom_call_target="tpu_custom_call" | custom-call | flops 3221225472 | bytes 12582912 | tf_op jit(solution)/shard_map/pallas_call | solution.py:192
  72.7 3.2 %collective-permute-start.2 = (bf16[128,2048]{1,0:T(8,128)(2,1)S(1)}, bf16[128,2048]{1,0:T(8,128)(2,1)S(1)}, u32[]{:S(2)}, u32[]{:S(2)}) collective-permute-start(bf16[128,2048]{1,0:T(8,128)(2,1)S(1)} %get-tuple-element.15.refs_0_), channel_id=1, source_target_pairs={{0,48},{16,0},{32,16},{48,32},{1,49},{17,1},{33,17},{49,33},{2,50}... | collective-permute-start | bytes 1572872 | tf_op jit(solution)/shard_map/ppermute | solution.py:329
  75.9 0.8 collective-permute-start.1
  76.7 0.9 collective-permute-start
  77.6 6.5 %all-to-all-start.2 = ((bf16[128,8,512]{2,1,0:T(8,128)(2,1)}), bf16[128,8,512]{2,1,0:T(8,128)(2,1)S(1)}, u32[]{:S(2)}, u32[]{:S(2)}) async-start(bf16[128,8,512]{2,1,0:T(8,128)(2,1)} %bitcast.13), calls=%async_computation.2 | async-start | bytes 2097152 | tf_op jit(solution)/shard_map/all_to_all | solution.py:332
  84.2 25.5 %collective-permute-done.2.refs_3_ = bf16[128,2048]{1,0:T(8,128)(2,1)S(1)} collective-permute-done((bf16[128,2048]{1,0:T(8,128)(2,1)S(1)}, bf16[128,2048]{1,0:T(8,128)(2,1)S(1)}, u32[]{:S(2)}, u32[]{:S(2)}) %collective-permute-start.2) | collective-permute-done | bytes 524320 | tf_op jit(solution)/shard_map/ppermute | solution.py:329
  110.2 3.0 %collective-permute-done.refs_1_ = bf16[128,2048]{1,0:T(8,128)(2,1)} collective-permute-done((bf16[128,2048]{1,0:T(8,128)(2,1)S(1)}, bf16[128,2048]{1,0:T(8,128)(2,1)}, u32[]{:S(2)}, u32[]{:S(2)}) %collective-permute-start) | collective-permute-done | bytes 524320 | tf_op jit(solution)/shard_map/ppermute | solution.py:329
  113.3 2.1 %collective-permute-done.4.refs_5_ = bf16[128,2048]{1,0:T(8,128)(2,1)} collective-permute-done((bf16[128,2048]{1,0:T(8,128)(2,1)}, bf16[128,2048]{1,0:T(8,128)(2,1)}, u32[]{:S(2)}, u32[]{:S(2)}) %collective-permute-start.4) | collective-permute-done | bytes 524320 | tf_op jit(solution)/shard_map/ppermute | solution.py:331
  115.5 4.3 %shard_map.110 = f32[256,2048]{1,0:T(8,128)} custom-call(s32[8]{0:T(128)S(1)} %stack.35.order, bf16[8,128,256]{2,1,0:T(8,128)(2,1)S(1)} %all-to-all-done.3.blocks, bf16[128,2048]{1,0:T(8,128)(2,1)S(1)} %get-tuple-element.15.refs_0_, bf16[128,2048]{1,0:T(8,128)(2,1)} %collective-permute-done.refs_1_, bf16[128,2048]{1,0:T(8,128)(2,1)S(1)} %collective-permute-done.1.refs_2_, ...), custom_call_target="tpu_custom_call" | custom-call | flops 1073741824 | bytes 7340032 | tf_op jit(solution)/shard_map/pallas_call | solution.py:228
  119.8 4.6 %all-to-all-start.4 = ((f32[16,16,2048]{2,1,0:T(8,128)}), f32[16,16,2048]{2,1,0:T(8,128)}, u32[]{:S(2)}, u32[]{:S(2)}) async-start(f32[16,16,2048]{2,1,0:T(8,128)} %bitcast.23), calls=%async_computation.4 | async-start | bytes 4194304 | tf_op jit(solution)/shard_map/all_to_all | solution.py:341
  124.7 3.3 %shard_map.105.count = bf16[2048,1024]{1,0:T(8,128)(2,1)S(1)} custom-call(s32[4,1024]{1,0:T(4,128)S(1)} %reshape.41.ids), custom_call_target="tpu_custom_call" | custom-call | flops 16777216 | bytes 4194304 | tf_op jit(solution)/shard_map/pallas_call | solution.py:253
  128.4 6.3 %shard_map.109 = f32[2048,512]{1,0:T(8,128)} custom-call(bf16[2048,1024]{1,0:T(8,128)(2,1)S(1)} %shard_map.105.count, bf16[1024,512]{1,0:T(8,128)(2,1)S(1)} %bitcast.27, f32[2048,512]{1,0:T(8,128)S(1)} %copy-done, f32[2048,128]{1,0:T(8,128)S(1)} %broadcast_in_dim.14.accum), custom_call_target="tpu_custom_call" | custom-call | flops 2147483648 | bytes 13631488 | tf_op jit(solution)/shard_map/pallas_call | solution.py:277
  134.7 20.3 %all-to-all-done.4 = f32[16,16,2048]{2,1,0:T(8,128)} async-done(((f32[16,16,2048]{2,1,0:T(8,128)}), f32[16,16,2048]{2,1,0:T(8,128)}, u32[]{:S(2)}, u32[]{:S(2)}) %all-to-all-start.4) | async-done | bytes 2097184 | tf_op jit(solution)/shard_map/all_to_all | solution.py:341
  155.0 2.4 %reduce_sum.9 = f32[16,2048]{1,0:T(8,128)} reduce(f32[16,16,2048]{2,1,0:T(8,128)} %all-to-all-done.4, f32[]{:T(128)} %constant.56.clone.1), dimensions={0}, to_apply=%region_0.1 | reduce | flops 491520 | bytes 2228228 | tf_op jit(solution)/shard_map/reduce_sum | solution.py:344
  (31 shorter events, 3.8 us)
Async XLA Ops:
  3.0 0.7 copy-start.1
  6.5 20.2 %all-to-all-start = ((s32[128,1,32]{2,1,0:T(1,128)}), s32[128,1,32]{2,1,0:T(1,128)S(1)}, u32[]{:S(2)}, u32[]{:S(2)}) async-start(s32[128,1,32]{2,1,0:T(1,128)} %bitcast.4), calls=%async_computation | async-start | bytes 131072 | tf_op jit(solution)/shard_map/all_to_all | solution.py:307
  26.7 34.9 %copy-start.6 = (s32[128]{0:T(128)S(1)}, s32[128]{0:T(128)}, u32[]{:S(2)}) copy-start(s32[128]{0:T(128)} %param.14) | copy-start | bytes 1540
  26.7 35.1 %copy-start.3 = (f32[2048]{0:T(1024)S(1)}, f32[2048]{0:T(1024)}, u32[]{:S(2)}) copy-start(f32[2048]{0:T(1024)} %param.16) | copy-start | bytes 24580
  26.7 35.1 %copy-start.4 = (f32[2048]{0:T(1024)S(1)}, f32[2048]{0:T(1024)}, u32[]{:S(2)}) copy-start(f32[2048]{0:T(1024)} %param.17) | copy-start | bytes 24580
  58.1 19.5 %all-to-all-start.3 = ((bf16[8,128,256]{2,1,0:T(8,128)(2,1)}), bf16[8,128,256]{2,1,0:T(8,128)(2,1)S(1)}, u32[]{:S(2)}, u32[]{:S(2)}) async-start(bf16[8,128,256]{2,1,0:T(8,128)(2,1)} %get-tuple-element.14), calls=%async_computation.3 | async-start | bytes 1048576 | tf_op jit(solution)/shard_map/all_to_all | solution.py:318
  61.7 3.4 %copy-start.2 = (bf16[2048,2048]{1,0:T(8,128)(2,1)S(1)}, bf16[2048,2048]{1,0:T(8,128)(2,1)}, u32[]{:S(2)}) copy-start(bf16[2048,2048]{1,0:T(8,128)(2,1)} %w_hbm.1) | copy-start | bytes 25165828
  72.7 37.0 %collective-permute-start.2 = (bf16[128,2048]{1,0:T(8,128)(2,1)S(1)}, bf16[128,2048]{1,0:T(8,128)(2,1)S(1)}, u32[]{:S(2)}, u32[]{:S(2)}) collective-permute-start(bf16[128,2048]{1,0:T(8,128)(2,1)S(1)} %get-tuple-element.15.refs_0_), channel_id=1, source_target_pairs={{0,48},{16,0},{32,16},{48,32},{1,49},{17,1},{33,17},{49,33},{2,50}... | collective-permute-start | bytes 1572872 | tf_op jit(solution)/shard_map/ppermute | solution.py:329
  75.9 33.8 %collective-permute-start.1 = (bf16[128,2048]{1,0:T(8,128)(2,1)S(1)}, bf16[128,2048]{1,0:T(8,128)(2,1)S(1)}, u32[]{:S(2)}, u32[]{:S(2)}) collective-permute-start(bf16[128,2048]{1,0:T(8,128)(2,1)S(1)} %get-tuple-element.15.refs_0_), channel_id=1, source_target_pairs={{0,32},{16,48},{32,0},{48,16},{1,33},{17,49},{33,1},{49,17},{2,34}... | collective-permute-start | bytes 1572872 | tf_op jit(solution)/shard_map/ppermute | solution.py:329
  76.7 36.5 %collective-permute-start = (bf16[128,2048]{1,0:T(8,128)(2,1)S(1)}, bf16[128,2048]{1,0:T(8,128)(2,1)}, u32[]{:S(2)}, u32[]{:S(2)}) collective-permute-start(bf16[128,2048]{1,0:T(8,128)(2,1)S(1)} %get-tuple-element.15.refs_0_), channel_id=1, source_target_pairs={{0,16},{16,32},{32,48},{48,0},{1,17},{17,33},{33,49},{49,1},{2,18}... | collective-permute-start | bytes 1572872 | tf_op jit(solution)/shard_map/ppermute | solution.py:329
  77.6 42.2 %all-to-all-start.2 = ((bf16[128,8,512]{2,1,0:T(8,128)(2,1)}), bf16[128,8,512]{2,1,0:T(8,128)(2,1)S(1)}, u32[]{:S(2)}, u32[]{:S(2)}) async-start(bf16[128,8,512]{2,1,0:T(8,128)(2,1)} %bitcast.13), calls=%async_computation.2 | async-start | bytes 2097152 | tf_op jit(solution)/shard_map/all_to_all | solution.py:332
  84.1 29.2 %collective-permute-start.3 = (bf16[128,2048]{1,0:T(8,128)(2,1)S(1)}, bf16[128,2048]{1,0:T(8,128)(2,1)}, u32[]{:S(2)}, u32[]{:S(2)}) collective-permute-start(bf16[128,2048]{1,0:T(8,128)(2,1)S(1)} %get-tuple-element.15.refs_0_), channel_id=1, source_target_pairs={{0,64},{64,0},{1,65},{65,1},{2,66},{66,2},{3,67},{67,3},{4,68},{68... | collective-permute-start | bytes 1572872 | tf_op jit(solution)/shard_map/ppermute | solution.py:331
  109.7 3.6 %collective-permute-start.6 = (bf16[128,2048]{1,0:T(8,128)(2,1)S(1)}, bf16[128,2048]{1,0:T(8,128)(2,1)}, u32[]{:S(2)}, u32[]{:S(2)}) collective-permute-start(bf16[128,2048]{1,0:T(8,128)(2,1)S(1)} %collective-permute-done.2.refs_3_), channel_id=1, source_target_pairs={{0,64},{64,0},{1,65},{65,1},{2,66},{66,2},{3,67},{67,3},{4,68},{68... | collective-permute-start | bytes 1572872 | tf_op jit(solution)/shard_map/ppermute | solution.py:331
  109.7 3.7 %collective-permute-start.5 = (bf16[128,2048]{1,0:T(8,128)(2,1)S(1)}, bf16[128,2048]{1,0:T(8,128)(2,1)}, u32[]{:S(2)}, u32[]{:S(2)}) collective-permute-start(bf16[128,2048]{1,0:T(8,128)(2,1)S(1)} %collective-permute-done.1.refs_2_), channel_id=1, source_target_pairs={{0,64},{64,0},{1,65},{65,1},{2,66},{66,2},{3,67},{67,3},{4,68},{68... | collective-permute-start | bytes 1572872 | tf_op jit(solution)/shard_map/ppermute | solution.py:331
  113.2 2.3 %collective-permute-start.4 = (bf16[128,2048]{1,0:T(8,128)(2,1)}, bf16[128,2048]{1,0:T(8,128)(2,1)}, u32[]{:S(2)}, u32[]{:S(2)}) collective-permute-start(bf16[128,2048]{1,0:T(8,128)(2,1)} %collective-permute-done.refs_1_), channel_id=1, source_target_pairs={{0,64},{64,0},{1,65},{65,1},{2,66},{66,2},{3,67},{67,3},{4,68},{68... | collective-permute-start | bytes 1572872 | tf_op jit(solution)/shard_map/ppermute | solution.py:331
  119.8 8.3 %copy-start.5 = (f32[2048]{0:T(1024)S(1)}, f32[2048]{0:T(1024)}, u32[]{:S(2)}) copy-start(f32[2048]{0:T(1024)} %param.10) | copy-start | bytes 24580
  119.8 35.3 %all-to-all-start.4 = ((f32[16,16,2048]{2,1,0:T(8,128)}), f32[16,16,2048]{2,1,0:T(8,128)}, u32[]{:S(2)}, u32[]{:S(2)}) async-start(f32[16,16,2048]{2,1,0:T(8,128)} %bitcast.23), calls=%async_computation.4 | async-start | bytes 4194304 | tf_op jit(solution)/shard_map/all_to_all | solution.py:341
  124.7 3.7 %copy-start = (f32[2048,512]{1,0:T(8,128)S(1)}, f32[2048,512]{1,0:T(8,128)}, u32[]{:S(2)}) copy-start(f32[2048,512]{1,0:T(8,128)} %table.1) | copy-start | bytes 12582916

commit v3 on v1

v3 whole, which is shorter than its diff:
```python
import functools

import jax
import jax.numpy as jnp
from jax import lax
from jax.experimental import pallas as pl
from jax.experimental.pallas import tpu as pltpu
from jax.sharding import Mesh, PartitionSpec as P

learn_rate = 0.1
AXES = ("role", "z", "x", "y")
BF = jnp.bfloat16
F32 = jnp.float32
I32 = jnp.int32


def iota(shape, dim):
    return lax.broadcasted_iota(I32, shape, dim)


def dot(a, b):
    return jnp.dot(a, b, preferred_element_type=F32)


def dot_t(a, b):
    return lax.dot_general(a, b, (((1,), (1,)), ((), ())), preferred_element_type=F32)


def params(mib):
    return pltpu.CompilerParams(vmem_limit_bytes=mib << 20)


def cost(flops, nbytes):
    return pl.CostEstimate(flops=flops, bytes_accessed=nbytes, transcendentals=0)


SMEM = pl.BlockSpec(memory_space=pltpu.SMEM)
VMEM = pl.BlockSpec(memory_space=pltpu.VMEM)


def struct(shape, dtype):
    return jax.ShapeDtypeStruct(shape, dtype)


def split_int(v):
    return (v >> 6).astype(F32).astype(BF), (v & 63).astype(F32).astype(BF)


def route_kernel(own, rows, lens, labels, out, cols, tgt_r):
    features, bag_len, samples = rows.shape
    devices, width = out.shape
    cap = width // bag_len
    bags = samples * features
    sub = iota((devices, samples), 0)
    hot = jnp.concatenate([(own[f] == sub).astype(F32) for f in range(features)], axis=1)
    hot_bf = hot.astype(BF)
    upper = (iota((bags, bags), 0) < iota((bags, bags), 1)).astype(F32).astype(BF)
    rank = jnp.sum(dot(hot_bf, upper) * hot, axis=0, keepdims=True).astype(I32)
    column = iota((width, bags), 0)
    wanted = jnp.zeros((width, bags), I32)
    for j in range(bag_len):
        value = jnp.concatenate(
            [
                jnp.where(j < lens[f : f + 1, :], rows[f, j : j + 1, :] + 1, 0)
                for f in range(features)
            ],
            axis=1,
        )
        wanted = jnp.where(column == j * cap + rank, value, wanted)
    hi, lo = split_int(wanted)
    out[...] = dot_t(hot_bf, hi).astype(I32) * 64 + dot_t(hot_bf, lo).astype(I32) - 1
    line = iota((samples, samples), 0)
    flat = jnp.where(line == features, labels[...].astype(F32), 0.0)
    for f in range(features):
        target = own[f] * cap + rank[:, f * samples : (f + 1) * samples]
        tgt_r[f : f + 1, :] = target
        flat = jnp.where(line == f, target.astype(F32), flat)
    cols[...] = flat.T


def route(own, rows, lens, labels, devices, cap):
    features, bag_len, samples = rows.shape
    return pl.pallas_call(
        route_kernel,
        out_shape=(
            struct((devices, bag_len * cap), I32),
            struct((samples, samples), F32),
            struct((features, samples), I32),
        ),
        compiler_params=params(12),
    )(own, rows, lens, labels)


def lookup_kernel(bag_len, ids, table, out):
    sources, width = ids.shape
    cap = width // bag_len
    slots = sources * cap
    depth = table.shape[0]
    wanted = ids[...]
    hi, lo = split_int(jnp.where(wanted < 0, 4095, wanted))
    rep = (iota((slots, sources), 0) // cap == iota((slots, sources), 1)).astype(F32).astype(BF)
    mine = (iota((slots, width), 1) % cap == iota((slots, width), 0) % cap).astype(F32)
    spread = iota((width, bag_len * 128), 0) // cap == iota((width, bag_len * 128), 1) // 128
    spread = spread.astype(F32).astype(BF)
    hi = dot((dot(rep, hi) * mine).astype(BF), spread)
    lo = dot((dot(rep, lo) * mine).astype(BF), spread)
    lane = iota((slots, 128), 1)
    low, high = (lane % 64).astype(F32), (lane // 64).astype(F32)
    near = []
    for j in range(bag_len):
        part = slice(j * 128, (j + 1) * 128)
        near.append(jnp.where(lo[:, part] == low, hi[:, part] - high, -1.0).astype(BF))
    one, zero = jnp.ones((), BF), jnp.zeros((), BF)
    pieces = []
    for k in range(depth // 128):
        at = jnp.asarray(2.0 * k, BF)
        count = jnp.where(near[0] == at, one, zero)
        for j in range(1, bag_len):
            count = count + jnp.where(near[j] == at, one, zero)
        pieces.append(count)
    out[...] = dot(jnp.concatenate(pieces, axis=1), table[...]).astype(BF)


def lookup(ids, table, bag_len):
    sources, width = ids.shape
    depth, wide = table.shape
    cap = width // bag_len
    block = 32
    return pl.pallas_call(
        lambda *refs: lookup_kernel(bag_len, *refs),
        grid=(sources // block,),
        in_specs=[
            pl.BlockSpec((block, width), lambda i: (i, 0)),
            pl.BlockSpec((depth, wide), lambda i: (0, 0)),
        ],
        out_specs=pl.BlockSpec((block * cap, wide), lambda i: (i, 0)),
        out_shape=jax.ShapeDtypeStruct((sources * cap, wide), BF),
        compiler_params=params(20),
        cost_estimate=cost(2 * sources * cap * depth * wide, 4 << 20),
    )(ids, table)


def pool_kernel(at, slots, cols, pooled, *refs):
    sends, bags = refs[:-1], refs[-1]
    features, samples, wide = bags.shape
    total = slots.shape[0]
    lane = iota((samples, total), 1).astype(F32)
    for f in range(features):
        pick = (cols[:, f : f + 1] == lane).astype(F32).astype(BF)
        bag = dot(pick, slots[...]).astype(BF)
        pooled[:, f * wide : (f + 1) * wide] = bag
        bags[f] = bag
    for s, send in enumerate(sends):
        half = ((at[1] + s) % len(sends)) // 2
        for r in range(2):
            send[r] = bags[2 * r + half]


def pool(at, slots, cols, features, ring):
    samples = cols.shape[0]
    total, wide = slots.shape
    return pl.pallas_call(
        pool_kernel,
        in_specs=[SMEM, VMEM, VMEM],
        out_specs=[VMEM] * (1 + ring),
        out_shape=[struct((samples, features * wide), BF)]
        + [struct((2, samples, wide), BF)] * ring,
        scratch_shapes=[pltpu.VMEM((features, samples, wide), BF)],
        compiler_params=params(12),
        cost_estimate=cost(1 << 20, 1 << 16),
    )(at, slots, cols)


def forward_kernel(label, at, pooled, cols, bias, head, w, dpre_out, same, other):
    pre = dot(pooled[...], w[...]) + bias[...]
    sig = jax.nn.sigmoid(pre)
    logit = jnp.sum(pre * sig * head[...], axis=1, keepdims=True)
    dlogit = jax.nn.sigmoid(logit) - cols[:, label : label + 1]
    dpre = (dlogit * head[...] * sig * (1.0 + pre * (1.0 - sig))).astype(BF)
    dpre_out[...] = dpre
    half = dpre.shape[1] // 2

    @pl.when(at[1] % 2 == 0)
    def _():
        same[...] = dpre[:, :half]
        other[...] = dpre[:, half:]

    @pl.when(at[1] % 2 == 1)
    def _():
        same[...] = dpre[:, half:]
        other[...] = dpre[:, :half]


def forward(at, pooled, cols, bias, head, w, features):
    samples, hidden = pooled.shape[0], w.shape[1]
    return pl.pallas_call(
        functools.partial(forward_kernel, features),
        in_specs=[SMEM] + [VMEM] * 5,
        out_specs=[VMEM] * 3,
        out_shape=[struct((samples, hidden), BF)] + [struct((samples, hidden // 2), BF)] * 2,
        compiler_params=params(24),
        cost_estimate=cost(2 * samples * w.size, 10 << 20),
    )(at, pooled, cols, bias, head, w)


def backward_kernel(dpre, tgt_r, w, sending):
    features, samples = tgt_r.shape
    total, wide = sending.shape
    sub = iota((total, samples), 0)
    acc = jnp.zeros((total, wide), F32)
    for f in range(features):
        grad = dot_t(dpre[...], w[f * wide : (f + 1) * wide, :]).astype(BF)
        put = (tgt_r[f : f + 1, :] == sub).astype(F32).astype(BF)
        acc += dot(put, grad)
    sending[...] = acc.astype(BF)


def backward(dpre, tgt_r, w, total):
    features, samples = tgt_r.shape
    wide = w.shape[0] // features
    return pl.pallas_call(
        backward_kernel,
        in_specs=[VMEM] * 3,
        out_specs=VMEM,
        out_shape=struct((total, wide), BF),
        compiler_params=params(24),
        cost_estimate=cost(4 * samples * w.size, 10 << 20),
    )(dpre, tgt_r, w)


def turn_kernel(at, *refs):
    pieces, keep, give = refs[:-2], refs[-2], refs[-1]
    for s, piece in enumerate(pieces):
        samples = piece.shape[1]
        part = slice(s * samples, (s + 1) * samples)
        keep[:, part] = piece[at[0]].T
        give[:, part] = piece[1 - at[0]].T


def turn(at, pieces):
    _, samples, wide = pieces[0].shape
    shape = (wide, samples * len(pieces))
    return pl.pallas_call(
        turn_kernel,
        in_specs=[SMEM] + [VMEM] * len(pieces),
        out_specs=[VMEM] * 2,
        out_shape=[struct(shape, BF)] * 2,
        compiler_params=params(12),
        cost_estimate=cost(1 << 20, 2 << 20),
    )(at, *pieces)


def weight_kernel(at, keep, got, *refs):
    ring = 4
    mine, other = refs[:ring], refs[ring : 2 * ring]
    first, second = refs[2 * ring : 3 * ring], refs[3 * ring : 4 * ring]
    acc = refs[4 * ring]
    half = acc.shape[1] // 2
    left = jnp.concatenate([keep[...], got[...]], axis=1)
    right = jnp.concatenate([ref[...] for ref in mine + other], axis=0)
    acc[...] = dot(left, right)
    for s in range(ring):
        x, y = (at[2] + s) % ring, (at[3] + s) % ring
        for p in range(2):
            first[s][p * 64 : (p + 1) * 64, :] = acc[pl.ds(p * 256 + x * 64, 64), :half]
            for q in range(ring):
                k = (p * ring + q) * 16
                second[s][k : k + 16, :] = acc[pl.ds(p * 256 + q * 64 + y * 16, 16), half:]


def weight_part(at, keep, got, mine, other):
    ring = len(mine)
    wide, samples = keep.shape
    half = mine[0].shape[1]
    return pl.pallas_call(
        weight_kernel,
        in_specs=[SMEM] + [VMEM] * (2 + 2 * ring),
        out_specs=[VMEM] * (2 * ring),
        out_shape=[struct((wide // ring, half // 2), F32)] * (2 * ring),
        scratch_shapes=[pltpu.VMEM((wide, half), F32)],
        compiler_params=params(24),
        cost_estimate=cost(4 * wide * samples * half, 8 << 20),
    )(at, keep, got, *mine, *other)


def middle_kernel(at, *refs):
    ring = 4
    first, second = refs[:ring], refs[ring : 2 * ring]
    out = refs[2 * ring : 4 * ring]
    for parts, axis, outs in ((first, 3, out[:ring]), (second, 2, out[ring:])):
        acc = refs[-1]
        acc[...] = (parts[0][...] + parts[1][...]) + (parts[2][...] + parts[3][...])
        for s in range(ring):
            k = (at[axis] + s) % ring
            for p in range(2):
                outs[s][p * 16 : (p + 1) * 16, :] = acc[pl.ds(p * 64 + k * 16, 16), :]


def middle(at, first, second):
    ring = len(first)
    rows, half = first[0].shape
    return pl.pallas_call(
        middle_kernel,
        in_specs=[SMEM] + [VMEM] * (2 * ring),
        out_specs=[VMEM] * (2 * ring),
        out_shape=[struct((rows // ring, half), F32)] * (2 * ring),
        scratch_shapes=[pltpu.VMEM((rows, half), F32)],
        compiler_params=params(12),
        cost_estimate=cost(1 << 20, 3 << 20),
    )(at, *first, *second)


def last_kernel(at, *refs):
    ring = 4
    keep, give = refs[-2], refs[-1]
    half = keep.shape[1] // 2
    for k, parts in enumerate((refs[:ring], refs[ring : 2 * ring])):
        acc = (parts[0][...] + parts[1][...]) + (parts[2][...] + parts[3][...])
        even = (at[1] % 2) == 0
        keep[:, k * half : (k + 1) * half] = jnp.where(even, acc[:16], acc[16:])
        give[:, k * half : (k + 1) * half] = jnp.where(even, acc[16:], acc[:16])


def last(at, first, second):
    ring = len(first)
    rows, half = first[0].shape
    return pl.pallas_call(
        last_kernel,
        in_specs=[SMEM] + [VMEM] * (2 * ring),
        out_specs=[VMEM] * 2,
        out_shape=[struct((rows // 2, 2 * half), F32)] * 2,
        compiler_params=params(12),
        cost_estimate=cost(1 << 16, 1 << 18),
    )(at, *first, *second)


def shifted(value, axis, shift):
    ring = lax.axis_size(axis)
    return lax.ppermute(value, axis, [(i, (i + shift) % ring) for i in range(ring)])


def swapped(value):
    return lax.ppermute(value, "role", [(0, 1), (1, 0)])


def counts_kernel(ids, out):
    block, slots = out.shape
    bag_len = ids.shape[0]
    row = iota((block, slots), 0) + pl.program_id(0) * block
    count = jnp.zeros((block, slots), F32)
    for j in range(bag_len):
        count += (ids[j : j + 1, :] == row).astype(F32)
    out[...] = count.astype(BF)


def counts(ids, rows):
    bag_len, slots = ids.shape
    block = 256
    return pl.pallas_call(
        counts_kernel,
        grid=(rows // block,),
        in_specs=[pl.BlockSpec((bag_len, slots), lambda i: (0, 0))],
        out_specs=pl.BlockSpec((block, slots), lambda i: (i, 0)),
        out_shape=jax.ShapeDtypeStruct((rows, slots), BF),
        compiler_params=params(16),
        cost_estimate=pl.CostEstimate(
            flops=8 * rows * slots, bytes_accessed=2 * rows * slots, transcendentals=0
        ),
    )(ids)


def update_kernel(count, grads, table, accum, out):
    row_grad = dot(count[...], grads[...])
    square = jnp.sum(row_grad * row_grad, axis=1, keepdims=True)
    new_accum = accum[:, 0:1] + square * (1.0 / row_grad.shape[1])
    out[...] = table[...] - learn_rate * row_grad / jnp.sqrt(new_accum + 1e-6)


def update(count, grads, table, accum):
    rows, wide = table.shape
    slots = grads.shape[0]
    block = 256
    return pl.pallas_call(
        update_kernel,
        grid=(rows // block,),
        in_specs=[
            pl.BlockSpec((block, slots), lambda i: (i, 0)),
            pl.BlockSpec((slots, wide), lambda i: (0, 0)),
            pl.BlockSpec((block, wide), lambda i: (i, 0)),
            pl.BlockSpec((block, 128), lambda i: (i, 0)),
        ],
        out_specs=pl.BlockSpec((block, wide), lambda i: (i, 0)),
        out_shape=jax.ShapeDtypeStruct((rows, wide), F32),
        compiler_params=params(32),
        cost_estimate=pl.CostEstimate(
            flops=2 * rows * slots * wide, bytes_accessed=13 << 20, transcendentals=0
        ),
    )(count, grads, table, accum)


def per_device(
    emb_table, row_accum, owners, local_rows, lengths, labels, w_hidden, hidden_bias, w_logit
):
    devices = lax.axis_size(AXES)
    ring = lax.axis_size("z")
    samples, features, bag_len = local_rows.shape
    rows_dev, width = emb_table.shape
    cap = 2 * samples * features // devices
    at = jnp.stack([lax.axis_index(axis) for axis in AXES]).astype(I32)
    outgoing, cols, tgt_r = route(
        owners.transpose(1, 2, 0),
        local_rows.transpose(1, 2, 0),
        lengths.T,
        labels[None, :],
        devices,
        cap,
    )
    table_bf = emb_table.astype(BF)
    incoming = lax.all_to_all(outgoing, AXES, split_axis=0, concat_axis=0, tiled=True)
    found = lookup(incoming, table_bf, bag_len)
    slots = lax.all_to_all(
        found.reshape(devices, cap, width), AXES, split_axis=0, concat_axis=0, tiled=True
    ).reshape(devices * cap, width)
    ids_r = incoming.reshape(devices, bag_len, cap).transpose(1, 0, 2).reshape(bag_len, -1)
    count = counts(ids_r, rows_dev)
    accum = jnp.broadcast_to(row_accum[:, None], (rows_dev, 128))
    pooled, *pieces = pool(at, slots, cols, features, ring)
    pieces = [pieces[0]] + [shifted(pieces[s], "z", s) for s in range(1, ring)]
    dpre, same, diff = forward(
        at, pooled, cols, hidden_bias[None, :], w_logit[None, :], w_hidden, features
    )
    mine = [same] + [shifted(same if s % 2 == 0 else diff, "z", s) for s in range(1, ring)]
    sending = backward(dpre, tgt_r, w_hidden, devices * cap)
    received = lax.all_to_all(
        sending.reshape(devices, cap, width), AXES, split_axis=0, concat_axis=0, tiled=True
    )
    keep, give = turn(at, pieces)
    got = swapped(give)
    other = [swapped(v) for v in mine]
    parts = weight_part(at, keep, got, mine, other)
    first = [parts[0]] + [shifted(parts[s], "x", s) for s in range(1, ring)]
    second = [parts[ring]] + [shifted(parts[ring + s], "y", s) for s in range(1, ring)]
    parts = middle(at, first, second)
    first = [parts[0]] + [shifted(parts[s], "y", s) for s in range(1, ring)]
    second = [parts[ring]] + [shifted(parts[ring + s], "x", s) for s in range(1, ring)]
    mine, give = last(at, first, second)
    got = lax.ppermute(give, "z", [(i, i ^ 1) for i in range(ring)])
    even = at[1] % 2 == 0
    w_grad = jnp.concatenate(
        [jnp.where(even, mine, got), jnp.where(even, got, mine)], axis=1
    )
    new_table = update(count, received.reshape(devices * cap, width), emb_table, accum)
    return (new_table, w_grad)


def solution(mesh):
    split = Mesh(mesh.devices.reshape(2, 4, 4, 4), AXES)
    placed = (
        P(AXES, None),
        P(AXES),
        P(AXES, None, None),
        P(AXES, None, None),
        P(AXES, None),
        P(AXES),
        P(),
        P(),
        P(),
    )
    return jax.shard_map(
        per_device,
        mesh=split,
        in_specs=placed,
        out_specs=(P(AXES, None), P(AXES, None)),
        check_vma=False,
    )
```

time: 267 us -> 142 us (0.53)
  waiting for transfers between devices: 174 us -> 38.4 us
  starting transfers between devices: 24.4 us -> 55 us
  between operations: 13.9 us -> 0.85 us
  matrix products: 8.12 us -> 0 us
    reduce_scatter x4 -> x0, waiting for transfers between devices: 150 us -> none  [per_device(): w_grad = lax.psum_scatter(w_grad, axis, scatter_dimension=0, tiled=True)]
    ppermute x0 -> x24, starting transfers between devices: none -> 32.6 us  [the longest x18 30.9 us: shifted(): lax.ppermute(value, axis, [(i, (i + shift) % ring) for i in range(ring)])]
    ppermute x0 -> x24, waiting for transfers between devices: none -> 13.9 us  [the longest x18 12.1 us: shifted(): lax.ppermute(value, axis, [(i, (i + shift) % ring) for i in range(ring)])]
    dot_general x1 -> x0, matrix products: 8.12 us -> none  [per_device(): lax.dot_general(pooled, dpre, (((0,), (0,)), ((), ())), preferred_element...]
    pallas_call x2 -> x8, Pallas kernels: 11.7 us -> 15.6 us  [the longest x1 5.22 us: backward(): pl.pallas_call(backward_kernel, in_specs=[VMEM] * 3, out_specs=VMEM, out_...]
    pallas_call x1, Pallas kernels: 8.34 us -> 5.44 us  [lookup(): pl.pallas_call(lambda *refs: lookup_kernel(bag_len, *refs), grid=(sources...]
    unnamed x19 -> x24, local copies, waits for them, and re-layouts: 11.2 us -> 12.5 us
  transfers between devices with their start and end apart: 7 -> 27, of which waited for: 6 -> 12; matrix products, arithmetic and copies ran while one was open for 1% -> 2% of each run, Pallas kernels for 4% -> 16%
where the time goes in v3:
time: 142 us; the launch traced here: 141 us
  starting transfers between devices  55 us (39%)
  waiting for transfers between devices  38.4 us (27%)
  Pallas kernels  30.6 us (22%)
  local copies, waits for them, and re-layouts  13.2 us (9%)
  other arithmetic  3.21 us (2%)
    ppermute x18, starting transfers between devices, shifted(): lax.ppermute(value, axis, [(i, (i + shift) % ring) for i in range(ring)])  30.9 us
    all_to_all x1, waiting for transfers between devices, per_device(): lax.all_to_all(found.reshape(devices, cap, width), AXES, split_axis=0, co...  17.9 us
    unnamed x24, local copies, waits for them, and re-layouts  12.5 us
    ppermute x18, waiting for transfers between devices, shifted(): lax.ppermute(value, axis, [(i, (i + shift) % ring) for i in range(ring)])  12.1 us
    all_to_all x1, starting transfers between devices, per_device(): lax.all_to_all(outgoing, AXES, split_axis=0, concat_axis=0, tiled=True)  11.1 us
    all_to_all x1, starting transfers between devices, per_device(): lax.all_to_all(sending.reshape(devices, cap, width), AXES, split_axis=0,...  6.63 us
    all_to_all x1, waiting for transfers between devices, per_device(): lax.all_to_all(outgoing, AXES, split_axis=0, concat_axis=0, tiled=True)  6.59 us
    pallas_call x1, Pallas kernels, update(): pl.pallas_call(update_kernel, grid=(rows // block,), in_specs=[pl.BlockSp...  6.31 us
  transfers between devices with their start and end apart: 27, of which 12 were waited for; matrix products, arithmetic and copies ran while one was open for 2% of the time, Pallas kernels for 16%

profile of v3, /device:TPU:0, one launch (start us, length us, event | category | flops | bytes accessed | tf_op | source)
XLA Modules:
  0.0 141.3 jit_solution(9248011650751040012)
XLA Ops:
  4.5 11.1 %all-to-all-start = ((s32[128,1,32]{2,1,0:T(1,128)}), s32[128,1,32]{2,1,0:T(1,128)S(1)}, u32[]{:S(2)}, u32[]{:S(2)}) async-start(s32[128,1,32]{2,1,0:T(1,128)} %bitcast.5), calls=%async_computation | async-start | bytes 131072 | tf_op jit(solution)/shard_map/all_to_all | solution.py:419
  15.6 2.5 %convert_element_type.3.refs_1_ = bf16[2048,512]{1,0:T(8,128)(2,1)S(1)} convert(f32[2048,512]{1,0:T(8,128)} %table.1) | non-fusion elementwise | flops 1048576 | bytes 6291456 | tf_op jit(solution)/shard_map/convert_element_type | solution.py:418
  18.1 6.6 %all-to-all-done = s32[128,1,32]{2,1,0:T(1,128)S(1)} async-done(((s32[128,1,32]{2,1,0:T(1,128)}), s32[128,1,32]{2,1,0:T(1,128)S(1)}, u32[]{:S(2)}, u32[]{:S(2)}) %all-to-all-start) | async-done | bytes 16416 | tf_op jit(solution)/shard_map/all_to_all | solution.py:419
  24.7 5.4 %shard_map.106 = bf16[1024,512]{1,0:T(8,128)(2,1)} custom-call(s32[128,32]{1,0:T(8,128)S(1)} %bitcast.23, bf16[2048,512]{1,0:T(8,128)(2,1)S(1)} %convert_element_type.3.refs_1_), custom_call_target="tpu_custom_call" | custom-call | flops 2147483648 | bytes 4194304 | tf_op jit(solution)/shard_map/pallas_call | solution.py:129
  30.1 4.6 %all-to-all-start.1 = ((bf16[128,8,512]{2,1,0:T(8,128)(2,1)}), bf16[128,8,512]{2,1,0:T(8,128)(2,1)S(1)}, u32[]{:S(2)}, u32[]{:S(2)}) async-start(bf16[128,8,512]{2,1,0:T(8,128)(2,1)} %bitcast.13), calls=%async_computation.1 | async-start | bytes 2097152 | tf_op jit(solution)/shard_map/all_to_all | solution.py:421
  34.8 17.9 %all-to-all-done.1 = bf16[128,8,512]{2,1,0:T(8,128)(2,1)S(1)} async-done(((bf16[128,8,512]{2,1,0:T(8,128)(2,1)}), bf16[128,8,512]{2,1,0:T(8,128)(2,1)S(1)}, u32[]{:S(2)}, u32[]{:S(2)}) %all-to-all-start.1) | async-done | bytes 1048608 | tf_op jit(solution)/shard_map/all_to_all | solution.py:421
  54.3 3.2 %collective-permute-start.1 = (bf16[2,128,512]{2,1,0:T(8,128)(2,1)S(1)}, bf16[2,128,512]{2,1,0:T(8,128)(2,1)S(1)}, u32[]{:S(2)}, u32[]{:S(2)}) collective-permute-start(bf16[2,128,512]{2,1,0:T(8,128)(2,1)S(1)} %get-tuple-element.40), channel_id=1, source_target_pairs={{0,32},{16,48},{32,0},{48,16},{1,33},{17,49},{33,1},{49,17},{2,34}... | collective-permute-start | bytes 786440 | tf_op jit(solution)/shard_map/ppermute | solution.py:339
  58.7 3.4 %copy-done = bf16[2048,2048]{1,0:T(8,128)(2,1)S(1)} copy-done((bf16[2048,2048]{1,0:T(8,128)(2,1)S(1)}, bf16[2048,2048]{1,0:T(8,128)(2,1)}, u32[]{:S(2)}) %copy-start) | copy-done | bytes 8388632
  62.1 3.2 %shard_map.108 = (bf16[128,2048]{1,0:T(8,128)(2,1)S(1)}, bf16[128,1024]{1,0:T(8,128)(2,1)}, bf16[128,1024]{1,0:T(8,128)(2,1)}) custom-call(s32[4]{0:T(128)S(1)} %pad_add_fusion.at, bf16[128,2048]{1,0:T(8,128)(2,1)S(1)} %get-tuple-element.35.pooled, f32[128,128]{1,0:T(8,128)S(1)} %get-tuple-element.34.cols, f32[1,2048]{1,0:T(1,128)S(1)} %bitcast.24, ...), custom_call_target="tpu_custom_call" | custom-call | flops 1073741824 | bytes 10485760 | tf_op jit(solution)/shard_map/pallas_call | solution.py:196
  72.1 5.2 %shard_map.109 = bf16[1024,512]{1,0:T(8,128)(2,1)} custom-call(bf16[128,2048]{1,0:T(8,128)(2,1)S(1)} %get-tuple-element.36.dpre, s32[4,128]{1,0:T(4,128)S(1)} %get-tuple-element.37.tgt_r, bf16[2048,2048]{1,0:T(8,128)(2,1)S(1)} %copy-done.1), custom_call_target="tpu_custom_call" | custom-call | flops 2147483648 | bytes 10485760 | tf_op jit(solution)/shard_map/pallas_call | solution.py:221
  77.3 6.6 %all-to-all-start.2 = ((bf16[128,8,512]{2,1,0:T(8,128)(2,1)}), bf16[128,8,512]{2,1,0:T(8,128)(2,1)S(1)}, u32[]{:S(2)}, u32[]{:S(2)}) async-start(bf16[128,8,512]{2,1,0:T(8,128)(2,1)} %bitcast.17), calls=%async_computation.2 | async-start | bytes 2097152 | tf_op jit(solution)/shard_map/all_to_all | solution.py:434
  86.9 2.6 %shard_map.112 = (f32[128,512]{1,0:T(8,128)S(1)}, f32[128,512]{1,0:T(8,128)S(1)}, f32[128,512]{1,0:T(8,128)S(1)}, f32[128,512]{1,0:T(8,128)S(1)}, f32[128,512]{1...) custom-call(s32[4]{0:T(128)S(1)} %pad_add_fusion.at, ...), custom_call_target="tpu_custom_call" | custom-call | flops 1073741824 | bytes 8388608 | tf_op jit(solution)/shard_map/pallas_call | solution.py:275
  90.6 2.7 %collective-permute-start.12 = (f32[128,512]{1,0:T(8,128)S(1)}, f32[128,512]{1,0:T(8,128)S(1)}, u32[]{:S(2)}, u32[]{:S(2)}) collective-permute-start(f32[128,512]{1,0:T(8,128)S(1)} %get-tuple-element.48), channel_id=1, source_target_pairs={{0,8},{4,12},{8,0},{12,4},{1,9},{5,13},{9,1},{13,5},{2,10},{6,14},... | collective-permute-start | bytes 786440 | tf_op jit(solution)/shard_map/ppermute | solution.py:339
  96.2 2.8 %collective-permute-start.15 = (f32[128,512]{1,0:T(8,128)S(1)}, f32[128,512]{1,0:T(8,128)S(1)}, u32[]{:S(2)}, u32[]{:S(2)}) collective-permute-start(f32[128,512]{1,0:T(8,128)S(1)} %get-tuple-element.52), channel_id=1, source_target_pairs={{0,2},{1,3},{2,0},{3,1},{4,6},{5,7},{6,4},{7,5},{8,10},{9,11},{10,... | collective-permute-start | bytes 786440 | tf_op jit(solution)/shard_map/ppermute | solution.py:339
  98.9 4.6 %collective-permute-done.11.refs_1_ = f32[128,512]{1,0:T(8,128)S(1)} collective-permute-done((f32[128,512]{1,0:T(8,128)S(1)}, f32[128,512]{1,0:T(8,128)S(1)}, u32[]{:S(2)}, u32[]{:S(2)}) %collective-permute-start.11) | collective-permute-done | bytes 262176 | tf_op jit(solution)/shard_map/ppermute | solution.py:339
  103.5 2.8 %collective-permute-start.16 = (f32[128,512]{1,0:T(8,128)S(1)}, f32[128,512]{1,0:T(8,128)S(1)}, u32[]{:S(2)}, u32[]{:S(2)}) collective-permute-start(f32[128,512]{1,0:T(8,128)S(1)} %get-tuple-element.53), channel_id=1, source_target_pairs={{0,3},{1,0},{2,1},{3,2},{4,7},{5,4},{6,5},{7,6},{8,11},{9,8},{10,9... | collective-permute-start | bytes 786440 | tf_op jit(solution)/shard_map/ppermute | solution.py:339
  106.3 2.9 %collective-permute-done.12.refs_2_ = f32[128,512]{1,0:T(8,128)S(1)} collective-permute-done((f32[128,512]{1,0:T(8,128)S(1)}, f32[128,512]{1,0:T(8,128)S(1)}, u32[]{:S(2)}, u32[]{:S(2)}) %collective-permute-start.12) | collective-permute-done | bytes 262176 | tf_op jit(solution)/shard_map/ppermute | solution.py:339
  113.6 3.9 %collective-permute-start.18 = (f32[32,512]{1,0:T(8,128)S(1)}, f32[32,512]{1,0:T(8,128)S(1)}, u32[]{:S(2)}, u32[]{:S(2)}) collective-permute-start(f32[32,512]{1,0:T(8,128)S(1)} %get-tuple-element.56), channel_id=1, source_target_pairs={{0,2},{1,3},{2,0},{3,1},{4,6},{5,7},{6,4},{7,5},{8,10},{9,11},{10,... | collective-permute-start | bytes 196616 | tf_op jit(solution)/shard_map/ppermute | solution.py:339
  117.8 2.3 %collective-permute-start.21 = (f32[32,512]{1,0:T(8,128)S(1)}, f32[32,512]{1,0:T(8,128)S(1)}, u32[]{:S(2)}, u32[]{:S(2)}) collective-permute-start(f32[32,512]{1,0:T(8,128)S(1)} %get-tuple-element.60), channel_id=1, source_target_pairs={{0,8},{4,12},{8,0},{12,4},{1,9},{5,13},{9,1},{13,5},{2,10},{6,14},... | collective-permute-start | bytes 196616 | tf_op jit(solution)/shard_map/ppermute | solution.py:339
  120.1 2.6 %collective-permute-start.22 = (f32[32,512]{1,0:T(8,128)S(1)}, f32[32,512]{1,0:T(8,128)S(1)}, u32[]{:S(2)}, u32[]{:S(2)}) collective-permute-start(f32[32,512]{1,0:T(8,128)S(1)} %get-tuple-element.61), channel_id=1, source_target_pairs={{0,12},{4,0},{8,4},{12,8},{1,13},{5,1},{9,5},{13,9},{2,14},{6,2},{... | collective-permute-start | bytes 196616 | tf_op jit(solution)/shard_map/ppermute | solution.py:339
  123.1 3.3 %shard_map.105.count = bf16[2048,1024]{1,0:T(8,128)(2,1)S(1)} custom-call(s32[4,1024]{1,0:T(4,128)S(1)} %reshape.27.ids), custom_call_target="tpu_custom_call" | custom-call | flops 16777216 | bytes 4194304 | tf_op jit(solution)/shard_map/pallas_call | solution.py:359
  129.9 2.2 %copy-done.2 = f32[2048,512]{1,0:T(8,128)S(1)} copy-done((f32[2048,512]{1,0:T(8,128)S(1)}, f32[2048,512]{1,0:T(8,128)}, u32[]{:S(2)}) %copy-start.2) | copy-done | bytes 4194328
  132.1 2.2 %copy-done.4 = bf16[2048,1024]{1,0:T(8,128)(2,1)S(1)} copy-done((bf16[2048,1024]{1,0:T(8,128)(2,1)S(1)}, bf16[2048,1024]{1,0:T(8,128)(2,1)}, u32[]{:S(2)}) %copy-start.4) | copy-done | bytes 4194328
  134.3 6.3 %shard_map.110 = f32[2048,512]{1,0:T(8,128)} custom-call(bf16[2048,1024]{1,0:T(8,128)(2,1)S(1)} %copy-done.4, bf16[1024,512]{1,0:T(8,128)(2,1)S(1)} %bitcast.21, f32[2048,512]{1,0:T(8,128)S(1)} %copy-done.2, f32[2048,128]{1,0:T(8,128)S(1)} %broadcast_in_dim.18.accum), custom_call_target="tpu_custom_call" | custom-call | flops 2147483648 | bytes 13631488 | tf_op jit(solution)/shard_map/pallas_call | solution.py:383
  (73 shorter events, 29.4 us)
Async XLA Ops:
  4.5 20.2 %all-to-all-start = ((s32[128,1,32]{2,1,0:T(1,128)}), s32[128,1,32]{2,1,0:T(1,128)S(1)}, u32[]{:S(2)}, u32[]{:S(2)}) async-start(s32[128,1,32]{2,1,0:T(1,128)} %bitcast.5), calls=%async_computation | async-start | bytes 131072 | tf_op jit(solution)/shard_map/all_to_all | solution.py:419
  30.1 22.6 %all-to-all-start.1 = ((bf16[128,8,512]{2,1,0:T(8,128)(2,1)}), bf16[128,8,512]{2,1,0:T(8,128)(2,1)S(1)}, u32[]{:S(2)}, u32[]{:S(2)}) async-start(bf16[128,8,512]{2,1,0:T(8,128)(2,1)} %bitcast.13), calls=%async_computation.1 | async-start | bytes 2097152 | tf_op jit(solution)/shard_map/all_to_all | solution.py:421
  54.1 13.2 %collective-permute-start = (bf16[2,128,512]{2,1,0:T(8,128)(2,1)S(1)}, bf16[2,128,512]{2,1,0:T(8,128)(2,1)S(1)}, u32[]{:S(2)}, u32[]{:S(2)}) collective-permute-start(bf16[2,128,512]{2,1,0:T(8,128)(2,1)S(1)} %get-tuple-element.39), channel_id=1, source_target_pairs={{0,16},{16,32},{32,48},{48,0},{1,17},{17,33},{33,49},{49,1},{2,18}... | collective-permute-start | bytes 786440 | tf_op jit(solution)/shard_map/ppermute | solution.py:339
  54.3 15.4 %collective-permute-start.1 = (bf16[2,128,512]{2,1,0:T(8,128)(2,1)S(1)}, bf16[2,128,512]{2,1,0:T(8,128)(2,1)S(1)}, u32[]{:S(2)}, u32[]{:S(2)}) collective-permute-start(bf16[2,128,512]{2,1,0:T(8,128)(2,1)S(1)} %get-tuple-element.40), channel_id=1, source_target_pairs={{0,32},{16,48},{32,0},{48,16},{1,33},{17,49},{33,1},{49,17},{2,34}... | collective-permute-start | bytes 786440 | tf_op jit(solution)/shard_map/ppermute | solution.py:339
  57.5 13.7 %collective-permute-start.2 = (bf16[2,128,512]{2,1,0:T(8,128)(2,1)S(1)}, bf16[2,128,512]{2,1,0:T(8,128)(2,1)S(1)}, u32[]{:S(2)}, u32[]{:S(2)}) collective-permute-start(bf16[2,128,512]{2,1,0:T(8,128)(2,1)S(1)} %get-tuple-element.41), channel_id=1, source_target_pairs={{0,48},{16,0},{32,16},{48,32},{1,49},{17,1},{33,17},{49,33},{2,50}... | collective-permute-start | bytes 786440 | tf_op jit(solution)/shard_map/ppermute | solution.py:339
  65.3 18.8 %collective-permute-start.6 = (bf16[128,1024]{1,0:T(8,128)(2,1)}, bf16[128,1024]{1,0:T(8,128)(2,1)}, u32[]{:S(2)}, u32[]{:S(2)}) collective-permute-start(bf16[128,1024]{1,0:T(8,128)(2,1)} %get-tuple-element.45), channel_id=1, source_target_pairs={{0,48},{16,0},{32,16},{48,32},{1,49},{17,1},{33,17},{49,33},{2,50}... | collective-permute-start | bytes 786440 | tf_op jit(solution)/shard_map/ppermute | solution.py:339
  65.3 19.3 %collective-permute-start.4 = (bf16[128,1024]{1,0:T(8,128)(2,1)}, bf16[128,1024]{1,0:T(8,128)(2,1)}, u32[]{:S(2)}, u32[]{:S(2)}) collective-permute-start(bf16[128,1024]{1,0:T(8,128)(2,1)} %get-tuple-element.45), channel_id=1, source_target_pairs={{0,16},{16,32},{32,48},{48,0},{1,17},{17,33},{33,49},{49,1},{2,18}... | collective-permute-start | bytes 786440 | tf_op jit(solution)/shard_map/ppermute | solution.py:339
  67.3 17.4 %collective-permute-start.5 = (bf16[128,1024]{1,0:T(8,128)(2,1)}, bf16[128,1024]{1,0:T(8,128)(2,1)}, u32[]{:S(2)}, u32[]{:S(2)}) collective-permute-start(bf16[128,1024]{1,0:T(8,128)(2,1)} %get-tuple-element.44.refs_0_), channel_id=1, source_target_pairs={{0,32},{16,48},{32,0},{48,16},{1,33},{17,49},{33,1},{49,17},{2,34}... | collective-permute-start | bytes 786440 | tf_op jit(solution)/shard_map/ppermute | solution.py:339
  72.0 14.9 %collective-permute-start.3 = (bf16[512,512]{1,0:T(8,128)(2,1)S(1)}, bf16[512,512]{1,0:T(8,128)(2,1)S(1)}, u32[]{:S(2)}, u32[]{:S(2)}) collective-permute-start(bf16[512,512]{1,0:T(8,128)(2,1)S(1)} %get-tuple-element.43), channel_id=1, source_target_pairs={{0,64},{64,0},{1,65},{65,1},{2,66},{66,2},{3,67},{67,3},{4,68},{68... | collective-permute-start | bytes 1572872 | tf_op jit(solution)/shard_map/ppermute | solution.py:343
  77.3 52.2 %all-to-all-start.2 = ((bf16[128,8,512]{2,1,0:T(8,128)(2,1)}), bf16[128,8,512]{2,1,0:T(8,128)(2,1)S(1)}, u32[]{:S(2)}, u32[]{:S(2)}) async-start(bf16[128,8,512]{2,1,0:T(8,128)(2,1)} %bitcast.17), calls=%async_computation.2 | async-start | bytes 2097152 | tf_op jit(solution)/shard_map/all_to_all | solution.py:434
  84.7 2.2 %collective-permute-start.9 = (bf16[128,1024]{1,0:T(8,128)(2,1)}, bf16[128,1024]{1,0:T(8,128)(2,1)S(1)}, u32[]{:S(2)}, u32[]{:S(2)}) collective-permute-start(bf16[128,1024]{1,0:T(8,128)(2,1)} %collective-permute-done.5.refs_2_), channel_id=1, source_target_pairs={{0,64},{64,0},{1,65},{65,1},{2,66},{66,2},{3,67},{67,3},{4,68},{68... | collective-permute-start | bytes 786440 | tf_op jit(solution)/shard_map/ppermute | solution.py:343
  89.5 14.0 %collective-permute-start.11 = (f32[128,512]{1,0:T(8,128)S(1)}, f32[128,512]{1,0:T(8,128)S(1)}, u32[]{:S(2)}, u32[]{:S(2)}) collective-permute-start(f32[128,512]{1,0:T(8,128)S(1)} %get-tuple-element.47), channel_id=1, source_target_pairs={{0,4},{4,8},{8,12},{12,0},{1,5},{5,9},{9,13},{13,1},{2,6},{6,10},{... | collective-permute-start | bytes 786440 | tf_op jit(solution)/shard_map/ppermute | solution.py:339
  90.6 18.7 %collective-permute-start.12 = (f32[128,512]{1,0:T(8,128)S(1)}, f32[128,512]{1,0:T(8,128)S(1)}, u32[]{:S(2)}, u32[]{:S(2)}) collective-permute-start(f32[128,512]{1,0:T(8,128)S(1)} %get-tuple-element.48), channel_id=1, source_target_pairs={{0,8},{4,12},{8,0},{12,4},{1,9},{5,13},{9,1},{13,5},{2,10},{6,14},... | collective-permute-start | bytes 786440 | tf_op jit(solution)/shard_map/ppermute | solution.py:339
  93.2 16.0 %collective-permute-start.13 = (f32[128,512]{1,0:T(8,128)S(1)}, f32[128,512]{1,0:T(8,128)S(1)}, u32[]{:S(2)}, u32[]{:S(2)}) collective-permute-start(f32[128,512]{1,0:T(8,128)S(1)} %get-tuple-element.49), channel_id=1, source_target_pairs={{0,12},{4,0},{8,4},{12,8},{1,13},{5,1},{9,5},{13,9},{2,14},{6,2},{... | collective-permute-start | bytes 786440 | tf_op jit(solution)/shard_map/ppermute | solution.py:339
  94.7 14.6 %collective-permute-start.14 = (f32[128,512]{1,0:T(8,128)S(1)}, f32[128,512]{1,0:T(8,128)S(1)}, u32[]{:S(2)}, u32[]{:S(2)}) collective-permute-start(f32[128,512]{1,0:T(8,128)S(1)} %get-tuple-element.51), channel_id=1, source_target_pairs={{0,1},{1,2},{2,3},{3,0},{4,5},{5,6},{6,7},{7,4},{8,9},{9,10},{10,1... | collective-permute-start | bytes 786440 | tf_op jit(solution)/shard_map/ppermute | solution.py:339
  96.2 14.9 %collective-permute-start.15 = (f32[128,512]{1,0:T(8,128)S(1)}, f32[128,512]{1,0:T(8,128)S(1)}, u32[]{:S(2)}, u32[]{:S(2)}) collective-permute-start(f32[128,512]{1,0:T(8,128)S(1)} %get-tuple-element.52), channel_id=1, source_target_pairs={{0,2},{1,3},{2,0},{3,1},{4,6},{5,7},{6,4},{7,5},{8,10},{9,11},{10,... | collective-permute-start | bytes 786440 | tf_op jit(solution)/shard_map/ppermute | solution.py:339
  103.5 8.1 %collective-permute-start.16 = (f32[128,512]{1,0:T(8,128)S(1)}, f32[128,512]{1,0:T(8,128)S(1)}, u32[]{:S(2)}, u32[]{:S(2)}) collective-permute-start(f32[128,512]{1,0:T(8,128)S(1)} %get-tuple-element.53), channel_id=1, source_target_pairs={{0,3},{1,0},{2,1},{3,2},{4,7},{5,4},{6,5},{7,6},{8,11},{9,8},{10,9... | collective-permute-start | bytes 786440 | tf_op jit(solution)/shard_map/ppermute | solution.py:339
  112.3 7.8 %collective-permute-start.17 = (f32[32,512]{1,0:T(8,128)S(1)}, f32[32,512]{1,0:T(8,128)S(1)}, u32[]{:S(2)}, u32[]{:S(2)}) collective-permute-start(f32[32,512]{1,0:T(8,128)S(1)} %get-tuple-element.55), channel_id=1, source_target_pairs={{0,1},{1,2},{2,3},{3,0},{4,5},{5,6},{6,7},{7,4},{8,9},{9,10},{10,1... | collective-permute-start | bytes 196616 | tf_op jit(solution)/shard_map/ppermute | solution.py:339
  113.6 14.9 %collective-permute-start.18 = (f32[32,512]{1,0:T(8,128)S(1)}, f32[32,512]{1,0:T(8,128)S(1)}, u32[]{:S(2)}, u32[]{:S(2)}) collective-permute-start(f32[32,512]{1,0:T(8,128)S(1)} %get-tuple-element.56), channel_id=1, source_target_pairs={{0,2},{1,3},{2,0},{3,1},{4,6},{5,7},{6,4},{7,5},{8,10},{9,11},{10,... | collective-permute-start | bytes 196616 | tf_op jit(solution)/shard_map/ppermute | solution.py:339
  117.5 10.9 %collective-permute-start.19 = (f32[32,512]{1,0:T(8,128)S(1)}, f32[32,512]{1,0:T(8,128)S(1)}, u32[]{:S(2)}, u32[]{:S(2)}) collective-permute-start(f32[32,512]{1,0:T(8,128)S(1)} %get-tuple-element.57), channel_id=1, source_target_pairs={{0,3},{1,0},{2,1},{3,2},{4,7},{5,4},{6,5},{7,6},{8,11},{9,8},{10,9... | collective-permute-start | bytes 196616 | tf_op jit(solution)/shard_map/ppermute | solution.py:339
  117.8 10.7 %collective-permute-start.20 = (f32[32,512]{1,0:T(8,128)S(1)}, f32[32,512]{1,0:T(8,128)S(1)}, u32[]{:S(2)}, u32[]{:S(2)}) collective-permute-start(f32[32,512]{1,0:T(8,128)S(1)} %get-tuple-element.59), channel_id=1, source_target_pairs={{0,4},{4,8},{8,12},{12,0},{1,5},{5,9},{9,13},{13,1},{2,6},{6,10},{... | collective-permute-start | bytes 196616 | tf_op jit(solution)/shard_map/ppermute | solution.py:339
  117.8 10.7 %collective-permute-start.21 = (f32[32,512]{1,0:T(8,128)S(1)}, f32[32,512]{1,0:T(8,128)S(1)}, u32[]{:S(2)}, u32[]{:S(2)}) collective-permute-start(f32[32,512]{1,0:T(8,128)S(1)} %get-tuple-element.60), channel_id=1, source_target_pairs={{0,8},{4,12},{8,0},{12,4},{1,9},{5,13},{9,1},{13,5},{2,10},{6,14},... | collective-permute-start | bytes 196616 | tf_op jit(solution)/shard_map/ppermute | solution.py:339
  120.1 8.3 %collective-permute-start.22 = (f32[32,512]{1,0:T(8,128)S(1)}, f32[32,512]{1,0:T(8,128)S(1)}, u32[]{:S(2)}, u32[]{:S(2)}) collective-permute-start(f32[32,512]{1,0:T(8,128)S(1)} %get-tuple-element.61), channel_id=1, source_target_pairs={{0,12},{4,0},{8,4},{12,8},{1,13},{5,1},{9,5},{13,9},{2,14},{6,2},{... | collective-permute-start | bytes 196616 | tf_op jit(solution)/shard_map/ppermute | solution.py:339
  129.1 11.5 %collective-permute-start.23 = (f32[16,1024]{1,0:T(8,128)S(1)}, f32[16,1024]{1,0:T(8,128)S(1)}, u32[]{:S(2)}, u32[]{:S(2)}) collective-permute-start(f32[16,1024]{1,0:T(8,128)S(1)} %get-tuple-element.63), channel_id=1, source_target_pairs={{0,16},{16,0},{32,48},{48,32},{1,17},{17,1},{33,49},{49,33},{2,18}... | collective-permute-start | bytes 196616 | tf_op jit(solution)/shard_map/ppermute | solution.py:447
  (15 other events, 136.5 us)

commit v4 on v3

v4 whole, which is shorter than its diff:
```python
import functools
import itertools

import jax
import jax.numpy as jnp
from jax import lax
from jax.experimental import pallas as pl
from jax.experimental.pallas import tpu as pltpu
from jax.sharding import Mesh, PartitionSpec as P

learn_rate = 0.1
AXES = ("role", "z", "x", "y")
BF = jnp.bfloat16
F32 = jnp.float32
I32 = jnp.int32


def iota(shape, dim):
    return lax.broadcasted_iota(I32, shape, dim)


def dot(a, b):
    return jnp.dot(a, b, preferred_element_type=F32)


def dot_t(a, b):
    return lax.dot_general(a, b, (((1,), (1,)), ((), ())), preferred_element_type=F32)


def params(mib):
    return pltpu.CompilerParams(vmem_limit_bytes=mib << 20)


def cost(flops, nbytes):
    return pl.CostEstimate(flops=flops, bytes_accessed=nbytes, transcendentals=0)


SMEM = pl.BlockSpec(memory_space=pltpu.SMEM)
VMEM = pl.BlockSpec(memory_space=pltpu.VMEM)
HBM = pl.BlockSpec(memory_space=pltpu.HBM)


def struct(shape, dtype):
    return jax.ShapeDtypeStruct(shape, dtype)


def split_int(v):
    return (v >> 6).astype(F32).astype(BF), (v & 63).astype(F32).astype(BF)


def route_kernel(*refs):
    hbm, (out, cols, tgt_r), local, sems = refs[:4], refs[4:7], refs[7:11], refs[11]
    copies = [pltpu.make_async_copy(a, b, sems.at[k]) for k, (a, b) in enumerate(zip(hbm, local))]
    for copy in copies:
        copy.start()
    for copy in copies:
        copy.wait()
    own, rows, lens, labels = local
    features, bag_len, samples = rows.shape
    devices, width = out.shape
    cap = width // bag_len
    bags = samples * features
    sub = iota((devices, samples), 0)
    hot = jnp.concatenate([(own[f] == sub).astype(F32) for f in range(features)], axis=1)
    hot_bf = hot.astype(BF)
    upper = (iota((bags, bags), 0) < iota((bags, bags), 1)).astype(F32).astype(BF)
    rank = jnp.sum(dot(hot_bf, upper) * hot, axis=0, keepdims=True).astype(I32)
    column = iota((width, bags), 0)
    wanted = jnp.zeros((width, bags), I32)
    for j in range(bag_len):
        value = jnp.concatenate(
            [
                jnp.where(j < lens[f : f + 1, :], rows[f, j : j + 1, :] + 1, 0)
                for f in range(features)
            ],
            axis=1,
        )
        wanted = jnp.where(column == j * cap + rank, value, wanted)
    hi, lo = split_int(wanted)
    out[...] = dot_t(hot_bf, hi).astype(I32) * 64 + dot_t(hot_bf, lo).astype(I32) - 1
    line = iota((samples, samples), 0)
    flat = jnp.where(line == features, labels[...].astype(F32), 0.0)
    for f in range(features):
        target = own[f] * cap + rank[:, f * samples : (f + 1) * samples]
        tgt_r[f : f + 1, :] = target
        flat = jnp.where(line == f, target.astype(F32), flat)
    cols[...] = flat.T


def route(own, rows, lens, labels, devices, cap):
    features, bag_len, samples = rows.shape
    return pl.pallas_call(
        route_kernel,
        in_specs=[HBM] * 4,
        out_shape=(
            struct((devices, bag_len * cap), I32),
            struct((samples, samples), F32),
            struct((features, samples), I32),
        ),
        scratch_shapes=[pltpu.VMEM(v.shape, v.dtype) for v in (own, rows, lens, labels)]
        + [pltpu.SemaphoreType.DMA((4,))],
        compiler_params=params(58),
    )(own, rows, lens, labels)


def lookup_kernel(bag_len, block, ids, table, out):
    sources, width = ids.shape
    cap = width // bag_len
    slots = block * cap
    depth = table.shape[0]
    rep = (iota((slots, block), 0) // cap == iota((slots, block), 1)).astype(F32).astype(BF)
    mine = (iota((slots, width), 1) % cap == iota((slots, width), 0) % cap).astype(F32)
    spread = iota((width, bag_len * 128), 0) // cap == iota((width, bag_len * 128), 1) // 128
    spread = spread.astype(F32).astype(BF)
    lane = iota((slots, 128), 1)
    low, high = (lane % 64).astype(F32), (lane // 64).astype(F32)
    one, zero = jnp.ones((), BF), jnp.zeros((), BF)

    for i in range(sources // block):
        wanted = ids[i * block : (i + 1) * block, :]
        hi, lo = split_int(jnp.where(wanted < 0, 4095, wanted))
        hi = dot((dot(rep, hi) * mine).astype(BF), spread)
        lo = dot((dot(rep, lo) * mine).astype(BF), spread)
        near = []
        for j in range(bag_len):
            part = slice(j * 128, (j + 1) * 128)
            near.append(jnp.where(lo[:, part] == low, hi[:, part] - high, -1.0).astype(BF))
        pieces = []
        for k in range(depth // 128):
            at = jnp.asarray(2.0 * k, BF)
            count = jnp.where(near[0] == at, one, zero)
            for j in range(1, bag_len):
                count = count + jnp.where(near[j] == at, one, zero)
            pieces.append(count)
        total = dot(jnp.concatenate(pieces, axis=1), table[...])
        out[i * slots : (i + 1) * slots, :] = total.astype(BF)


def lookup(ids, table, bag_len):
    sources, width = ids.shape
    depth, wide = table.shape
    cap = width // bag_len
    return pl.pallas_call(
        functools.partial(lookup_kernel, bag_len, 32),
        in_specs=[VMEM, VMEM],
        out_specs=VMEM,
        out_shape=struct((sources * cap, wide), BF),
        compiler_params=params(24),
        cost_estimate=cost(2 * sources * cap * depth * wide, 4 << 20),
    )(ids, table)


def forward_kernel(features, at, slots, cols, bias, head, w, early, *refs):
    own, give, dpre_out, bags, blocks, quarters = refs
    total, wide = slots.shape
    samples, hidden = dpre_out.shape
    lane = iota((samples, total), 1).astype(F32)
    for f in range(features):
        pick = (cols[:, f : f + 1] == lane).astype(F32).astype(BF)
        bags[f] = dot(pick, slots[...]).astype(BF)
    for k in range(2):
        blocks[k] = bags[k]
        for z in range(4):
            start = (z % 2) * 256 + k * 128
            blocks[2 + k, :, z * 128 : (z + 1) * 128] = bags[2 + z // 2, :, start : start + 128]
    pre = bias[...]
    for f in range(features):
        pre = pre + dot(bags[f], w[f * wide : (f + 1) * wide, :])
    sig = jax.nn.sigmoid(pre)
    logit = jnp.sum(pre * sig * head[...], axis=1, keepdims=True)
    dlogit = jax.nn.sigmoid(logit) - cols[:, features : features + 1]
    dpre = (dlogit * head[...] * sig * (1.0 + pre * (1.0 - sig))).astype(BF)
    dpre_out[...] = dpre
    for q in range(4):
        quarters[q] = dpre[:, q * wide : (q + 1) * wide]
    for packs, role, ring in ((own, at[0], at[1]), (give, 1 - at[0], at[2])):
        for s in range(4):
            to = (ring + s) % 4
            packs[s, 0] = blocks[2 * role + to // 2]
            packs[s, 1] = quarters[2 * (to % 2)]
            packs[s, 2] = quarters[2 * (to % 2) + 1]


def forward(at, slots, cols, bias, head, w, features, early):
    samples, hidden = cols.shape[0], w.shape[1]
    wide = slots.shape[1]
    return pl.pallas_call(
        functools.partial(forward_kernel, features),
        in_specs=[SMEM] + [VMEM] * 5 + [HBM],
        out_specs=[VMEM] * 3,
        out_shape=[struct((4, 3, samples, wide), BF)] * 2 + [struct((samples, hidden), BF)],
        scratch_shapes=[pltpu.VMEM((4, samples, wide), BF)] * 3,
        compiler_params=params(20),
        cost_estimate=cost(2 * samples * w.size, 10 << 20),
    )(at, slots, cols, bias, head, w, early)


def merge_kernel(own, got, *outs):
    for s, out in enumerate(outs):
        out[0] = own[s]
        out[1] = got[s]


def merge(own, got):
    ring, *rest = own.shape
    return pl.pallas_call(
        merge_kernel,
        in_specs=[VMEM] * 2,
        out_specs=[VMEM] * ring,
        out_shape=[struct((2, *rest), BF)] * ring,
        compiler_params=params(16),
        cost_estimate=cost(1 << 20, 6 << 20),
    )(own, got)


def backward_kernel(dpre, tgt_r, w, sending):
    features, samples = tgt_r.shape
    total, wide = sending.shape
    sub = iota((total, samples), 0)
    acc = jnp.zeros((total, wide), F32)
    for f in range(features):
        grad = dot_t(dpre[...], w[f * wide : (f + 1) * wide, :]).astype(BF)
        put = (tgt_r[f : f + 1, :] == sub).astype(F32).astype(BF)
        acc += dot(put, grad)
    sending[...] = acc.astype(BF)


def backward(dpre, tgt_r, w, total):
    features, samples = tgt_r.shape
    wide = w.shape[0] // features
    return pl.pallas_call(
        backward_kernel,
        in_specs=[VMEM] * 3,
        out_specs=VMEM,
        out_shape=struct((total, wide), BF),
        compiler_params=params(24),
        cost_estimate=cost(8 * samples * w.size, 10 << 20),
    )(dpre, tgt_r, w)


def weight_kernel(at, *refs):
    packs, outs, acc = refs[:4], refs[4:8], refs[8]
    half = acc.shape[1] // 2
    left = jnp.concatenate([pack[k, 0] for pack in packs for k in range(2)], axis=0)
    for q in range(2):
        right = jnp.concatenate([pack[k, 1 + q] for pack in packs for k in range(2)], axis=0)
        acc[:, q * half : (q + 1) * half] = lax.dot_general(
            left, right, (((0,), (0,)), ((), ())), preferred_element_type=F32
        )
    for s in range(4):
        first = (at[3] + s) % 4
        for p in range(2):
            for q in range(4):
                row = jnp.where(
                    at[0] == 0,
                    p * 256 + first * 64 + q * 16,
                    q * 128 + p * 64 + first * 16,
                )
                k = (p * 4 + q) * 16
                outs[s][k : k + 16, :] = acc[pl.ds(pl.multiple_of(row, 16), 16), :]


def weight_part(at, packs):
    *_, samples, wide = packs[0].shape
    return pl.pallas_call(
        weight_kernel,
        in_specs=[SMEM] + [VMEM] * 4,
        out_specs=[VMEM] * 4,
        out_shape=[struct((wide // 4, 2 * wide), F32)] * 4,
        scratch_shapes=[pltpu.VMEM((wide, 2 * wide), F32)],
        compiler_params=params(24),
        cost_estimate=cost(32 * wide * samples * wide, 8 << 20),
    )(at, *packs)


def middle_kernel(at, *refs):
    parts, outs, acc = refs[:4], refs[4:8], refs[8]
    acc[...] = (parts[0][...] + parts[1][...]) + (parts[2][...] + parts[3][...])
    for s in range(4):
        second = (at[4] + s) % 4
        for p in range(2):
            row = pl.multiple_of(p * 64 + second * 16, 16)
            outs[s][p * 16 : (p + 1) * 16, :] = acc[pl.ds(row, 16), :]


def middle(at, parts):
    rows, wide = parts[0].shape
    return pl.pallas_call(
        middle_kernel,
        in_specs=[SMEM] + [VMEM] * 4,
        out_specs=[VMEM] * 4,
        out_shape=[struct((rows // 4, wide), F32)] * 4,
        scratch_shapes=[pltpu.VMEM((rows, wide), F32)],
        compiler_params=params(12),
        cost_estimate=cost(1 << 20, 3 << 20),
    )(at, *parts)


def last_kernel(at, *refs):
    parts, keep, give = refs[:4], refs[4], refs[5]
    acc = (parts[0][...] + parts[1][...]) + (parts[2][...] + parts[3][...])
    even = at[1] % 2 == 0
    keep[...] = jnp.where(even, acc[:16], acc[16:])
    give[...] = jnp.where(even, acc[16:], acc[:16])


def last(at, parts):
    rows, wide = parts[0].shape
    return pl.pallas_call(
        last_kernel,
        in_specs=[SMEM] + [VMEM] * 4,
        out_specs=[VMEM] * 2,
        out_shape=[struct((rows // 2, wide), F32)] * 2,
        compiler_params=params(12),
        cost_estimate=cost(1 << 16, 1 << 18),
    )(at, *parts)


def device(place):
    role, z, x, y = place
    return ((role * 4 + z) * 4 + x) * 4 + y


def along(value, axes, move):
    pairs = []
    for here in itertools.product(range(2), range(4), range(4), range(4)):
        to = list(here)
        axis = axes[here[0]]
        to[axis] = move(here[axis])
        pairs.append((device(here), device(to)))
    return lax.ppermute(value, AXES, pairs)


def around(values, axes):
    return [values[0]] + [
        along(value, axes, lambda i, s=s: (i + s) % 4) for s, value in enumerate(values) if s
    ]


def near_kernel(ids, near):
    bag_len, rows, slots = near.shape
    row = iota((rows, slots), 0)
    low, high = (row % 64).astype(F32), (row // 64).astype(F32)
    wanted = ids[...]
    wanted = jnp.where(wanted < 0, 4095, wanted)
    hi, lo = (wanted >> 6).astype(F32), (wanted & 63).astype(F32)
    for j in range(bag_len):
        part = jnp.where(lo[j : j + 1] == low, hi[j : j + 1] - high, -1.0)
        near[j] = part.astype(BF)


def nearby(ids):
    bag_len, slots = ids.shape
    return pl.pallas_call(
        near_kernel,
        in_specs=[VMEM],
        out_specs=VMEM,
        out_shape=struct((bag_len, 128, slots), BF),
        compiler_params=params(12),
        cost_estimate=cost(1 << 34, 1 << 20),
    )(ids)


def update_kernel(near, grads, table, accum, out):
    block, wide = table.shape
    bag_len, _, slots = near.shape
    step = pl.program_id(0)
    one, zero = jnp.ones((), BF), jnp.zeros((), BF)
    pieces, before = [], []
    for k in range(block // 128):
        chunk = step * (block // 128) + k
        here = jnp.full((128, slots), (2 * chunk).astype(F32), F32).astype(BF)
        count = jnp.where(near[0] == here, one, zero)
        for j in range(1, bag_len):
            count = count + jnp.where(near[j] == here, one, zero)
        pieces.append(count)
        before.append(jnp.broadcast_to(accum[pl.ds(chunk, 1), :], (128, 128)).T[:, 0:1])
    row_grad = dot(jnp.concatenate(pieces, axis=0), grads[...])
    square = jnp.sum(row_grad * row_grad, axis=1, keepdims=True)
    new_accum = jnp.concatenate(before, axis=0) + square * (1.0 / wide)
    out[...] = table[...] - row_grad * (learn_rate / jnp.sqrt(new_accum + 1e-6))


def update(near, grads, table, accum):
    rows, wide = table.shape
    slots = grads.shape[0]
    block = 512
    return pl.pallas_call(
        update_kernel,
        grid=(rows // block,),
        in_specs=[
            pl.BlockSpec(near.shape, lambda i: (0, 0, 0)),
            pl.BlockSpec((slots, wide), lambda i: (0, 0)),
            pl.BlockSpec((block, wide), lambda i: (i, 0)),
            pl.BlockSpec(accum.shape, lambda i: (0, 0)),
        ],
        out_specs=pl.BlockSpec((block, wide), lambda i: (i, 0)),
        out_shape=struct((rows, wide), F32),
        compiler_params=params(58),
        cost_estimate=cost(4 * rows * slots * wide, 9 << 20),
    )(near, grads, table, accum)


def per_device(
    emb_table, row_accum, owners, local_rows, lengths, labels, w_hidden, hidden_bias, w_logit
):
    devices = lax.axis_size(AXES)
    samples, features, bag_len = local_rows.shape
    rows_dev, width = emb_table.shape
    cap = 2 * samples * features // devices
    role, z, x, y = (lax.axis_index(axis) for axis in AXES)
    odd = role == 1
    at = jnp.stack(
        [
            role,
            jnp.where(odd, x, z),
            jnp.where(odd, z, x),
            jnp.where(odd, y, x),
            jnp.where(odd, z, y),
        ]
    ).astype(I32)
    outgoing, cols, tgt_r = route(
        owners.transpose(1, 2, 0),
        local_rows.transpose(1, 2, 0),
        lengths.T,
        labels[None, :],
        devices,
        cap,
    )
    table_bf = emb_table.astype(BF)
    incoming = lax.all_to_all(outgoing, AXES, split_axis=0, concat_axis=0, tiled=True)
    found = lookup(incoming, table_bf, bag_len)
    slots = lax.all_to_all(
        found.reshape(devices, cap, width), AXES, split_axis=0, concat_axis=0, tiled=True
    ).reshape(devices * cap, width)
    ids_r = incoming.reshape(devices, bag_len, cap).transpose(1, 0, 2).reshape(bag_len, -1)
    near = nearby(ids_r)
    own, give, dpre = forward(
        at, slots, cols, hidden_bias[None, :], w_logit[None, :], w_hidden, features, near
    )
    got = lax.ppermute(give, "role", [(0, 1), (1, 0)])
    sending = backward(dpre, tgt_r, w_hidden, devices * cap)
    packs = around(merge(own, got), (1, 2))
    *parts, sending = lax.optimization_barrier((*weight_part(at, packs), sending))
    received = lax.all_to_all(
        sending.reshape(devices, cap, width), AXES, split_axis=0, concat_axis=0, tiled=True
    )
    new_table = update(
        near, received.reshape(devices * cap, width), emb_table, row_accum.reshape(-1, 128)
    )
    parts = around(parts, (2, 3))
    parts = around(middle(at, parts), (3, 1))
    *parts, new_table = lax.optimization_barrier((*parts, new_table))
    mine, give = last(at, parts)
    got = along(give, (1, 2), lambda i: i ^ 1)
    even = at[1] % 2 == 0
    w_grad = jnp.concatenate([jnp.where(even, mine, got), jnp.where(even, got, mine)], axis=1)
    return (new_table, w_grad)


def solution(mesh):
    split = Mesh(mesh.devices.reshape(2, 4, 4, 4), AXES)
    placed = (
        P(AXES, None),
        P(AXES),
        P(AXES, None, None),
        P(AXES, None, None),
        P(AXES, None),
        P(AXES),
        P(),
        P(),
        P(),
    )
    return jax.shard_map(
        per_device,
        mesh=split,
        in_specs=placed,
        out_specs=(P(AXES, None), P(AXES, None)),
        check_vma=False,
    )
```

time: 142 us -> 140 us (0.986)
  waiting for transfers between devices: 38.4 us -> 59.3 us
  starting transfers between devices: 55 us -> 39.8 us
  local copies, waits for them, and re-layouts: 13.2 us -> 9.01 us
  Pallas kernels: 30.6 us -> 27.2 us
    ppermute x24 -> x11, waiting for transfers between devices: 13.9 us -> 35.5 us  [the longest x10 32.1 us: along(): return lax.ppermute(value, AXES, pairs)]
    ppermute x24 -> x11, starting transfers between devices: 32.6 us -> 17.3 us  [the longest x10 17.2 us: along(): return lax.ppermute(value, AXES, pairs)]
    pallas_call x8 -> x7, Pallas kernels: 15.9 us -> 10.9 us  [the longest x1 5.35 us: lookup(): pl.pallas_call(functools.partial(lookup_kernel, bag_len, 32), in_specs=[V...]
    unnamed x24 -> x20, local copies, waits for them, and re-layouts: 12.5 us -> 8.55 us
    pallas_call x1, Pallas kernels: 6.31 us -> 7.86 us  [update(): pl.pallas_call(update_kernel, grid=(rows // block,), in_specs=[pl.BlockSp...]
  transfers between devices with their start and end apart: 27 -> 14, of which waited for: 12 -> 9; matrix products, arithmetic and copies ran while one was open for 2% -> 2% of each run, Pallas kernels for 16% -> 10%
where the time goes in v4:
time: 140 us; the launch traced here: 139 us
  waiting for transfers between devices  59.3 us (42%)
  starting transfers between devices  39.8 us (28%)
  Pallas kernels  27.2 us (19%)
  local copies, waits for them, and re-layouts  9.01 us (6%)
  other arithmetic  3.14 us (2%)
    ppermute x10, waiting for transfers between devices, along(): return lax.ppermute(value, AXES, pairs)  32.1 us
    all_to_all x1, waiting for transfers between devices, per_device(): lax.all_to_all(found.reshape(devices, cap, width), AXES, split_axis=0, co...  17.3 us
    ppermute x10, starting transfers between devices, along(): return lax.ppermute(value, AXES, pairs)  17.2 us
    all_to_all x1, starting transfers between devices, per_device(): lax.all_to_all(outgoing, AXES, split_axis=0, concat_axis=0, tiled=True)  11.1 us
    unnamed x20, local copies, waits for them, and re-layouts  8.55 us
    pallas_call x1, Pallas kernels, update(): pl.pallas_call(update_kernel, grid=(rows // block,), in_specs=[pl.BlockSp...  7.86 us
    all_to_all x1, starting transfers between devices, per_device(): lax.all_to_all(sending.reshape(devices, cap, width), AXES, split_axis=0,...  6.68 us
    all_to_all x1, waiting for transfers between devices, per_device(): lax.all_to_all(outgoing, AXES, split_axis=0, concat_axis=0, tiled=True)  6.48 us
  transfers between devices with their start and end apart: 14, of which 9 were waited for; matrix products, arithmetic and copies ran while one was open for 2% of the time, Pallas kernels for 10%

profile of v4, /device:TPU:0, one launch (start us, length us, event | category | flops | bytes accessed | tf_op | source)
XLA Modules:
  0.0 139.2 jit_solution(1329810966608032524)
XLA Ops:
  0.6 1.9 %shard_map.104 = (s32[128,32]{1,0:T(8,128)}, f32[128,128]{1,0:T(8,128)}, s32[4,128]{1,0:T(4,128)}) custom-call(s32[4,1,128]{2,1,0:T(1,128)} %bitcast.31, s32[4,4,128]{2,1,0:T(4,128)} %bitcast.30, s32[4,128]{1,0:T(4,128)} %bitcast.32, s32[1,128]{1,0:T(1,128)} %bitcast.33), custom_call_target="tpu_custom_call" | custom-call | tf_op jit(solution)/shard_map/pallas_call | solution.py:92
  2.5 11.1 %all-to-all-start = ((s32[128,1,32]{2,1,0:T(1,128)}), s32[128,1,32]{2,1,0:T(1,128)S(1)}, u32[]{:S(2)}, u32[]{:S(2)}) async-start(s32[128,1,32]{2,1,0:T(1,128)} %bitcast.29), calls=%async_computation | async-start | bytes 131072 | tf_op jit(solution)/shard_map/all_to_all | solution.py:431
  13.7 2.5 %convert_element_type.3.table = bf16[2048,512]{1,0:T(8,128)(2,1)S(1)} convert(f32[2048,512]{1,0:T(8,128)} %table.1) | non-fusion elementwise | flops 1048576 | bytes 6291456 | tf_op jit(solution)/shard_map/convert_element_type | solution.py:430
  16.2 6.5 %all-to-all-done = s32[128,1,32]{2,1,0:T(1,128)S(1)} async-done(((s32[128,1,32]{2,1,0:T(1,128)}), s32[128,1,32]{2,1,0:T(1,128)S(1)}, u32[]{:S(2)}, u32[]{:S(2)}) %all-to-all-start) | async-done | bytes 16416 | tf_op jit(solution)/shard_map/all_to_all | solution.py:431
  22.7 5.4 %shard_map.105 = bf16[1024,512]{1,0:T(8,128)(2,1)} custom-call(s32[128,32]{1,0:T(8,128)S(1)} %bitcast.24, bf16[2048,512]{1,0:T(8,128)(2,1)S(1)} %convert_element_type.3.table), custom_call_target="tpu_custom_call" | custom-call | flops 2147483648 | bytes 4194304 | tf_op jit(solution)/shard_map/pallas_call | solution.py:143
  28.1 4.6 %all-to-all-start.1 = ((bf16[128,8,512]{2,1,0:T(8,128)(2,1)}), bf16[128,8,512]{2,1,0:T(8,128)(2,1)S(1)}, u32[]{:S(2)}, u32[]{:S(2)}) async-start(bf16[128,8,512]{2,1,0:T(8,128)(2,1)} %bitcast.12), calls=%async_computation.1 | async-start | bytes 2097152 | tf_op jit(solution)/shard_map/all_to_all | solution.py:433
  33.4 17.3 %all-to-all-done.1 = bf16[128,8,512]{2,1,0:T(8,128)(2,1)S(1)} async-done(((bf16[128,8,512]{2,1,0:T(8,128)(2,1)}), bf16[128,8,512]{2,1,0:T(8,128)(2,1)S(1)}, u32[]{:S(2)}, u32[]{:S(2)}) %all-to-all-start.1) | async-done | bytes 1048608 | tf_op jit(solution)/shard_map/all_to_all | solution.py:433
  50.7 3.4 %copy-done = bf16[2048,2048]{1,0:T(8,128)(2,1)S(1)} copy-done((bf16[2048,2048]{1,0:T(8,128)(2,1)S(1)}, bf16[2048,2048]{1,0:T(8,128)(2,1)}, u32[]{:S(2)}) %copy-start) | copy-done | bytes 8388632
  54.1 3.2 %shard_map.107 = (bf16[4,3,128,512]{3,2,1,0:T(8,128)(2,1)S(1)}, bf16[4,3,128,512]{3,2,1,0:T(8,128)(2,1)S(1)}, bf16[128,2048]{1,0:T(8,128)(2,1)S(1)}) custom-call(s32[5]{0:T(128)S(1)} %stack.23.at, bf16[1024,512]{1,0:T(8,128)(2,1)S(1)} %bitcast.23, f32[128,128]{1,0:T(8,128)S(1)} %copy-done.3, f32[1,2048]{1,0:T(1,128)S(1)} %bitcast.25, ...), custom_call_target="tpu_custom_call" | custom-call | flops 1073741824 | bytes 10485760 | tf_op jit(solution)/shard_map/pallas_call | solution.py:187
  57.4 3.4 %collective-permute-done.got = bf16[4,3,128,512]{3,2,1,0:T(8,128)(2,1)S(1)} collective-permute-done((bf16[4,3,128,512]{3,2,1,0:T(8,128)(2,1)S(1)}, bf16[4,3,128,512]{3,2,1,0:T(8,128)(2,1)S(1)}, u32[]{:S(2)}, u32[]{:S(2)}) %collective-permute-start) | collective-permute-done | bytes 1572896 | tf_op jit(solution)/shard_map/ppermute | solution.py:441
  61.2 3.2 %collective-permute-start.2 = (bf16[2,3,128,512]{3,2,1,0:T(8,128)(2,1)S(1)}, bf16[2,3,128,512]{3,2,1,0:T(8,128)(2,1)S(1)}, u32[]{:S(2)}, u32[]{:S(2)}) collective-permute-start(bf16[2,3,128,512]{3,2,1,0:T(8,128)(2,1)S(1)} %get-tuple-element.38), channel_id=1, source_target_pairs={{0,32},{1,33},{2,34},{3,35},{4,36},{5,37},{6,38},{7,39},{8,40},{9,... | collective-permute-start | bytes 2359304 | tf_op jit(solution)/shard_map/ppermute | solution.py:331
  65.6 3.4 %copy-done.1 = bf16[2048,2048]{1,0:T(8,128)(2,1)S(1)} copy-done((bf16[2048,2048]{1,0:T(8,128)(2,1)S(1)}, bf16[2048,2048]{1,0:T(8,128)(2,1)}, u32[]{:S(2)}) %copy-start.1) | copy-done | bytes 8388632
  68.9 5.2 %shard_map.110 = bf16[1024,512]{1,0:T(8,128)(2,1)} custom-call(bf16[128,2048]{1,0:T(8,128)(2,1)S(1)} %get-tuple-element.44.dpre, s32[4,128]{1,0:T(4,128)S(1)} %copy-done.8, bf16[2048,2048]{1,0:T(8,128)(2,1)S(1)} %copy-done.1), custom_call_target="tpu_custom_call" | custom-call | flops 4294967296 | bytes 10485760 | tf_op jit(solution)/shard_map/pallas_call | solution.py:231
  74.2 8.5 %collective-permute-done.2.refs_2_ = bf16[2,3,128,512]{3,2,1,0:T(8,128)(2,1)S(1)} collective-permute-done((bf16[2,3,128,512]{3,2,1,0:T(8,128)(2,1)S(1)}, bf16[2,3,128,512]{3,2,1,0:T(8,128)(2,1)S(1)}, u32[]{:S(2)}, u32[]{:S(2)}) %collective-permute-start.2) | collective-permute-done | bytes 786464 | tf_op jit(solution)/shard_map/ppermute | solution.py:331
  83.6 2.0 %shard_map.109 = (f32[128,1024]{1,0:T(8,128)S(1)}, f32[128,1024]{1,0:T(8,128)S(1)}, f32[128,1024]{1,0:T(8,128)S(1)}, f32[128,1024]{1,0:T(8,128)S(1)}) custom-call(s32[5]{0:T(128)S(1)} %stack.23.at, bf16[2,3,128,512]{3,2,1,0:T(8,128)(2,1)S(1)} %get-tuple-element.36.refs_0_, bf16[2,3,128,512]{3,2,1,0:T(8,128)(2,1)S(1)} %collective-permute-done.1.refs_1_, ...), custom_call_target="tpu_custom_call" | custom-call | flops 1073741824 | bytes 8388608 | tf_op jit(solution)/shard_map/pallas_call | solution.py:265
  86.3 6.7 %all-to-all-start.2 = ((bf16[128,8,512]{2,1,0:T(8,128)(2,1)}), bf16[128,8,512]{2,1,0:T(8,128)(2,1)S(1)}, u32[]{:S(2)}, u32[]{:S(2)}) async-start(bf16[128,8,512]{2,1,0:T(8,128)(2,1)} %bitcast.18), calls=%async_computation.2 | async-start | bytes 2097152 | tf_op jit(solution)/shard_map/all_to_all | solution.py:445
  94.1 2.7 %collective-permute-start.5 = (f32[128,1024]{1,0:T(8,128)S(1)}, f32[128,1024]{1,0:T(8,128)S(1)}, u32[]{:S(2)}, u32[]{:S(2)}) collective-permute-start(f32[128,1024]{1,0:T(8,128)S(1)} %get-tuple-element.48), channel_id=1, source_target_pairs={{0,8},{1,9},{2,10},{3,11},{4,12},{5,13},{6,14},{7,15},{8,0},{9,1},... | collective-permute-start | bytes 1572872 | tf_op jit(solution)/shard_map/ppermute | solution.py:331
  98.2 14.2 %collective-permute-done.4.refs_1_ = f32[128,1024]{1,0:T(8,128)S(1)} collective-permute-done((f32[128,1024]{1,0:T(8,128)S(1)}, f32[128,1024]{1,0:T(8,128)S(1)}, u32[]{:S(2)}, u32[]{:S(2)}) %collective-permute-start.4) | collective-permute-done | bytes 524320 | tf_op jit(solution)/shard_map/ppermute | solution.py:331
  112.4 5.9 %collective-permute-done.5.refs_2_ = f32[128,1024]{1,0:T(8,128)S(1)} collective-permute-done((f32[128,1024]{1,0:T(8,128)S(1)}, f32[128,1024]{1,0:T(8,128)S(1)}, u32[]{:S(2)}, u32[]{:S(2)}) %collective-permute-start.5) | collective-permute-done | bytes 524320 | tf_op jit(solution)/shard_map/ppermute | solution.py:331
  119.0 1.5 %collective-permute-start.7 = (f32[32,1024]{1,0:T(8,128)S(1)}, f32[32,1024]{1,0:T(8,128)S(1)}, u32[]{:S(2)}, u32[]{:S(2)}) collective-permute-start(f32[32,1024]{1,0:T(8,128)S(1)} %get-tuple-element.51), channel_id=1, source_target_pairs={{0,1},{1,2},{2,3},{3,0},{4,5},{5,6},{6,7},{7,4},{8,9},{9,10},{10,1... | collective-permute-start | bytes 393224 | tf_op jit(solution)/shard_map/ppermute | solution.py:331
  120.6 2.8 %collective-permute-start.8 = (f32[32,1024]{1,0:T(8,128)S(1)}, f32[32,1024]{1,0:T(8,128)S(1)}, u32[]{:S(2)}, u32[]{:S(2)}) collective-permute-start(f32[32,1024]{1,0:T(8,128)S(1)} %get-tuple-element.52), channel_id=1, source_target_pairs={{0,2},{1,3},{2,0},{3,1},{4,6},{5,7},{6,4},{7,5},{8,10},{9,11},{10,... | collective-permute-start | bytes 393224 | tf_op jit(solution)/shard_map/ppermute | solution.py:331
  125.7 7.9 %shard_map.112 = f32[2048,512]{1,0:T(8,128)} custom-call(bf16[4,128,1024]{2,1,0:T(8,128)(2,1)} %copy-done.2, bf16[1024,512]{1,0:T(8,128)(2,1)} %bitcast.27, f32[2048,512]{1,0:T(8,128)} %table.1, f32[16,128]{1,0:T(8,128)} %bitcast.34), custom_call_target="tpu_custom_call" | custom-call | flops 4294967296 | bytes 9437184 | tf_op jit(solution)/shard_map/pallas_call | solution.py:388
  134.2 1.8 %collective-permute-start.10 = (f32[16,1024]{1,0:T(8,128)S(1)}, f32[16,1024]{1,0:T(8,128)S(1)}, u32[]{:S(2)}, u32[]{:S(2)}) collective-permute-start(f32[16,1024]{1,0:T(8,128)S(1)} %get-tuple-element.61), channel_id=1, source_target_pairs={{0,16},{1,17},{2,18},{3,19},{4,20},{5,21},{6,22},{7,23},{8,24},{9,... | collective-permute-start | bytes 196616 | tf_op jit(solution)/shard_map/ppermute | solution.py:331
  136.0 2.5 %collective-permute-done.10 = f32[16,1024]{1,0:T(8,128)S(1)} collective-permute-done((f32[16,1024]{1,0:T(8,128)S(1)}, f32[16,1024]{1,0:T(8,128)S(1)}, u32[]{:S(2)}, u32[]{:S(2)}) %collective-permute-start.10) | collective-permute-done | bytes 65568 | tf_op jit(solution)/shard_map/ppermute | solution.py:331
  (41 shorter events, 10.9 us)
Async XLA Ops:
  2.5 20.2 %all-to-all-start = ((s32[128,1,32]{2,1,0:T(1,128)}), s32[128,1,32]{2,1,0:T(1,128)S(1)}, u32[]{:S(2)}, u32[]{:S(2)}) async-start(s32[128,1,32]{2,1,0:T(1,128)} %bitcast.29), calls=%async_computation | async-start | bytes 131072 | tf_op jit(solution)/shard_map/all_to_all | solution.py:431
  28.1 22.6 %all-to-all-start.1 = ((bf16[128,8,512]{2,1,0:T(8,128)(2,1)}), bf16[128,8,512]{2,1,0:T(8,128)(2,1)S(1)}, u32[]{:S(2)}, u32[]{:S(2)}) async-start(bf16[128,8,512]{2,1,0:T(8,128)(2,1)} %bitcast.12), calls=%async_computation.1 | async-start | bytes 2097152 | tf_op jit(solution)/shard_map/all_to_all | solution.py:433
  33.1 17.6 %copy-start.3 = (f32[128,128]{1,0:T(8,128)S(1)}, f32[128,128]{1,0:T(8,128)}, u32[]{:S(2)}) copy-start(f32[128,128]{1,0:T(8,128)} %get-tuple-element.33.cols) | copy-start | bytes 196612
  33.1 17.6 %copy-start.4 = (f32[2048]{0:T(1024)S(1)}, f32[2048]{0:T(1024)}, u32[]{:S(2)}) copy-start(f32[2048]{0:T(1024)} %param.16) | copy-start | bytes 24580
  33.1 17.6 %copy-start.5 = (f32[2048]{0:T(1024)S(1)}, f32[2048]{0:T(1024)}, u32[]{:S(2)}) copy-start(f32[2048]{0:T(1024)} %param.17) | copy-start | bytes 24580
  33.4 23.9 %copy-start.2 = (bf16[4,128,1024]{2,1,0:T(8,128)(2,1)}, bf16[4,128,1024]{2,1,0:T(8,128)(2,1)S(1)}, u32[]{:S(2)}) copy-start(bf16[4,128,1024]{2,1,0:T(8,128)(2,1)S(1)} %shard_map.106.early.near) | copy-start | bytes 3145732
  50.7 3.4 %copy-start = (bf16[2048,2048]{1,0:T(8,128)(2,1)S(1)}, bf16[2048,2048]{1,0:T(8,128)(2,1)}, u32[]{:S(2)}) copy-start(bf16[2048,2048]{1,0:T(8,128)(2,1)} %w.3) | copy-start | bytes 25165828
  57.3 8.3 %copy-start.8 = (s32[4,128]{1,0:T(4,128)S(1)}, s32[4,128]{1,0:T(4,128)}, u32[]{:S(2)}) copy-start(s32[4,128]{1,0:T(4,128)} %get-tuple-element.45.tgt_r) | copy-start | bytes 6148
  57.3 3.5 %collective-permute-start = (bf16[4,3,128,512]{3,2,1,0:T(8,128)(2,1)S(1)}, bf16[4,3,128,512]{3,2,1,0:T(8,128)(2,1)S(1)}, u32[]{:S(2)}, u32[]{:S(2)}) collective-permute-start(bf16[4,3,128,512]{3,2,1,0:T(8,128)(2,1)S(1)} %get-tuple-element.35), channel_id=1, source_target_pairs={{0,64},{64,0},{1,65},{65,1},{2,66},{66,2},{3,67},{67,3},{4,68},{68... | collective-permute-start | bytes 4718600 | tf_op jit(solution)/shard_map/ppermute | solution.py:441
  61.0 13.3 %collective-permute-start.1 = (bf16[2,3,128,512]{3,2,1,0:T(8,128)(2,1)S(1)}, bf16[2,3,128,512]{3,2,1,0:T(8,128)(2,1)S(1)}, u32[]{:S(2)}, u32[]{:S(2)}) collective-permute-start(bf16[2,3,128,512]{3,2,1,0:T(8,128)(2,1)S(1)} %get-tuple-element.37), channel_id=1, source_target_pairs={{0,16},{1,17},{2,18},{3,19},{4,20},{5,21},{6,22},{7,23},{8,24},{9,... | collective-permute-start | bytes 2359304 | tf_op jit(solution)/shard_map/ppermute | solution.py:331
  61.2 21.6 %collective-permute-start.2 = (bf16[2,3,128,512]{3,2,1,0:T(8,128)(2,1)S(1)}, bf16[2,3,128,512]{3,2,1,0:T(8,128)(2,1)S(1)}, u32[]{:S(2)}, u32[]{:S(2)}) collective-permute-start(bf16[2,3,128,512]{3,2,1,0:T(8,128)(2,1)S(1)} %get-tuple-element.38), channel_id=1, source_target_pairs={{0,32},{1,33},{2,34},{3,35},{4,36},{5,37},{6,38},{7,39},{8,40},{9,... | collective-permute-start | bytes 2359304 | tf_op jit(solution)/shard_map/ppermute | solution.py:331
  64.4 19.2 %collective-permute-start.3 = (bf16[2,3,128,512]{3,2,1,0:T(8,128)(2,1)S(1)}, bf16[2,3,128,512]{3,2,1,0:T(8,128)(2,1)S(1)}, u32[]{:S(2)}, u32[]{:S(2)}) collective-permute-start(bf16[2,3,128,512]{3,2,1,0:T(8,128)(2,1)S(1)} %get-tuple-element.39), channel_id=1, source_target_pairs={{0,48},{1,49},{2,50},{3,51},{4,52},{5,53},{6,54},{7,55},{8,56},{9,... | collective-permute-start | bytes 2359304 | tf_op jit(solution)/shard_map/ppermute | solution.py:331
  65.5 3.4 %copy-start.1 = (bf16[2048,2048]{1,0:T(8,128)(2,1)S(1)}, bf16[2048,2048]{1,0:T(8,128)(2,1)}, u32[]{:S(2)}) copy-start(bf16[2048,2048]{1,0:T(8,128)(2,1)} %w.3) | copy-start | bytes 25165828
  85.5 0.8 copy-start.6
  86.3 6.7 %copy-start.7 = (f32[128,1024]{1,0:T(8,128)S(1)}, f32[128,1024]{1,0:T(8,128)}, u32[]{:S(2)}) copy-start(f32[128,1024]{1,0:T(8,128)} %copy-done.6) | copy-start | bytes 1572868
  86.3 38.4 %all-to-all-start.2 = ((bf16[128,8,512]{2,1,0:T(8,128)(2,1)}), bf16[128,8,512]{2,1,0:T(8,128)(2,1)S(1)}, u32[]{:S(2)}, u32[]{:S(2)}) async-start(bf16[128,8,512]{2,1,0:T(8,128)(2,1)} %bitcast.18), calls=%async_computation.2 | async-start | bytes 2097152 | tf_op jit(solution)/shard_map/all_to_all | solution.py:445
  93.0 19.3 %collective-permute-start.4 = (f32[128,1024]{1,0:T(8,128)S(1)}, f32[128,1024]{1,0:T(8,128)S(1)}, u32[]{:S(2)}, u32[]{:S(2)}) collective-permute-start(f32[128,1024]{1,0:T(8,128)S(1)} %copy-done.7), channel_id=1, source_target_pairs={{0,4},{1,5},{2,6},{3,7},{4,8},{5,9},{6,10},{7,11},{8,12},{9,13},{1... | collective-permute-start | bytes 1572872 | tf_op jit(solution)/shard_map/ppermute | solution.py:331
  94.1 24.2 %collective-permute-start.5 = (f32[128,1024]{1,0:T(8,128)S(1)}, f32[128,1024]{1,0:T(8,128)S(1)}, u32[]{:S(2)}, u32[]{:S(2)}) collective-permute-start(f32[128,1024]{1,0:T(8,128)S(1)} %get-tuple-element.48), channel_id=1, source_target_pairs={{0,8},{1,9},{2,10},{3,11},{4,12},{5,13},{6,14},{7,15},{8,0},{9,1},... | collective-permute-start | bytes 1572872 | tf_op jit(solution)/shard_map/ppermute | solution.py:331
  96.7 21.6 %collective-permute-start.6 = (f32[128,1024]{1,0:T(8,128)S(1)}, f32[128,1024]{1,0:T(8,128)S(1)}, u32[]{:S(2)}, u32[]{:S(2)}) collective-permute-start(f32[128,1024]{1,0:T(8,128)S(1)} %get-tuple-element.49), channel_id=1, source_target_pairs={{0,12},{1,13},{2,14},{3,15},{4,0},{5,1},{6,2},{7,3},{8,4},{9,5},{1... | collective-permute-start | bytes 1572872 | tf_op jit(solution)/shard_map/ppermute | solution.py:331
  119.0 14.5 %collective-permute-start.7 = (f32[32,1024]{1,0:T(8,128)S(1)}, f32[32,1024]{1,0:T(8,128)S(1)}, u32[]{:S(2)}, u32[]{:S(2)}) collective-permute-start(f32[32,1024]{1,0:T(8,128)S(1)} %get-tuple-element.51), channel_id=1, source_target_pairs={{0,1},{1,2},{2,3},{3,0},{4,5},{5,6},{6,7},{7,4},{8,9},{9,10},{10,1... | collective-permute-start | bytes 393224 | tf_op jit(solution)/shard_map/ppermute | solution.py:331
  120.6 13.0 %collective-permute-start.8 = (f32[32,1024]{1,0:T(8,128)S(1)}, f32[32,1024]{1,0:T(8,128)S(1)}, u32[]{:S(2)}, u32[]{:S(2)}) collective-permute-start(f32[32,1024]{1,0:T(8,128)S(1)} %get-tuple-element.52), channel_id=1, source_target_pairs={{0,2},{1,3},{2,0},{3,1},{4,6},{5,7},{6,4},{7,5},{8,10},{9,11},{10,... | collective-permute-start | bytes 393224 | tf_op jit(solution)/shard_map/ppermute | solution.py:331
  123.3 10.2 %collective-permute-start.9 = (f32[32,1024]{1,0:T(8,128)S(1)}, f32[32,1024]{1,0:T(8,128)S(1)}, u32[]{:S(2)}, u32[]{:S(2)}) collective-permute-start(f32[32,1024]{1,0:T(8,128)S(1)} %get-tuple-element.53), channel_id=1, source_target_pairs={{0,3},{1,0},{2,1},{3,2},{4,7},{5,4},{6,5},{7,6},{8,11},{9,8},{10,9... | collective-permute-start | bytes 393224 | tf_op jit(solution)/shard_map/ppermute | solution.py:331
  124.7 1.0 copy-start.9
  134.2 4.3 %collective-permute-start.10 = (f32[16,1024]{1,0:T(8,128)S(1)}, f32[16,1024]{1,0:T(8,128)S(1)}, u32[]{:S(2)}, u32[]{:S(2)}) collective-permute-start(f32[16,1024]{1,0:T(8,128)S(1)} %get-tuple-element.61), channel_id=1, source_target_pairs={{0,16},{1,17},{2,18},{3,19},{4,20},{5,21},{6,22},{7,23},{8,24},{9,... | collective-permute-start | bytes 196616 | tf_op jit(solution)/shard_map/ppermute | solution.py:331

commit v5 on v4

--- a/solution.py
+++ b/solution.py
@@ -234,7 +234,7 @@
         out_specs=VMEM,
         out_shape=struct((total, wide), BF),
         compiler_params=params(24),
-        cost_estimate=cost(8 * samples * w.size, 10 << 20),
+        cost_estimate=cost(28 * samples * w.size, 10 << 20),
     )(dpre, tgt_r, w)
 
 
@@ -269,7 +269,7 @@
         out_shape=[struct((wide // 4, 2 * wide), F32)] * 4,
         scratch_shapes=[pltpu.VMEM((wide, 2 * wide), F32)],
         compiler_params=params(24),
-        cost_estimate=cost(32 * wide * samples * wide, 8 << 20),
+        cost_estimate=cost(4 * 10**10, 8 << 20),
     )(at, *packs)
 
 
@@ -441,16 +441,15 @@
     got = lax.ppermute(give, "role", [(0, 1), (1, 0)])
     sending = backward(dpre, tgt_r, w_hidden, devices * cap)
     packs = around(merge(own, got), (1, 2))
-    *parts, sending = lax.optimization_barrier((*weight_part(at, packs), sending))
     received = lax.all_to_all(
         sending.reshape(devices, cap, width), AXES, split_axis=0, concat_axis=0, tiled=True
     )
     new_table = update(
         near, received.reshape(devices * cap, width), emb_table, row_accum.reshape(-1, 128)
     )
-    parts = around(parts, (2, 3))
+    parts = around(weight_part(at, packs), (2, 3))
+    *parts, new_table = lax.optimization_barrier((*parts, new_table))
     parts = around(middle(at, parts), (3, 1))
-    *parts, new_table = lax.optimization_barrier((*parts, new_table))
     mine, give = last(at, parts)
     got = along(give, (1, 2), lambda i: i ^ 1)
     even = at[1] % 2 == 0

time: 140 us -> 127 us (0.907)
  waiting for transfers between devices: 59.3 us -> 50 us
  starting transfers between devices: 39.8 us -> 35.6 us
  Pallas kernels: 27.2 us -> 29.9 us
  local copies, waits for them, and re-layouts: 9.01 us -> 7.24 us
    ppermute x10, waiting for transfers between devices: 32.1 us -> 20.6 us  [along(): return lax.ppermute(value, AXES, pairs)]
    ppermute x10, starting transfers between devices: 17.2 us -> 13.5 us  [along(): return lax.ppermute(value, AXES, pairs)]
    all_to_all x1, waiting for transfers between devices: 0.01 us -> 1.84 us  [per_device(): lax.all_to_all(sending.reshape(devices, cap, width), AXES, split_axis=0,...]
    unnamed x20 -> x14, local copies, waits for them, and re-layouts: 8.55 us -> 6.78 us
    pallas_call x1, Pallas kernels: 1.96 us -> 3.6 us  [weight_part(): pl.pallas_call(weight_kernel, in_specs=[SMEM] + [VMEM] * 4, out_specs=[VM...]
  transfers between devices with their start and end apart: 14 -> 14, of which waited for: 9 -> 12; matrix products, arithmetic and copies ran while one was open for 2% -> 2% of each run, Pallas kernels for 10% -> 13%
where the time goes in v5:
time: 127 us
  waiting for transfers between devices  50 us (39%)
  starting transfers between devices  35.6 us (28%)
  Pallas kernels  29.9 us (24%)
  local copies, waits for them, and re-layouts  7.24 us (6%)
  other arithmetic  3.14 us (2%)
    ppermute x10, waiting for transfers between devices, along(): return lax.ppermute(value, AXES, pairs)  20.6 us
    all_to_all x1, waiting for transfers between devices, per_device(): lax.all_to_all(found.reshape(devices, cap, width), AXES, split_axis=0, co...  17.7 us
    ppermute x10, starting transfers between devices, along(): return lax.ppermute(value, AXES, pairs)  13.5 us
    all_to_all x1, starting transfers between devices, per_device(): lax.all_to_all(outgoing, AXES, split_axis=0, concat_axis=0, tiled=True)  11.1 us
    pallas_call x1, Pallas kernels, update(): pl.pallas_call(update_kernel, grid=(rows // block,), in_specs=[pl.BlockSp...  7.86 us
    unnamed x14, local copies, waits for them, and re-layouts  6.78 us
    all_to_all x1, waiting for transfers between devices, per_device(): lax.all_to_all(outgoing, AXES, split_axis=0, concat_axis=0, tiled=True)  6.48 us
    all_to_all x1, starting transfers between devices, per_device(): lax.all_to_all(sending.reshape(devices, cap, width), AXES, split_axis=0,...  6.3 us
  transfers between devices with their start and end apart: 14, of which 12 were waited for; matrix products, arithmetic and copies ran while one was open for 2% of the time, Pallas kernels for 13%

profile of v5, /device:TPU:0, one launch (start us, length us, event | category | flops | bytes accessed | tf_op | source)
XLA Modules:
  0.0 126.7 jit_solution(16448608485061774386)
XLA Ops:
  0.6 1.9 %shard_map.104 = (s32[128,32]{1,0:T(8,128)}, f32[128,128]{1,0:T(8,128)}, s32[4,128]{1,0:T(4,128)}) custom-call(s32[4,1,128]{2,1,0:T(1,128)} %bitcast.30, s32[4,4,128]{2,1,0:T(4,128)} %bitcast.29, s32[4,128]{1,0:T(4,128)} %bitcast.31, s32[1,128]{1,0:T(1,128)} %bitcast.32), custom_call_target="tpu_custom_call" | custom-call | tf_op jit(solution)/shard_map/pallas_call | solution.py:92
  2.5 11.1 %all-to-all-start = ((s32[128,1,32]{2,1,0:T(1,128)}), s32[128,1,32]{2,1,0:T(1,128)S(1)}, u32[]{:S(2)}, u32[]{:S(2)}) async-start(s32[128,1,32]{2,1,0:T(1,128)} %bitcast.28), calls=%async_computation | async-start | bytes 131072 | tf_op jit(solution)/shard_map/all_to_all | solution.py:431
  13.7 2.5 %convert_element_type.3.table = bf16[2048,512]{1,0:T(8,128)(2,1)S(1)} convert(f32[2048,512]{1,0:T(8,128)} %table.1) | non-fusion elementwise | flops 1048576 | bytes 6291456 | tf_op jit(solution)/shard_map/convert_element_type | solution.py:430
  16.2 6.5 %all-to-all-done = s32[128,1,32]{2,1,0:T(1,128)S(1)} async-done(((s32[128,1,32]{2,1,0:T(1,128)}), s32[128,1,32]{2,1,0:T(1,128)S(1)}, u32[]{:S(2)}, u32[]{:S(2)}) %all-to-all-start) | async-done | bytes 16416 | tf_op jit(solution)/shard_map/all_to_all | solution.py:431
  23.1 5.3 %shard_map.105 = bf16[1024,512]{1,0:T(8,128)(2,1)} custom-call(s32[128,32]{1,0:T(8,128)S(1)} %bitcast.24, bf16[2048,512]{1,0:T(8,128)(2,1)S(1)} %convert_element_type.3.table), custom_call_target="tpu_custom_call" | custom-call | flops 2147483648 | bytes 4194304 | tf_op jit(solution)/shard_map/pallas_call | solution.py:143
  28.4 4.6 %all-to-all-start.1 = ((bf16[128,8,512]{2,1,0:T(8,128)(2,1)}), bf16[128,8,512]{2,1,0:T(8,128)(2,1)S(1)}, u32[]{:S(2)}, u32[]{:S(2)}) async-start(bf16[128,8,512]{2,1,0:T(8,128)(2,1)} %bitcast.12), calls=%async_computation.1 | async-start | bytes 2097152 | tf_op jit(solution)/shard_map/all_to_all | solution.py:433
  33.3 17.7 %all-to-all-done.1 = bf16[128,8,512]{2,1,0:T(8,128)(2,1)S(1)} async-done(((bf16[128,8,512]{2,1,0:T(8,128)(2,1)}), bf16[128,8,512]{2,1,0:T(8,128)(2,1)S(1)}, u32[]{:S(2)}, u32[]{:S(2)}) %all-to-all-start.1) | async-done | bytes 1048608 | tf_op jit(solution)/shard_map/all_to_all | solution.py:433
  51.0 3.4 %copy-done = bf16[2048,2048]{1,0:T(8,128)(2,1)S(1)} copy-done((bf16[2048,2048]{1,0:T(8,128)(2,1)S(1)}, bf16[2048,2048]{1,0:T(8,128)(2,1)}, u32[]{:S(2)}) %copy-start) | copy-done | bytes 8388632
  54.4 3.1 %shard_map.107 = (bf16[4,3,128,512]{3,2,1,0:T(8,128)(2,1)S(1)}, bf16[4,3,128,512]{3,2,1,0:T(8,128)(2,1)S(1)}, bf16[128,2048]{1,0:T(8,128)(2,1)S(1)}) custom-call(s32[5]{0:T(128)S(1)} %stack.23.at, bf16[1024,512]{1,0:T(8,128)(2,1)S(1)} %bitcast.23, f32[128,128]{1,0:T(8,128)S(1)} %copy-done.3, f32[1,2048]{1,0:T(1,128)S(1)} %bitcast.25, ...), custom_call_target="tpu_custom_call" | custom-call | flops 1073741824 | bytes 10485760 | tf_op jit(solution)/shard_map/pallas_call | solution.py:187
  57.7 3.4 %collective-permute-done.got = bf16[4,3,128,512]{3,2,1,0:T(8,128)(2,1)S(1)} collective-permute-done((bf16[4,3,128,512]{3,2,1,0:T(8,128)(2,1)S(1)}, bf16[4,3,128,512]{3,2,1,0:T(8,128)(2,1)S(1)}, u32[]{:S(2)}, u32[]{:S(2)}) %collective-permute-start) | collective-permute-done | bytes 1572896 | tf_op jit(solution)/shard_map/ppermute | solution.py:441
  62.6 3.2 %collective-permute-start.2 = (bf16[2,3,128,512]{3,2,1,0:T(8,128)(2,1)}, bf16[2,3,128,512]{3,2,1,0:T(8,128)(2,1)}, u32[]{:S(2)}, u32[]{:S(2)}) collective-permute-start(bf16[2,3,128,512]{3,2,1,0:T(8,128)(2,1)} %get-tuple-element.33), channel_id=1, source_target_pairs={{0,32},{1,33},{2,34},{3,35},{4,36},{5,37},{6,38},{7,39},{8,40},{9,... | collective-permute-start | bytes 2359304 | tf_op jit(solution)/shard_map/ppermute | solution.py:331
  66.9 3.4 %copy-done.1 = bf16[2048,2048]{1,0:T(8,128)(2,1)S(1)} copy-done((bf16[2048,2048]{1,0:T(8,128)(2,1)S(1)}, bf16[2048,2048]{1,0:T(8,128)(2,1)}, u32[]{:S(2)}) %copy-start.1) | copy-done | bytes 8388632
  70.3 5.2 %shard_map.110 = bf16[1024,512]{1,0:T(8,128)(2,1)} custom-call(bf16[128,2048]{1,0:T(8,128)(2,1)S(1)} %get-tuple-element.39.dpre, s32[4,128]{1,0:T(4,128)S(1)} %copy-done.6, bf16[2048,2048]{1,0:T(8,128)(2,1)S(1)} %copy-done.1), custom_call_target="tpu_custom_call" | custom-call | flops 15032385536 | bytes 10485760 | tf_op jit(solution)/shard_map/pallas_call | solution.py:231
  75.5 6.3 %all-to-all-start.2 = ((bf16[128,8,512]{2,1,0:T(8,128)(2,1)}), bf16[128,8,512]{2,1,0:T(8,128)(2,1)}, u32[]{:S(2)}, u32[]{:S(2)}) async-start(bf16[128,8,512]{2,1,0:T(8,128)(2,1)} %bitcast.18), calls=%async_computation.2 | async-start | bytes 2097152 | tf_op jit(solution)/shard_map/all_to_all | solution.py:444
  81.8 2.6 %collective-permute-done.2.refs_2_ = bf16[2,3,128,512]{3,2,1,0:T(8,128)(2,1)} collective-permute-done((bf16[2,3,128,512]{3,2,1,0:T(8,128)(2,1)}, bf16[2,3,128,512]{3,2,1,0:T(8,128)(2,1)}, u32[]{:S(2)}, u32[]{:S(2)}) %collective-permute-start.2) | collective-permute-done | bytes 786464 | tf_op jit(solution)/shard_map/ppermute | solution.py:331
  84.5 6.3 %collective-permute-done.3.refs_3_ = bf16[2,3,128,512]{3,2,1,0:T(8,128)(2,1)} collective-permute-done((bf16[2,3,128,512]{3,2,1,0:T(8,128)(2,1)S(1)}, bf16[2,3,128,512]{3,2,1,0:T(8,128)(2,1)}, u32[]{:S(2)}, u32[]{:S(2)}) %collective-permute-start.3) | collective-permute-done | bytes 786464 | tf_op jit(solution)/shard_map/ppermute | solution.py:331
  90.7 3.6 %shard_map.109 = (f32[128,1024]{1,0:T(8,128)S(1)}, f32[128,1024]{1,0:T(8,128)}, f32[128,1024]{1,0:T(8,128)S(1)}, f32[128,1024]{1,0:T(8,128)S(1)}) custom-call(s32[5]{0:T(128)S(1)} %stack.23.at, bf16[2,3,128,512]{3,2,1,0:T(8,128)(2,1)S(1)} %get-tuple-element.31.refs_0_, bf16[2,3,128,512]{3,2,1,0:T(8,128)(2,1)S(1)} %collective-permute-done.1.refs_1_, ...), custom_call_target="tpu_custom_call" | custom-call | flops 40000000000 | bytes 8388608 | tf_op jit(solution)/shard_map/pallas_call | solution.py:265
  94.4 3.2 %collective-permute-start.6 = (f32[128,1024]{1,0:T(8,128)S(1)}, f32[128,1024]{1,0:T(8,128)S(1)}, u32[]{:S(2)}, u32[]{:S(2)}) collective-permute-start(f32[128,1024]{1,0:T(8,128)S(1)} %get-tuple-element.38), channel_id=1, source_target_pairs={{0,12},{1,13},{2,14},{3,15},{4,0},{5,1},{6,2},{7,3},{8,4},{9,5},{1... | collective-permute-start | bytes 1572872 | tf_op jit(solution)/shard_map/ppermute | solution.py:331
  97.6 1.8 %all-to-all-done.2 = bf16[128,8,512]{2,1,0:T(8,128)(2,1)} async-done(((bf16[128,8,512]{2,1,0:T(8,128)(2,1)}), bf16[128,8,512]{2,1,0:T(8,128)(2,1)}, u32[]{:S(2)}, u32[]{:S(2)}) %all-to-all-start.2) | async-done | bytes 1048608 | tf_op jit(solution)/shard_map/all_to_all | solution.py:444
  99.4 7.9 %shard_map.111 = f32[2048,512]{1,0:T(8,128)} custom-call(bf16[4,128,1024]{2,1,0:T(8,128)(2,1)} %copy-done.2, bf16[1024,512]{1,0:T(8,128)(2,1)} %bitcast.19.grads, f32[2048,512]{1,0:T(8,128)} %table.1, f32[16,128]{1,0:T(8,128)} %bitcast.33), custom_call_target="tpu_custom_call" | custom-call | flops 4294967296 | bytes 9437184 | tf_op jit(solution)/shard_map/pallas_call | solution.py:388
  107.3 3.3 %collective-permute-done.4.refs_1_ = f32[128,1024]{1,0:T(8,128)S(1)} collective-permute-done((f32[128,1024]{1,0:T(8,128)}, f32[128,1024]{1,0:T(8,128)S(1)}, u32[]{:S(2)}, u32[]{:S(2)}) %collective-permute-start.4) | collective-permute-done | bytes 524320 | tf_op jit(solution)/shard_map/ppermute | solution.py:331
  113.0 3.1 %collective-permute-start.8 = (f32[32,1024]{1,0:T(8,128)S(1)}, f32[32,1024]{1,0:T(8,128)S(1)}, u32[]{:S(2)}, u32[]{:S(2)}) collective-permute-start(f32[32,1024]{1,0:T(8,128)S(1)} %get-tuple-element.48), channel_id=1, source_target_pairs={{0,2},{1,3},{2,0},{3,1},{4,6},{5,7},{6,4},{7,5},{8,10},{9,11},{10,... | collective-permute-start | bytes 393224 | tf_op jit(solution)/shard_map/ppermute | solution.py:331
  118.2 2.3 %collective-permute-done.8.refs_2_ = f32[32,1024]{1,0:T(8,128)S(1)} collective-permute-done((f32[32,1024]{1,0:T(8,128)S(1)}, f32[32,1024]{1,0:T(8,128)S(1)}, u32[]{:S(2)}, u32[]{:S(2)}) %collective-permute-start.8) | collective-permute-done | bytes 131104 | tf_op jit(solution)/shard_map/ppermute | solution.py:331
  121.8 4.2 %collective-permute-done.10 = f32[16,1024]{1,0:T(8,128)S(1)} collective-permute-done((f32[16,1024]{1,0:T(8,128)S(1)}, f32[16,1024]{1,0:T(8,128)S(1)}, u32[]{:S(2)}, u32[]{:S(2)}) %collective-permute-start.10) | collective-permute-done | bytes 65568 | tf_op jit(solution)/shard_map/ppermute | solution.py:331
  (35 shorter events, 10.0 us)
Async XLA Ops:
  2.5 20.2 %all-to-all-start = ((s32[128,1,32]{2,1,0:T(1,128)}), s32[128,1,32]{2,1,0:T(1,128)S(1)}, u32[]{:S(2)}, u32[]{:S(2)}) async-start(s32[128,1,32]{2,1,0:T(1,128)} %bitcast.28), calls=%async_computation | async-start | bytes 131072 | tf_op jit(solution)/shard_map/all_to_all | solution.py:431
  28.4 22.6 %all-to-all-start.1 = ((bf16[128,8,512]{2,1,0:T(8,128)(2,1)}), bf16[128,8,512]{2,1,0:T(8,128)(2,1)S(1)}, u32[]{:S(2)}, u32[]{:S(2)}) async-start(bf16[128,8,512]{2,1,0:T(8,128)(2,1)} %bitcast.12), calls=%async_computation.1 | async-start | bytes 2097152 | tf_op jit(solution)/shard_map/all_to_all | solution.py:433
  33.0 18.0 %copy-start.3 = (f32[128,128]{1,0:T(8,128)S(1)}, f32[128,128]{1,0:T(8,128)}, u32[]{:S(2)}) copy-start(f32[128,128]{1,0:T(8,128)} %get-tuple-element.28.cols) | copy-start | bytes 196612
  33.0 18.0 %copy-start.4 = (f32[2048]{0:T(1024)S(1)}, f32[2048]{0:T(1024)}, u32[]{:S(2)}) copy-start(f32[2048]{0:T(1024)} %param.16) | copy-start | bytes 24580
  33.0 18.0 %copy-start.5 = (f32[2048]{0:T(1024)S(1)}, f32[2048]{0:T(1024)}, u32[]{:S(2)}) copy-start(f32[2048]{0:T(1024)} %param.17) | copy-start | bytes 24580
  33.3 24.2 %copy-start.2 = (bf16[4,128,1024]{2,1,0:T(8,128)(2,1)}, bf16[4,128,1024]{2,1,0:T(8,128)(2,1)S(1)}, u32[]{:S(2)}) copy-start(bf16[4,128,1024]{2,1,0:T(8,128)(2,1)S(1)} %shard_map.106.early.near) | copy-start | bytes 3145732
  51.0 3.4 %copy-start = (bf16[2048,2048]{1,0:T(8,128)(2,1)S(1)}, bf16[2048,2048]{1,0:T(8,128)(2,1)}, u32[]{:S(2)}) copy-start(bf16[2048,2048]{1,0:T(8,128)(2,1)} %w.3) | copy-start | bytes 25165828
  57.6 9.4 %copy-start.6 = (s32[4,128]{1,0:T(4,128)S(1)}, s32[4,128]{1,0:T(4,128)}, u32[]{:S(2)}) copy-start(s32[4,128]{1,0:T(4,128)} %get-tuple-element.40.tgt_r) | copy-start | bytes 6148
  57.6 3.5 %collective-permute-start = (bf16[4,3,128,512]{3,2,1,0:T(8,128)(2,1)S(1)}, bf16[4,3,128,512]{3,2,1,0:T(8,128)(2,1)S(1)}, u32[]{:S(2)}, u32[]{:S(2)}) collective-permute-start(bf16[4,3,128,512]{3,2,1,0:T(8,128)(2,1)S(1)} %get-tuple-element.30), channel_id=1, source_target_pairs={{0,64},{64,0},{1,65},{65,1},{2,66},{66,2},{3,67},{67,3},{4,68},{68... | collective-permute-start | bytes 4718600 | tf_op jit(solution)/shard_map/ppermute | solution.py:441
  62.4 19.4 %collective-permute-start.1 = (bf16[2,3,128,512]{3,2,1,0:T(8,128)(2,1)}, bf16[2,3,128,512]{3,2,1,0:T(8,128)(2,1)S(1)}, u32[]{:S(2)}, u32[]{:S(2)}) collective-permute-start(bf16[2,3,128,512]{3,2,1,0:T(8,128)(2,1)} %get-tuple-element.32), channel_id=1, source_target_pairs={{0,16},{1,17},{2,18},{3,19},{4,20},{5,21},{6,22},{7,23},{8,24},{9,... | collective-permute-start | bytes 2359304 | tf_op jit(solution)/shard_map/ppermute | solution.py:331
  62.6 21.9 %collective-permute-start.2 = (bf16[2,3,128,512]{3,2,1,0:T(8,128)(2,1)}, bf16[2,3,128,512]{3,2,1,0:T(8,128)(2,1)}, u32[]{:S(2)}, u32[]{:S(2)}) collective-permute-start(bf16[2,3,128,512]{3,2,1,0:T(8,128)(2,1)} %get-tuple-element.33), channel_id=1, source_target_pairs={{0,32},{1,33},{2,34},{3,35},{4,36},{5,37},{6,38},{7,39},{8,40},{9,... | collective-permute-start | bytes 2359304 | tf_op jit(solution)/shard_map/ppermute | solution.py:331
  65.8 25.0 %collective-permute-start.3 = (bf16[2,3,128,512]{3,2,1,0:T(8,128)(2,1)S(1)}, bf16[2,3,128,512]{3,2,1,0:T(8,128)(2,1)}, u32[]{:S(2)}, u32[]{:S(2)}) collective-permute-start(bf16[2,3,128,512]{3,2,1,0:T(8,128)(2,1)S(1)} %get-tuple-element.34), channel_id=1, source_target_pairs={{0,48},{1,49},{2,50},{3,51},{4,52},{5,53},{6,54},{7,55},{8,56},{9,... | collective-permute-start | bytes 2359304 | tf_op jit(solution)/shard_map/ppermute | solution.py:331
  66.9 3.4 %copy-start.1 = (bf16[2048,2048]{1,0:T(8,128)(2,1)S(1)}, bf16[2048,2048]{1,0:T(8,128)(2,1)}, u32[]{:S(2)}) copy-start(bf16[2048,2048]{1,0:T(8,128)(2,1)} %w.3) | copy-start | bytes 25165828
  75.5 23.9 %all-to-all-start.2 = ((bf16[128,8,512]{2,1,0:T(8,128)(2,1)}), bf16[128,8,512]{2,1,0:T(8,128)(2,1)}, u32[]{:S(2)}, u32[]{:S(2)}) async-start(bf16[128,8,512]{2,1,0:T(8,128)(2,1)} %bitcast.18), calls=%async_computation.2 | async-start | bytes 2097152 | tf_op jit(solution)/shard_map/all_to_all | solution.py:444
  94.3 16.2 %collective-permute-start.4 = (f32[128,1024]{1,0:T(8,128)}, f32[128,1024]{1,0:T(8,128)S(1)}, u32[]{:S(2)}, u32[]{:S(2)}) collective-permute-start(f32[128,1024]{1,0:T(8,128)} %get-tuple-element.36), channel_id=1, source_target_pairs={{0,4},{1,5},{2,6},{3,7},{4,8},{5,9},{6,10},{7,11},{8,12},{9,13},{1... | collective-permute-start | bytes 1572872 | tf_op jit(solution)/shard_map/ppermute | solution.py:331
  94.3 16.2 %collective-permute-start.5 = (f32[128,1024]{1,0:T(8,128)S(1)}, f32[128,1024]{1,0:T(8,128)S(1)}, u32[]{:S(2)}, u32[]{:S(2)}) collective-permute-start(f32[128,1024]{1,0:T(8,128)S(1)} %get-tuple-element.37), channel_id=1, source_target_pairs={{0,8},{1,9},{2,10},{3,11},{4,12},{5,13},{6,14},{7,15},{8,0},{9,1},... | collective-permute-start | bytes 1572872 | tf_op jit(solution)/shard_map/ppermute | solution.py:331
  94.4 16.9 %collective-permute-start.6 = (f32[128,1024]{1,0:T(8,128)S(1)}, f32[128,1024]{1,0:T(8,128)S(1)}, u32[]{:S(2)}, u32[]{:S(2)}) collective-permute-start(f32[128,1024]{1,0:T(8,128)S(1)} %get-tuple-element.38), channel_id=1, source_target_pairs={{0,12},{1,13},{2,14},{3,15},{4,0},{5,1},{6,2},{7,3},{8,4},{9,5},{1... | collective-permute-start | bytes 1572872 | tf_op jit(solution)/shard_map/ppermute | solution.py:331
  112.0 6.2 %collective-permute-start.7 = (f32[32,1024]{1,0:T(8,128)S(1)}, f32[32,1024]{1,0:T(8,128)S(1)}, u32[]{:S(2)}, u32[]{:S(2)}) collective-permute-start(f32[32,1024]{1,0:T(8,128)S(1)} %get-tuple-element.47), channel_id=1, source_target_pairs={{0,1},{1,2},{2,3},{3,0},{4,5},{5,6},{6,7},{7,4},{8,9},{9,10},{10,1... | collective-permute-start | bytes 393224 | tf_op jit(solution)/shard_map/ppermute | solution.py:331
  113.0 7.4 %collective-permute-start.8 = (f32[32,1024]{1,0:T(8,128)S(1)}, f32[32,1024]{1,0:T(8,128)S(1)}, u32[]{:S(2)}, u32[]{:S(2)}) collective-permute-start(f32[32,1024]{1,0:T(8,128)S(1)} %get-tuple-element.48), channel_id=1, source_target_pairs={{0,2},{1,3},{2,0},{3,1},{4,6},{5,7},{6,4},{7,5},{8,10},{9,11},{10,... | collective-permute-start | bytes 393224 | tf_op jit(solution)/shard_map/ppermute | solution.py:331
  116.1 5.0 %collective-permute-start.9 = (f32[32,1024]{1,0:T(8,128)S(1)}, f32[32,1024]{1,0:T(8,128)S(1)}, u32[]{:S(2)}, u32[]{:S(2)}) collective-permute-start(f32[32,1024]{1,0:T(8,128)S(1)} %get-tuple-element.49), channel_id=1, source_target_pairs={{0,3},{1,0},{2,1},{3,2},{4,7},{5,4},{6,5},{7,6},{8,11},{9,8},{10,9... | collective-permute-start | bytes 393224 | tf_op jit(solution)/shard_map/ppermute | solution.py:331
  121.7 4.3 %collective-permute-start.10 = (f32[16,1024]{1,0:T(8,128)S(1)}, f32[16,1024]{1,0:T(8,128)S(1)}, u32[]{:S(2)}, u32[]{:S(2)}) collective-permute-start(f32[16,1024]{1,0:T(8,128)S(1)} %get-tuple-element.51), channel_id=1, source_target_pairs={{0,16},{1,17},{2,18},{3,19},{4,20},{5,21},{6,22},{7,23},{8,24},{9,... | collective-permute-start | bytes 196616 | tf_op jit(solution)/shard_map/ppermute | solution.py:331

commit v6 on v5

--- a/solution.py
+++ b/solution.py
@@ -38,6 +38,7 @@
 SMEM = pl.BlockSpec(memory_space=pltpu.SMEM)
 VMEM = pl.BlockSpec(memory_space=pltpu.VMEM)
 HBM = pl.BlockSpec(memory_space=pltpu.HBM)
+ANY = pl.BlockSpec(memory_space=pl.ANY)
 
 
 def struct(shape, dtype):
@@ -103,7 +104,7 @@
     )(own, rows, lens, labels)
 
 
-def lookup_kernel(bag_len, block, ids, table, out):
+def lookup_kernel(bag_len, block, ids, table, out, counts):
     sources, width = ids.shape
     cap = width // bag_len
     slots = block * cap
@@ -125,15 +126,13 @@
         for j in range(bag_len):
             part = slice(j * 128, (j + 1) * 128)
             near.append(jnp.where(lo[:, part] == low, hi[:, part] - high, -1.0).astype(BF))
-        pieces = []
         for k in range(depth // 128):
             at = jnp.asarray(2.0 * k, BF)
             count = jnp.where(near[0] == at, one, zero)
             for j in range(1, bag_len):
                 count = count + jnp.where(near[j] == at, one, zero)
-            pieces.append(count)
-        total = dot(jnp.concatenate(pieces, axis=1), table[...])
-        out[i * slots : (i + 1) * slots, :] = total.astype(BF)
+            counts[i * slots : (i + 1) * slots, k * 128 : (k + 1) * 128] = count
+    out[...] = dot(counts[...], table[...]).astype(BF)
 
 
 def lookup(ids, table, bag_len):
@@ -145,15 +144,28 @@
         in_specs=[VMEM, VMEM],
         out_specs=VMEM,
         out_shape=struct((sources * cap, wide), BF),
+        scratch_shapes=[pltpu.VMEM((sources * cap, depth), BF)],
         compiler_params=params(24),
         cost_estimate=cost(2 * sources * cap * depth * wide, 4 << 20),
     )(ids, table)
 
 
-def forward_kernel(features, at, slots, cols, bias, head, w, early, *refs):
-    own, give, dpre_out, bags, blocks, quarters = refs
+def load(hbm, vmem, sems):
+    parts = sems.shape[0]
+    rows = vmem.shape[0] // parts
+    copies = []
+    for k in range(parts):
+        part = pl.ds(k * rows, rows)
+        copies.append(pltpu.make_async_copy(hbm.at[part], vmem.at[part], sems.at[k]))
+        copies[-1].start()
+    return copies
+
+
+def forward_kernel(features, at, slots, cols, bias, head, w_any, early, *refs):
+    own, give, dpre_out, bags, blocks, w, sems = refs
     total, wide = slots.shape
     samples, hidden = dpre_out.shape
+    copies = load(w_any, w, sems)
     lane = iota((samples, total), 1).astype(F32)
     for f in range(features):
         pick = (cols[:, f : f + 1] == lane).astype(F32).astype(BF)
@@ -165,20 +177,19 @@
             blocks[2 + k, :, z * 128 : (z + 1) * 128] = bags[2 + z // 2, :, start : start + 128]
     pre = bias[...]
     for f in range(features):
+        for copy in copies[4 * f : 4 * f + 4]:
+            copy.wait()
         pre = pre + dot(bags[f], w[f * wide : (f + 1) * wide, :])
     sig = jax.nn.sigmoid(pre)
     logit = jnp.sum(pre * sig * head[...], axis=1, keepdims=True)
     dlogit = jax.nn.sigmoid(logit) - cols[:, features : features + 1]
     dpre = (dlogit * head[...] * sig * (1.0 + pre * (1.0 - sig))).astype(BF)
     dpre_out[...] = dpre
-    for q in range(4):
-        quarters[q] = dpre[:, q * wide : (q + 1) * wide]
-    for packs, role, ring in ((own, at[0], at[1]), (give, 1 - at[0], at[2])):
-        for s in range(4):
-            to = (ring + s) % 4
-            packs[s, 0] = blocks[2 * role + to // 2]
-            packs[s, 1] = quarters[2 * (to % 2)]
-            packs[s, 2] = quarters[2 * (to % 2) + 1]
+    for out, role in ((own, at[0]), (give, 1 - at[0])):
+        for k in range(2):
+            out[k] = blocks[2 * role + k]
+        for q in range(4):
+            out[2 + q] = dpre[:, q * wide : (q + 1) * wide]
 
 
 def forward(at, slots, cols, bias, head, w, features, early):
@@ -186,31 +197,35 @@
     wide = slots.shape[1]
     return pl.pallas_call(
         functools.partial(forward_kernel, features),
-        in_specs=[SMEM] + [VMEM] * 5 + [HBM],
+        in_specs=[SMEM] + [VMEM] * 4 + [ANY, HBM],
         out_specs=[VMEM] * 3,
-        out_shape=[struct((4, 3, samples, wide), BF)] * 2 + [struct((samples, hidden), BF)],
-        scratch_shapes=[pltpu.VMEM((4, samples, wide), BF)] * 3,
-        compiler_params=params(20),
+        out_shape=[struct((6, samples, wide), BF)] * 2 + [struct((samples, hidden), BF)],
+        scratch_shapes=[pltpu.VMEM((4, samples, wide), BF)] * 2
+        + [pltpu.VMEM(w.shape, BF), pltpu.SemaphoreType.DMA((4 * features,))],
+        compiler_params=params(48),
         cost_estimate=cost(2 * samples * w.size, 10 << 20),
     )(at, slots, cols, bias, head, w, early)
 
 
-def merge_kernel(own, got, *outs):
-    for s, out in enumerate(outs):
-        out[0] = own[s]
-        out[1] = got[s]
-
-
-def merge(own, got):
-    ring, *rest = own.shape
+def merge_kernel(at, own, got, *packs):
+    for s, pack in enumerate(packs):
+        to = (at[1] + s) % 4
+        for k, source in enumerate((own, got)):
+            pack[k, 0] = source[to // 2]
+            for q in range(2):
+                pack[k, 1 + q] = source[2 + 2 * (to % 2) + q]
+
+
+def merge(at, own, got):
+    _, samples, wide = own.shape
     return pl.pallas_call(
         merge_kernel,
-        in_specs=[VMEM] * 2,
-        out_specs=[VMEM] * ring,
-        out_shape=[struct((2, *rest), BF)] * ring,
+        in_specs=[SMEM] + [VMEM] * 2,
+        out_specs=[VMEM] * 4,
+        out_shape=[struct((2, 3, samples, wide), BF)] * 4,
         compiler_params=params(16),
         cost_estimate=cost(1 << 20, 6 << 20),
-    )(own, got)
+    )(at, own, got)
 
 
 def backward_kernel(dpre, tgt_r, w, sending):
@@ -248,7 +263,7 @@
             left, right, (((0,), (0,)), ((), ())), preferred_element_type=F32
         )
     for s in range(4):
-        first = (at[3] + s) % 4
+        first = (at[2] + s) % 4
         for p in range(2):
             for q in range(4):
                 row = jnp.where(
@@ -273,47 +288,42 @@
     )(at, *packs)
 
 
-def middle_kernel(at, *refs):
-    parts, outs, acc = refs[:4], refs[4:8], refs[8]
-    acc[...] = (parts[0][...] + parts[1][...]) + (parts[2][...] + parts[3][...])
-    for s in range(4):
-        second = (at[4] + s) % 4
-        for p in range(2):
-            row = pl.multiple_of(p * 64 + second * 16, 16)
-            outs[s][p * 16 : (p + 1) * 16, :] = acc[pl.ds(row, 16), :]
-
-
-def middle(at, parts):
+def middle_kernel(*refs):
+    parts, out = refs[:4], refs[4]
+    acc = (parts[0][...] + parts[1][...]) + (parts[2][...] + parts[3][...])
+    for k in range(8):
+        out[k] = acc[k * 16 : (k + 1) * 16]
+
+
+def middle(parts):
     rows, wide = parts[0].shape
     return pl.pallas_call(
         middle_kernel,
-        in_specs=[SMEM] + [VMEM] * 4,
-        out_specs=[VMEM] * 4,
-        out_shape=[struct((rows // 4, wide), F32)] * 4,
-        scratch_shapes=[pltpu.VMEM((rows, wide), F32)],
+        in_specs=[VMEM] * 4,
+        out_specs=VMEM,
+        out_shape=struct((8, rows // 8, wide), F32),
         compiler_params=params(12),
         cost_estimate=cost(1 << 20, 3 << 20),
-    )(at, *parts)
-
-
-def last_kernel(at, *refs):
-    parts, keep, give = refs[:4], refs[4], refs[5]
-    acc = (parts[0][...] + parts[1][...]) + (parts[2][...] + parts[3][...])
-    even = at[1] % 2 == 0
-    keep[...] = jnp.where(even, acc[:16], acc[16:])
-    give[...] = jnp.where(even, acc[16:], acc[:16])
-
-
-def last(at, parts):
-    rows, wide = parts[0].shape
+    )(*parts)
+
+
+def last_kernel(parts, out):
+    wide = parts.shape[2]
+    for k in range(2):
+        acc = (parts[4 * k] + parts[4 * k + 1]) + (parts[4 * k + 2] + parts[4 * k + 3])
+        out[:, k * wide : (k + 1) * wide] = acc
+
+
+def last(parts):
+    _, rows, wide = parts.shape
     return pl.pallas_call(
         last_kernel,
-        in_specs=[SMEM] + [VMEM] * 4,
-        out_specs=[VMEM] * 2,
-        out_shape=[struct((rows // 2, wide), F32)] * 2,
+        in_specs=[VMEM],
+        out_specs=VMEM,
+        out_shape=struct((rows, 2 * wide), F32),
         compiler_params=params(12),
         cost_estimate=cost(1 << 16, 1 << 18),
-    )(at, *parts)
+    )(parts)
 
 
 def device(place):
@@ -335,6 +345,15 @@
     return [values[0]] + [
         along(value, axes, lambda i, s=s: (i + s) % 4) for s, value in enumerate(values) if s
     ]
+
+
+def eights():
+    groups = []
+    for half, fixed in itertools.product(range(2), range(4)):
+        both = [(2 * half + p, k) for p in range(2) for k in range(4)]
+        groups.append([device((0, n, fixed, k)) for n, k in both])
+        groups.append([device((1, k, n, fixed)) for n, k in both])
+    return groups
 
 
 def near_kernel(ids, near):
@@ -414,9 +433,7 @@
         [
             role,
             jnp.where(odd, x, z),
-            jnp.where(odd, z, x),
             jnp.where(odd, y, x),
-            jnp.where(odd, z, y),
         ]
     ).astype(I32)
     outgoing, cols, tgt_r = route(
@@ -440,7 +457,7 @@
     )
     got = lax.ppermute(give, "role", [(0, 1), (1, 0)])
     sending = backward(dpre, tgt_r, w_hidden, devices * cap)
-    packs = around(merge(own, got), (1, 2))
+    packs = around(merge(at, own, got), (1, 2))
     received = lax.all_to_all(
         sending.reshape(devices, cap, width), AXES, split_axis=0, concat_axis=0, tiled=True
     )
@@ -449,11 +466,10 @@
     )
     parts = around(weight_part(at, packs), (2, 3))
     *parts, new_table = lax.optimization_barrier((*parts, new_table))
-    parts = around(middle(at, parts), (3, 1))
-    mine, give = last(at, parts)
-    got = along(give, (1, 2), lambda i: i ^ 1)
-    even = at[1] % 2 == 0
-    w_grad = jnp.concatenate([jnp.where(even, mine, got), jnp.where(even, got, mine)], axis=1)
+    part = lax.all_to_all(
+        middle(parts), AXES, split_axis=0, concat_axis=0, tiled=True, axis_index_groups=eights()
+    )
+    w_grad = last(part)
     return (new_table, w_grad)
 
 

time: 127 us -> 124 us (0.976)
  blocking collectives: 0 us -> 12.8 us
  waiting for transfers between devices: 50 us -> 41.5 us
  starting transfers between devices: 35.6 us -> 29.9 us
  local copies, waits for them, and re-layouts: 7.24 us -> 3.77 us
  Pallas kernels: 29.9 us -> 31.9 us
    all_to_all x0 -> x1, blocking collectives: none -> 12.8 us  [per_device(): lax.all_to_all(middle(parts), AXES, split_axis=0, concat_axis=0, tiled=Tr...]
    ppermute x10 -> x6, waiting for transfers between devices: 20.6 us -> 13.3 us  [along(): return lax.ppermute(value, AXES, pairs)]
    ppermute x10 -> x6, starting transfers between devices: 13.5 us -> 7.74 us  [along(): return lax.ppermute(value, AXES, pairs)]
    unnamed x14 -> x12, local copies, waits for them, and re-layouts: 6.78 us -> 3.41 us
    pallas_call x1, Pallas kernels: 3.12 us -> 5.17 us  [forward(): pl.pallas_call(functools.partial(forward_kernel, features), in_specs=[SME...]
  transfers between devices with their start and end apart: 14 -> 10, of which waited for: 12 -> 8; matrix products, arithmetic and copies ran while one was open for 2% -> 2% of each run, Pallas kernels for 13% -> 14%
where the time goes in v6:
time: 124 us; the launch traced here: 123 us
  waiting for transfers between devices  41.5 us (33%)
  Pallas kernels  31.9 us (26%)
  starting transfers between devices  29.9 us (24%)
  blocking collectives  12.8 us (10%)
  local copies, waits for them, and re-layouts  3.77 us (3%)
  other arithmetic  2.53 us (2%)
    all_to_all x1, waiting for transfers between devices, per_device(): lax.all_to_all(found.reshape(devices, cap, width), AXES, split_axis=0, co...  17.7 us
    ppermute x6, waiting for transfers between devices, along(): return lax.ppermute(value, AXES, pairs)  13.3 us
    all_to_all x1, blocking collectives, per_device(): lax.all_to_all(middle(parts), AXES, split_axis=0, concat_axis=0, tiled=Tr...  12.8 us
    all_to_all x1, starting transfers between devices, per_device(): lax.all_to_all(outgoing, AXES, split_axis=0, concat_axis=0, tiled=True)  11.1 us
    pallas_call x1, Pallas kernels, update(): pl.pallas_call(update_kernel, grid=(rows // block,), in_specs=[pl.BlockSp...  7.86 us
    ppermute x6, starting transfers between devices, along(): return lax.ppermute(value, AXES, pairs)  7.74 us
    all_to_all x1, waiting for transfers between devices, per_device(): lax.all_to_all(outgoing, AXES, split_axis=0, concat_axis=0, tiled=True)  6.5 us
    all_to_all x1, starting transfers between devices, per_device(): lax.all_to_all(sending.reshape(devices, cap, width), AXES, split_axis=0,...  6.3 us
  transfers between devices with their start and end apart: 10, of which 8 were waited for; matrix products, arithmetic and copies ran while one was open for 2% of the time, Pallas kernels for 14%

profile of v6, /device:TPU:0, one launch (start us, length us, event | category | flops | bytes accessed | tf_op | source)
XLA Modules:
  0.0 123.2 jit_solution(3590138161810510922)
XLA Ops:
  0.6 1.9 %shard_map.104 = (s32[128,32]{1,0:T(8,128)}, f32[128,128]{1,0:T(8,128)}, s32[4,128]{1,0:T(4,128)}) custom-call(s32[4,1,128]{2,1,0:T(1,128)} %bitcast.28, s32[4,4,128]{2,1,0:T(4,128)} %bitcast.27, s32[4,128]{1,0:T(4,128)} %bitcast.29, s32[1,128]{1,0:T(1,128)} %bitcast.30), custom_call_target="tpu_custom_call" | custom-call | tf_op jit(solution)/shard_map/pallas_call | solution.py:93
  2.5 11.1 %all-to-all-start = ((s32[128,1,32]{2,1,0:T(1,128)}), s32[128,1,32]{2,1,0:T(1,128)S(1)}, u32[]{:S(2)}, u32[]{:S(2)}) async-start(s32[128,1,32]{2,1,0:T(1,128)} %bitcast.26), calls=%async_computation | async-start | bytes 131072 | tf_op jit(solution)/shard_map/all_to_all | solution.py:448
  13.7 2.5 %convert_element_type.3.table = bf16[2048,512]{1,0:T(8,128)(2,1)S(1)} convert(f32[2048,512]{1,0:T(8,128)} %table.1) | non-fusion elementwise | flops 1048576 | bytes 6291456 | tf_op jit(solution)/shard_map/convert_element_type | solution.py:447
  16.2 6.5 %all-to-all-done = s32[128,1,32]{2,1,0:T(1,128)S(1)} async-done(((s32[128,1,32]{2,1,0:T(1,128)}), s32[128,1,32]{2,1,0:T(1,128)S(1)}, u32[]{:S(2)}, u32[]{:S(2)}) %all-to-all-start) | async-done | bytes 16416 | tf_op jit(solution)/shard_map/all_to_all | solution.py:448
  23.1 5.1 %shard_map.105 = bf16[1024,512]{1,0:T(8,128)(2,1)} custom-call(s32[128,32]{1,0:T(8,128)S(1)} %bitcast.22, bf16[2048,512]{1,0:T(8,128)(2,1)S(1)} %convert_element_type.3.table), custom_call_target="tpu_custom_call" | custom-call | flops 2147483648 | bytes 4194304 | tf_op jit(solution)/shard_map/pallas_call | solution.py:142
  28.2 4.6 %all-to-all-start.1 = ((bf16[128,8,512]{2,1,0:T(8,128)(2,1)}), bf16[128,8,512]{2,1,0:T(8,128)(2,1)S(1)}, u32[]{:S(2)}, u32[]{:S(2)}) async-start(bf16[128,8,512]{2,1,0:T(8,128)(2,1)} %bitcast.10), calls=%async_computation.1 | async-start | bytes 2097152 | tf_op jit(solution)/shard_map/all_to_all | solution.py:450
  33.1 17.7 %all-to-all-done.1 = bf16[128,8,512]{2,1,0:T(8,128)(2,1)S(1)} async-done(((bf16[128,8,512]{2,1,0:T(8,128)(2,1)}), bf16[128,8,512]{2,1,0:T(8,128)(2,1)S(1)}, u32[]{:S(2)}, u32[]{:S(2)}) %all-to-all-start.1) | async-done | bytes 1048608 | tf_op jit(solution)/shard_map/all_to_all | solution.py:450
  50.8 5.2 %shard_map.107 = (bf16[6,128,512]{2,1,0:T(8,128)(2,1)S(1)}, bf16[6,128,512]{2,1,0:T(8,128)(2,1)S(1)}, bf16[128,2048]{1,0:T(8,128)(2,1)S(1)}) custom-call(s32[3]{0:T(128)S(1)} %pad_add_fusion.at, bf16[1024,512]{1,0:T(8,128)(2,1)S(1)} %bitcast.21, f32[128,128]{1,0:T(8,128)S(1)} %copy-done.2, f32[1,2048]{1,0:T(1,128)S(1)} %bitcast.23, f32[1,2048]{1,0:T(1,128)S(1)} %bitcast.24, ...), custom_call_target="tpu_custom_call" | custom-call | flops 1073741824 | bytes 10485760 | tf_op jit(solution)/shard_map/pallas_call | solution.py:198
  56.1 2.3 %collective-permute-done.got = bf16[6,128,512]{2,1,0:T(8,128)(2,1)S(1)} collective-permute-done((bf16[6,128,512]{2,1,0:T(8,128)(2,1)S(1)}, bf16[6,128,512]{2,1,0:T(8,128)(2,1)S(1)}, u32[]{:S(2)}, u32[]{:S(2)}) %collective-permute-start) | collective-permute-done | bytes 786464 | tf_op jit(solution)/shard_map/ppermute | solution.py:458
  58.4 2.1 %shard_map.108 = (bf16[2,3,128,512]{3,2,1,0:T(8,128)(2,1)S(1)}, bf16[2,3,128,512]{3,2,1,0:T(8,128)(2,1)}, bf16[2,3,128,512]{3,2,1,0:T(8,128)(2,1)}, bf16[2,3,128,512]{3,2,1,0:T(8,128)(2,1)}) custom-call(s32[3]{0:T(128)S(1)} %pad_add_fusion.at, bf16[6,128,512]{2,1,0:T(8,128)(2,1)S(1)} %get-tuple-element.23.own, bf16[6,128,512]{2,1,0:T(8,128)(2,1)S(1)} %collective-permute-done.got), custom_call_target="tpu_custom_call" | custom-call | flops 1048576 | bytes 6291456 | tf_op jit(solution)/shard_map/pallas_call | solution.py:221
  60.6 3.2 %collective-permute-start.2 = (bf16[2,3,128,512]{3,2,1,0:T(8,128)(2,1)}, bf16[2,3,128,512]{3,2,1,0:T(8,128)(2,1)S(1)}, u32[]{:S(2)}, u32[]{:S(2)}) collective-permute-start(bf16[2,3,128,512]{3,2,1,0:T(8,128)(2,1)} %get-tuple-element.27), channel_id=1, source_target_pairs={{0,32},{1,33},{2,34},{3,35},{4,36},{5,37},{6,38},{7,39},{8,40},{9,... | collective-permute-start | bytes 2359304 | tf_op jit(solution)/shard_map/ppermute | solution.py:341
  63.8 1.2 collective-permute-start.3
  65.0 3.4 %copy-done = bf16[2048,2048]{1,0:T(8,128)(2,1)S(1)} copy-done((bf16[2048,2048]{1,0:T(8,128)(2,1)S(1)}, bf16[2048,2048]{1,0:T(8,128)(2,1)}, u32[]{:S(2)}) %copy-start) | copy-done | bytes 8388632
  68.4 5.2 %shard_map.110 = bf16[1024,512]{1,0:T(8,128)(2,1)} custom-call(bf16[128,2048]{1,0:T(8,128)(2,1)S(1)} %get-tuple-element.33.dpre, s32[4,128]{1,0:T(4,128)S(1)} %copy-done.5, bf16[2048,2048]{1,0:T(8,128)(2,1)S(1)} %copy-done), custom_call_target="tpu_custom_call" | custom-call | flops 15032385536 | bytes 10485760 | tf_op jit(solution)/shard_map/pallas_call | solution.py:246
  73.6 6.3 %all-to-all-start.2 = ((bf16[128,8,512]{2,1,0:T(8,128)(2,1)}), bf16[128,8,512]{2,1,0:T(8,128)(2,1)}, u32[]{:S(2)}, u32[]{:S(2)}) async-start(bf16[128,8,512]{2,1,0:T(8,128)(2,1)} %bitcast.16), calls=%async_computation.2 | async-start | bytes 2097152 | tf_op jit(solution)/shard_map/all_to_all | solution.py:461
  79.9 2.5 %collective-permute-done.2.refs_2_ = bf16[2,3,128,512]{3,2,1,0:T(8,128)(2,1)S(1)} collective-permute-done((bf16[2,3,128,512]{3,2,1,0:T(8,128)(2,1)}, bf16[2,3,128,512]{3,2,1,0:T(8,128)(2,1)S(1)}, u32[]{:S(2)}, u32[]{:S(2)}) %collective-permute-start.2) | collective-permute-done | bytes 786464 | tf_op jit(solution)/shard_map/ppermute | solution.py:341
  82.4 6.5 %collective-permute-done.3.refs_3_ = bf16[2,3,128,512]{3,2,1,0:T(8,128)(2,1)} collective-permute-done((bf16[2,3,128,512]{3,2,1,0:T(8,128)(2,1)}, bf16[2,3,128,512]{3,2,1,0:T(8,128)(2,1)}, u32[]{:S(2)}, u32[]{:S(2)}) %collective-permute-start.3) | collective-permute-done | bytes 786464 | tf_op jit(solution)/shard_map/ppermute | solution.py:341
  88.9 3.5 %shard_map.109 = (f32[128,1024]{1,0:T(8,128)S(1)}, f32[128,1024]{1,0:T(8,128)}, f32[128,1024]{1,0:T(8,128)}, f32[128,1024]{1,0:T(8,128)S(1)}) custom-call(s32[3]{0:T(128)S(1)} %pad_add_fusion.at, bf16[2,3,128,512]{3,2,1,0:T(8,128)(2,1)S(1)} %get-tuple-element.25.refs_0_, bf16[2,3,128,512]{3,2,1,0:T(8,128)(2,1)S(1)} %collective-permute-done.1.refs_1_, ...), custom_call_target="tpu_custom_call" | custom-call | flops 40000000000 | bytes 8388608 | tf_op jit(solution)/shard_map/pallas_call | solution.py:280
  92.5 3.2 %collective-permute-start.6 = (f32[128,1024]{1,0:T(8,128)S(1)}, f32[128,1024]{1,0:T(8,128)S(1)}, u32[]{:S(2)}, u32[]{:S(2)}) collective-permute-start(f32[128,1024]{1,0:T(8,128)S(1)} %get-tuple-element.32), channel_id=1, source_target_pairs={{0,12},{1,13},{2,14},{3,15},{4,0},{5,1},{6,2},{7,3},{8,4},{9,5},{1... | collective-permute-start | bytes 1572872 | tf_op jit(solution)/shard_map/ppermute | solution.py:341
  95.7 1.8 %all-to-all-done.2 = bf16[128,8,512]{2,1,0:T(8,128)(2,1)} async-done(((bf16[128,8,512]{2,1,0:T(8,128)(2,1)}), bf16[128,8,512]{2,1,0:T(8,128)(2,1)}, u32[]{:S(2)}, u32[]{:S(2)}) %all-to-all-start.2) | async-done | bytes 1048608 | tf_op jit(solution)/shard_map/all_to_all | solution.py:461
  97.5 7.9 %shard_map.111 = f32[2048,512]{1,0:T(8,128)} custom-call(bf16[4,128,1024]{2,1,0:T(8,128)(2,1)} %copy-done.1, bf16[1024,512]{1,0:T(8,128)(2,1)} %bitcast.17.grads, f32[2048,512]{1,0:T(8,128)} %table.1, f32[16,128]{1,0:T(8,128)} %bitcast.31), custom_call_target="tpu_custom_call" | custom-call | flops 4294967296 | bytes 9437184 | tf_op jit(solution)/shard_map/pallas_call | solution.py:407
  105.3 3.3 %collective-permute-done.4.refs_1_ = f32[128,1024]{1,0:T(8,128)S(1)} collective-permute-done((f32[128,1024]{1,0:T(8,128)}, f32[128,1024]{1,0:T(8,128)S(1)}, u32[]{:S(2)}, u32[]{:S(2)}) %collective-permute-start.4) | collective-permute-done | bytes 524320 | tf_op jit(solution)/shard_map/ppermute | solution.py:341
  108.7 0.9 collective-permute-done.6.refs_3_
  109.7 12.8 %all_to_all.26.parts = f32[8,16,1024]{2,1,0:T(8,128)S(1)} all-to-all(f32[8,16,1024]{2,1,0:T(8,128)S(1)} %shard_map.112), channel_id=1, replica_groups={{0,1,2,3,16,17,18,19},{64,80,96,112,68,84,100,116},{4,5,6,7,20,21,22,23..., dimensions={0} | all-to-all | bytes 1048576 | tf_op jit(solution)/shard_map/all_to_all | solution.py:469
  (24 shorter events, 1.7 us)
Async XLA Ops:
  2.5 20.2 %all-to-all-start = ((s32[128,1,32]{2,1,0:T(1,128)}), s32[128,1,32]{2,1,0:T(1,128)S(1)}, u32[]{:S(2)}, u32[]{:S(2)}) async-start(s32[128,1,32]{2,1,0:T(1,128)} %bitcast.26), calls=%async_computation | async-start | bytes 131072 | tf_op jit(solution)/shard_map/all_to_all | solution.py:448
  28.2 22.6 %all-to-all-start.1 = ((bf16[128,8,512]{2,1,0:T(8,128)(2,1)}), bf16[128,8,512]{2,1,0:T(8,128)(2,1)S(1)}, u32[]{:S(2)}, u32[]{:S(2)}) async-start(bf16[128,8,512]{2,1,0:T(8,128)(2,1)} %bitcast.10), calls=%async_computation.1 | async-start | bytes 2097152 | tf_op jit(solution)/shard_map/all_to_all | solution.py:450
  32.8 18.0 %copy-start.2 = (f32[128,128]{1,0:T(8,128)S(1)}, f32[128,128]{1,0:T(8,128)}, u32[]{:S(2)}) copy-start(f32[128,128]{1,0:T(8,128)} %get-tuple-element.22.cols) | copy-start | bytes 196612
  32.8 18.0 %copy-start.3 = (f32[2048]{0:T(1024)S(1)}, f32[2048]{0:T(1024)}, u32[]{:S(2)}) copy-start(f32[2048]{0:T(1024)} %param.16) | copy-start | bytes 24580
  32.8 18.0 %copy-start.4 = (f32[2048]{0:T(1024)S(1)}, f32[2048]{0:T(1024)}, u32[]{:S(2)}) copy-start(f32[2048]{0:T(1024)} %param.17) | copy-start | bytes 24580
  33.1 22.9 %copy-start.1 = (bf16[4,128,1024]{2,1,0:T(8,128)(2,1)}, bf16[4,128,1024]{2,1,0:T(8,128)(2,1)S(1)}, u32[]{:S(2)}) copy-start(bf16[4,128,1024]{2,1,0:T(8,128)(2,1)S(1)} %shard_map.106.early.near) | copy-start | bytes 3145732
  50.8 14.2 %copy-start.5 = (s32[4,128]{1,0:T(4,128)S(1)}, s32[4,128]{1,0:T(4,128)}, u32[]{:S(2)}) copy-start(s32[4,128]{1,0:T(4,128)} %get-tuple-element.34.tgt_r) | copy-start | bytes 6148
  56.0 2.4 %collective-permute-start = (bf16[6,128,512]{2,1,0:T(8,128)(2,1)S(1)}, bf16[6,128,512]{2,1,0:T(8,128)(2,1)S(1)}, u32[]{:S(2)}, u32[]{:S(2)}) collective-permute-start(bf16[6,128,512]{2,1,0:T(8,128)(2,1)S(1)} %get-tuple-element.24), channel_id=1, source_target_pairs={{0,64},{64,0},{1,65},{65,1},{2,66},{66,2},{3,67},{67,3},{4,68},{68... | collective-permute-start | bytes 2359304 | tf_op jit(solution)/shard_map/ppermute | solution.py:458
  60.5 19.4 %collective-permute-start.1 = (bf16[2,3,128,512]{3,2,1,0:T(8,128)(2,1)}, bf16[2,3,128,512]{3,2,1,0:T(8,128)(2,1)S(1)}, u32[]{:S(2)}, u32[]{:S(2)}) collective-permute-start(bf16[2,3,128,512]{3,2,1,0:T(8,128)(2,1)} %get-tuple-element.26), channel_id=1, source_target_pairs={{0,16},{1,17},{2,18},{3,19},{4,20},{5,21},{6,22},{7,23},{8,24},{9,... | collective-permute-start | bytes 2359304 | tf_op jit(solution)/shard_map/ppermute | solution.py:341
  60.6 21.8 %collective-permute-start.2 = (bf16[2,3,128,512]{3,2,1,0:T(8,128)(2,1)}, bf16[2,3,128,512]{3,2,1,0:T(8,128)(2,1)S(1)}, u32[]{:S(2)}, u32[]{:S(2)}) collective-permute-start(bf16[2,3,128,512]{3,2,1,0:T(8,128)(2,1)} %get-tuple-element.27), channel_id=1, source_target_pairs={{0,32},{1,33},{2,34},{3,35},{4,36},{5,37},{6,38},{7,39},{8,40},{9,... | collective-permute-start | bytes 2359304 | tf_op jit(solution)/shard_map/ppermute | solution.py:341
  63.8 25.1 %collective-permute-start.3 = (bf16[2,3,128,512]{3,2,1,0:T(8,128)(2,1)}, bf16[2,3,128,512]{3,2,1,0:T(8,128)(2,1)}, u32[]{:S(2)}, u32[]{:S(2)}) collective-permute-start(bf16[2,3,128,512]{3,2,1,0:T(8,128)(2,1)} %get-tuple-element.28), channel_id=1, source_target_pairs={{0,48},{1,49},{2,50},{3,51},{4,52},{5,53},{6,54},{7,55},{8,56},{9,... | collective-permute-start | bytes 2359304 | tf_op jit(solution)/shard_map/ppermute | solution.py:341
  65.0 3.4 %copy-start = (bf16[2048,2048]{1,0:T(8,128)(2,1)S(1)}, bf16[2048,2048]{1,0:T(8,128)(2,1)}, u32[]{:S(2)}) copy-start(bf16[2048,2048]{1,0:T(8,128)(2,1)} %w.1) | copy-start | bytes 25165828
  73.6 23.9 %all-to-all-start.2 = ((bf16[128,8,512]{2,1,0:T(8,128)(2,1)}), bf16[128,8,512]{2,1,0:T(8,128)(2,1)}, u32[]{:S(2)}, u32[]{:S(2)}) async-start(bf16[128,8,512]{2,1,0:T(8,128)(2,1)} %bitcast.16), calls=%async_computation.2 | async-start | bytes 2097152 | tf_op jit(solution)/shard_map/all_to_all | solution.py:461
  92.5 16.2 %collective-permute-start.4 = (f32[128,1024]{1,0:T(8,128)}, f32[128,1024]{1,0:T(8,128)S(1)}, u32[]{:S(2)}, u32[]{:S(2)}) collective-permute-start(f32[128,1024]{1,0:T(8,128)} %get-tuple-element.30), channel_id=1, source_target_pairs={{0,4},{1,5},{2,6},{3,7},{4,8},{5,9},{6,10},{7,11},{8,12},{9,13},{1... | collective-permute-start | bytes 1572872 | tf_op jit(solution)/shard_map/ppermute | solution.py:341
  92.5 16.2 %collective-permute-start.5 = (f32[128,1024]{1,0:T(8,128)}, f32[128,1024]{1,0:T(8,128)S(1)}, u32[]{:S(2)}, u32[]{:S(2)}) collective-permute-start(f32[128,1024]{1,0:T(8,128)} %get-tuple-element.31), channel_id=1, source_target_pairs={{0,8},{1,9},{2,10},{3,11},{4,12},{5,13},{6,14},{7,15},{8,0},{9,1},... | collective-permute-start | bytes 1572872 | tf_op jit(solution)/shard_map/ppermute | solution.py:341
  92.5 17.1 %collective-permute-start.6 = (f32[128,1024]{1,0:T(8,128)S(1)}, f32[128,1024]{1,0:T(8,128)S(1)}, u32[]{:S(2)}, u32[]{:S(2)}) collective-permute-start(f32[128,1024]{1,0:T(8,128)S(1)} %get-tuple-element.32), channel_id=1, source_target_pairs={{0,12},{1,13},{2,14},{3,15},{4,0},{5,1},{6,2},{7,3},{8,4},{9,5},{1... | collective-permute-start | bytes 1572872 | tf_op jit(solution)/shard_map/ppermute | solution.py:341

commit v7 on v6

--- a/solution.py
+++ b/solution.py
@@ -228,29 +228,33 @@
     )(at, own, got)
 
 
-def backward_kernel(dpre, tgt_r, w, sending):
+def backward_kernel(dpre, tgt_r, w_any, early, sending, w, sems):
     features, samples = tgt_r.shape
+    copies = load(w_any, w, sems)
     total, wide = sending.shape
     sub = iota((total, samples), 0)
     acc = jnp.zeros((total, wide), F32)
     for f in range(features):
+        for copy in copies[4 * f : 4 * f + 4]:
+            copy.wait()
         grad = dot_t(dpre[...], w[f * wide : (f + 1) * wide, :]).astype(BF)
         put = (tgt_r[f : f + 1, :] == sub).astype(F32).astype(BF)
         acc += dot(put, grad)
     sending[...] = acc.astype(BF)
 
 
-def backward(dpre, tgt_r, w, total):
+def backward(dpre, tgt_r, w, total, early):
     features, samples = tgt_r.shape
     wide = w.shape[0] // features
     return pl.pallas_call(
         backward_kernel,
-        in_specs=[VMEM] * 3,
+        in_specs=[VMEM] * 2 + [ANY, HBM],
         out_specs=VMEM,
         out_shape=struct((total, wide), BF),
-        compiler_params=params(24),
+        scratch_shapes=[pltpu.VMEM(w.shape, BF), pltpu.SemaphoreType.DMA((4 * features,))],
+        compiler_params=params(48),
         cost_estimate=cost(28 * samples * w.size, 10 << 20),
-    )(dpre, tgt_r, w)
+    )(dpre, tgt_r, w, early)
 
 
 def weight_kernel(at, *refs):
@@ -380,27 +384,47 @@
     )(ids)
 
 
-def update_kernel(near, grads, table, accum, out):
-    block, wide = table.shape
-    bag_len, _, slots = near.shape
+def counts_kernel(near, after, out):
+    block, slots = out.shape
     step = pl.program_id(0)
     one, zero = jnp.ones((), BF), jnp.zeros((), BF)
-    pieces, before = [], []
     for k in range(block // 128):
         chunk = step * (block // 128) + k
         here = jnp.full((128, slots), (2 * chunk).astype(F32), F32).astype(BF)
         count = jnp.where(near[0] == here, one, zero)
-        for j in range(1, bag_len):
+        for j in range(1, near.shape[0]):
             count = count + jnp.where(near[j] == here, one, zero)
-        pieces.append(count)
+        out[k * 128 : (k + 1) * 128, :] = count
+
+
+def counts(near, rows, after):
+    slots = near.shape[2]
+    block = 512
+    return pl.pallas_call(
+        counts_kernel,
+        grid=(rows // block,),
+        in_specs=[pl.BlockSpec(near.shape, lambda i: (0, 0, 0)), HBM],
+        out_specs=pl.BlockSpec((block, slots), lambda i: (i, 0)),
+        out_shape=struct((rows, slots), BF),
+        compiler_params=params(16),
+        cost_estimate=cost(8 * rows * slots, 5 << 20),
+    )(near, after)
+
+
+def update_kernel(count, grads, table, accum, out):
+    block, wide = table.shape
+    step = pl.program_id(0)
+    before = []
+    for k in range(block // 128):
+        chunk = step * (block // 128) + k
         before.append(jnp.broadcast_to(accum[pl.ds(chunk, 1), :], (128, 128)).T[:, 0:1])
-    row_grad = dot(jnp.concatenate(pieces, axis=0), grads[...])
+    row_grad = dot(count[...], grads[...])
     square = jnp.sum(row_grad * row_grad, axis=1, keepdims=True)
     new_accum = jnp.concatenate(before, axis=0) + square * (1.0 / wide)
     out[...] = table[...] - row_grad * (learn_rate / jnp.sqrt(new_accum + 1e-6))
 
 
-def update(near, grads, table, accum):
+def update(count, grads, table, accum):
     rows, wide = table.shape
     slots = grads.shape[0]
     block = 512
@@ -408,7 +432,7 @@
         update_kernel,
         grid=(rows // block,),
         in_specs=[
-            pl.BlockSpec(near.shape, lambda i: (0, 0, 0)),
+            pl.BlockSpec((block, slots), lambda i: (i, 0)),
             pl.BlockSpec((slots, wide), lambda i: (0, 0)),
             pl.BlockSpec((block, wide), lambda i: (i, 0)),
             pl.BlockSpec(accum.shape, lambda i: (0, 0)),
@@ -417,7 +441,7 @@
         out_shape=struct((rows, wide), F32),
         compiler_params=params(58),
         cost_estimate=cost(4 * rows * slots * wide, 9 << 20),
-    )(near, grads, table, accum)
+    )(count, grads, table, accum)
 
 
 def per_device(
@@ -456,13 +480,15 @@
         at, slots, cols, hidden_bias[None, :], w_logit[None, :], w_hidden, features, near
     )
     got = lax.ppermute(give, "role", [(0, 1), (1, 0)])
-    sending = backward(dpre, tgt_r, w_hidden, devices * cap)
-    packs = around(merge(at, own, got), (1, 2))
+    packs = merge(at, own, got)
+    count = counts(near, rows_dev, packs[0])
+    packs = around(packs, (1, 2))
+    sending = backward(dpre, tgt_r, w_hidden, devices * cap, count)
     received = lax.all_to_all(
         sending.reshape(devices, cap, width), AXES, split_axis=0, concat_axis=0, tiled=True
     )
     new_table = update(
-        near, received.reshape(devices * cap, width), emb_table, row_accum.reshape(-1, 128)
+        count, received.reshape(devices * cap, width), emb_table, row_accum.reshape(-1, 128)
     )
     parts = around(weight_part(at, packs), (2, 3))
     *parts, new_table = lax.optimization_barrier((*parts, new_table))

time: 124 us -> 122 us (0.984)
  Pallas kernels: 31.9 us -> 37.7 us
  waiting for transfers between devices: 41.5 us -> 36.3 us
  local copies, waits for them, and re-layouts: 3.77 us -> 0.39 us
    ppermute x6, waiting for transfers between devices: 13.3 us -> 1.97 us  [along(): return lax.ppermute(value, AXES, pairs)]
    all_to_all x1, waiting for transfers between devices: 1.79 us -> 7.83 us  [per_device(): lax.all_to_all(sending.reshape(devices, cap, width), AXES, split_axis=0,...]
    pallas_call x1 -> x2, Pallas kernels: 5.2 us -> 10.4 us  [the longest x1 8.8 us: backward(): pl.pallas_call(backward_kernel, in_specs=[VMEM] * 2 + [ANY, HBM], out_spe...]
    unnamed x12 -> x10, local copies, waits for them, and re-layouts: 3.41 us -> 0.03 us
  transfers between devices with their start and end apart: 10 -> 10, of which waited for: 8 -> 6; matrix products, arithmetic and copies ran while one was open for 2% -> 2% of each run, Pallas kernels for 14% -> 19%
where the time goes in v7:
time: 122 us; the launch traced here: 121 us
  Pallas kernels  37.7 us (31%)
  waiting for transfers between devices  36.3 us (30%)
  starting transfers between devices  30.7 us (25%)
  blocking collectives  12.8 us (10%)
  other arithmetic  2.53 us (2%)
    all_to_all x1, waiting for transfers between devices, per_device(): lax.all_to_all(found.reshape(devices, cap, width), AXES, split_axis=0, co...  17.7 us
    all_to_all x1, blocking collectives, per_device(): lax.all_to_all(middle(parts), AXES, split_axis=0, concat_axis=0, tiled=Tr...  12.8 us
    all_to_all x1, starting transfers between devices, per_device(): lax.all_to_all(outgoing, AXES, split_axis=0, concat_axis=0, tiled=True)  11.1 us
    pallas_call x1, Pallas kernels, backward(): pl.pallas_call(backward_kernel, in_specs=[VMEM] * 2 + [ANY, HBM], out_spe...  8.8 us
    ppermute x6, starting transfers between devices, along(): return lax.ppermute(value, AXES, pairs)  8.55 us
    pallas_call x1, Pallas kernels, update(): pl.pallas_call(update_kernel, grid=(rows // block,), in_specs=[pl.BlockSp...  8.27 us
    all_to_all x1, waiting for transfers between devices, per_device(): lax.all_to_all(sending.reshape(devices, cap, width), AXES, split_axis=0,...  7.83 us
    all_to_all x1, waiting for transfers between devices, per_device(): lax.all_to_all(outgoing, AXES, split_axis=0, concat_axis=0, tiled=True)  6.5 us
  transfers between devices with their start and end apart: 10, of which 6 were waited for; matrix products, arithmetic and copies ran while one was open for 2% of the time, Pallas kernels for 19%

profile of v7, /device:TPU:0, one launch (start us, length us, event | category | flops | bytes accessed | tf_op | source)
XLA Modules:
  0.0 121.2 jit_solution(2861752475994043700)
XLA Ops:
  0.6 1.9 %shard_map.104 = (s32[128,32]{1,0:T(8,128)}, f32[128,128]{1,0:T(8,128)}, s32[4,128]{1,0:T(4,128)}) custom-call(s32[4,1,128]{2,1,0:T(1,128)} %bitcast.28, s32[4,4,128]{2,1,0:T(4,128)} %bitcast.27, s32[4,128]{1,0:T(4,128)} %bitcast.29, s32[1,128]{1,0:T(1,128)} %bitcast.30), custom_call_target="tpu_custom_call" | custom-call | tf_op jit(solution)/shard_map/pallas_call | solution.py:93
  2.5 11.1 %all-to-all-start = ((s32[128,1,32]{2,1,0:T(1,128)}), s32[128,1,32]{2,1,0:T(1,128)S(1)}, u32[]{:S(2)}, u32[]{:S(2)}) async-start(s32[128,1,32]{2,1,0:T(1,128)} %bitcast.26), calls=%async_computation | async-start | bytes 131072 | tf_op jit(solution)/shard_map/all_to_all | solution.py:472
  13.7 2.5 %convert_element_type.3.table = bf16[2048,512]{1,0:T(8,128)(2,1)S(1)} convert(f32[2048,512]{1,0:T(8,128)} %table.1) | non-fusion elementwise | flops 1048576 | bytes 6291456 | tf_op jit(solution)/shard_map/convert_element_type | solution.py:471
  16.2 6.5 %all-to-all-done = s32[128,1,32]{2,1,0:T(1,128)S(1)} async-done(((s32[128,1,32]{2,1,0:T(1,128)}), s32[128,1,32]{2,1,0:T(1,128)S(1)}, u32[]{:S(2)}, u32[]{:S(2)}) %all-to-all-start) | async-done | bytes 16416 | tf_op jit(solution)/shard_map/all_to_all | solution.py:472
  23.1 5.1 %shard_map.105 = bf16[1024,512]{1,0:T(8,128)(2,1)} custom-call(s32[128,32]{1,0:T(8,128)S(1)} %bitcast.22, bf16[2048,512]{1,0:T(8,128)(2,1)S(1)} %convert_element_type.3.table), custom_call_target="tpu_custom_call" | custom-call | flops 2147483648 | bytes 4194304 | tf_op jit(solution)/shard_map/pallas_call | solution.py:142
  28.2 4.6 %all-to-all-start.1 = ((bf16[128,8,512]{2,1,0:T(8,128)(2,1)}), bf16[128,8,512]{2,1,0:T(8,128)(2,1)S(1)}, u32[]{:S(2)}, u32[]{:S(2)}) async-start(bf16[128,8,512]{2,1,0:T(8,128)(2,1)} %bitcast.10), calls=%async_computation.1 | async-start | bytes 2097152 | tf_op jit(solution)/shard_map/all_to_all | solution.py:474
  33.1 17.7 %all-to-all-done.1 = bf16[128,8,512]{2,1,0:T(8,128)(2,1)S(1)} async-done(((bf16[128,8,512]{2,1,0:T(8,128)(2,1)}), bf16[128,8,512]{2,1,0:T(8,128)(2,1)S(1)}, u32[]{:S(2)}, u32[]{:S(2)}) %all-to-all-start.1) | async-done | bytes 1048608 | tf_op jit(solution)/shard_map/all_to_all | solution.py:474
  50.8 5.2 %shard_map.107 = (bf16[6,128,512]{2,1,0:T(8,128)(2,1)S(1)}, bf16[6,128,512]{2,1,0:T(8,128)(2,1)S(1)}, bf16[128,2048]{1,0:T(8,128)(2,1)S(1)}) custom-call(s32[3]{0:T(128)S(1)} %pad_add_fusion.at, bf16[1024,512]{1,0:T(8,128)(2,1)S(1)} %bitcast.21, f32[128,128]{1,0:T(8,128)S(1)} %copy-done.1, f32[1,2048]{1,0:T(1,128)S(1)} %bitcast.23, f32[1,2048]{1,0:T(1,128)S(1)} %bitcast.24, ...), custom_call_target="tpu_custom_call" | custom-call | flops 1073741824 | bytes 10485760 | tf_op jit(solution)/shard_map/pallas_call | solution.py:198
  56.1 2.3 %collective-permute-done.got = bf16[6,128,512]{2,1,0:T(8,128)(2,1)S(1)} collective-permute-done((bf16[6,128,512]{2,1,0:T(8,128)(2,1)S(1)}, bf16[6,128,512]{2,1,0:T(8,128)(2,1)S(1)}, u32[]{:S(2)}, u32[]{:S(2)}) %collective-permute-start) | collective-permute-done | bytes 786464 | tf_op jit(solution)/shard_map/ppermute | solution.py:482
  58.4 2.1 %shard_map.108 = (bf16[2,3,128,512]{3,2,1,0:T(8,128)(2,1)S(1)}, bf16[2,3,128,512]{3,2,1,0:T(8,128)(2,1)}, bf16[2,3,128,512]{3,2,1,0:T(8,128)(2,1)}, bf16[2,3,128,512]{3,2,1,0:T(8,128)(2,1)}) custom-call(s32[3]{0:T(128)S(1)} %pad_add_fusion.at, bf16[6,128,512]{2,1,0:T(8,128)(2,1)S(1)} %get-tuple-element.23.own, bf16[6,128,512]{2,1,0:T(8,128)(2,1)S(1)} %collective-permute-done.got), custom_call_target="tpu_custom_call" | custom-call | flops 1048576 | bytes 6291456 | tf_op jit(solution)/shard_map/pallas_call | solution.py:221
  60.6 3.2 %collective-permute-start.2 = (bf16[2,3,128,512]{3,2,1,0:T(8,128)(2,1)}, bf16[2,3,128,512]{3,2,1,0:T(8,128)(2,1)}, u32[]{:S(2)}, u32[]{:S(2)}) collective-permute-start(bf16[2,3,128,512]{3,2,1,0:T(8,128)(2,1)} %get-tuple-element.27), channel_id=1, source_target_pairs={{0,32},{1,33},{2,34},{3,35},{4,36},{5,37},{6,38},{7,39},{8,40},{9,... | collective-permute-start | bytes 2359304 | tf_op jit(solution)/shard_map/ppermute | solution.py:345
  63.8 1.2 collective-permute-start.3
  65.0 1.6 %shard_map.110.early.count = bf16[2048,1024]{1,0:T(8,128)(2,1)S(1)} custom-call(bf16[4,128,1024]{2,1,0:T(8,128)(2,1)S(1)} %shard_map.106.early.near, bf16[2,3,128,512]{3,2,1,0:T(8,128)(2,1)S(1)} %get-tuple-element.25.refs_0_.after), custom_call_target="tpu_custom_call" | custom-call | flops 16777216 | bytes 5242880 | tf_op jit(solution)/shard_map/pallas_call | solution.py:403
  66.6 8.8 %shard_map.111 = bf16[1024,512]{1,0:T(8,128)(2,1)} custom-call(bf16[128,2048]{1,0:T(8,128)(2,1)S(1)} %get-tuple-element.33.dpre, s32[4,128]{1,0:T(4,128)S(1)} %copy-done.4, bf16[2048,2048]{1,0:T(8,128)(2,1)} %w_any.3, bf16[2048,1024]{1,0:T(8,128)(2,1)S(1)} %shard_map.110.early.count), custom_call_target="tpu_custom_call" | custom-call | flops 15032385536 | bytes 10485760 | tf_op jit(solution)/shard_map/pallas_call | solution.py:249
  75.4 6.3 %all-to-all-start.2 = ((bf16[128,8,512]{2,1,0:T(8,128)(2,1)}), bf16[128,8,512]{2,1,0:T(8,128)(2,1)}, u32[]{:S(2)}, u32[]{:S(2)}) async-start(bf16[128,8,512]{2,1,0:T(8,128)(2,1)} %bitcast.16), calls=%async_computation.2 | async-start | bytes 2097152 | tf_op jit(solution)/shard_map/all_to_all | solution.py:487
  81.7 0.8 collective-permute-done.2.refs_2_
  82.5 1.2 collective-permute-done.3.refs_3_
  83.7 3.7 %shard_map.109 = (f32[128,1024]{1,0:T(8,128)S(1)}, f32[128,1024]{1,0:T(8,128)}, f32[128,1024]{1,0:T(8,128)}, f32[128,1024]{1,0:T(8,128)S(1)}) custom-call(s32[3]{0:T(128)S(1)} %pad_add_fusion.at, bf16[2,3,128,512]{3,2,1,0:T(8,128)(2,1)S(1)} %get-tuple-element.25.refs_0_.after, bf16[2,3,128,512]{3,2,1,0:T(8,128)(2,1)S(1)} %collective-permute-done.1.refs_1_, ...), custom_call_target="tpu_custom_call" | custom-call | flops 40000000000 | bytes 8388608 | tf_op jit(solution)/shard_map/pallas_call | solution.py:284
  87.4 2.1 %collective-permute-start.5 = (f32[128,1024]{1,0:T(8,128)}, f32[128,1024]{1,0:T(8,128)S(1)}, u32[]{:S(2)}, u32[]{:S(2)}) collective-permute-start(f32[128,1024]{1,0:T(8,128)} %get-tuple-element.31), channel_id=1, source_target_pairs={{0,8},{1,9},{2,10},{3,11},{4,12},{5,13},{6,14},{7,15},{8,0},{9,1},... | collective-permute-start | bytes 1572872 | tf_op jit(solution)/shard_map/ppermute | solution.py:345
  89.5 2.0 %collective-permute-start.6 = (f32[128,1024]{1,0:T(8,128)S(1)}, f32[128,1024]{1,0:T(8,128)S(1)}, u32[]{:S(2)}, u32[]{:S(2)}) collective-permute-start(f32[128,1024]{1,0:T(8,128)S(1)} %get-tuple-element.32), channel_id=1, source_target_pairs={{0,12},{1,13},{2,14},{3,15},{4,0},{5,1},{6,2},{7,3},{8,4},{9,5},{1... | collective-permute-start | bytes 1572872 | tf_op jit(solution)/shard_map/ppermute | solution.py:345
  91.5 7.8 %all-to-all-done.2 = bf16[128,8,512]{2,1,0:T(8,128)(2,1)} async-done(((bf16[128,8,512]{2,1,0:T(8,128)(2,1)}), bf16[128,8,512]{2,1,0:T(8,128)(2,1)}, u32[]{:S(2)}, u32[]{:S(2)}) %all-to-all-start.2) | async-done | bytes 1048608 | tf_op jit(solution)/shard_map/all_to_all | solution.py:487
  99.3 8.3 %shard_map.112 = f32[2048,512]{1,0:T(8,128)} custom-call(bf16[2048,1024]{1,0:T(8,128)(2,1)} %copy-done, bf16[1024,512]{1,0:T(8,128)(2,1)} %bitcast.17.grads, f32[2048,512]{1,0:T(8,128)} %table.1, f32[16,128]{1,0:T(8,128)} %bitcast.31), custom_call_target="tpu_custom_call" | custom-call | flops 4294967296 | bytes 9437184 | tf_op jit(solution)/shard_map/pallas_call | solution.py:431
  107.7 12.8 %all_to_all.26.parts = f32[8,16,1024]{2,1,0:T(8,128)S(1)} all-to-all(f32[8,16,1024]{2,1,0:T(8,128)S(1)} %shard_map.113), channel_id=1, replica_groups={{0,1,2,3,16,17,18,19},{64,80,96,112,68,84,100,116},{4,5,6,7,20,21,22,23..., dimensions={0} | all-to-all | bytes 1048576 | tf_op jit(solution)/shard_map/all_to_all | solution.py:495
  120.5 0.7 shard_map.114
  (23 shorter events, 1.0 us)
Async XLA Ops:
  2.5 20.2 %all-to-all-start = ((s32[128,1,32]{2,1,0:T(1,128)}), s32[128,1,32]{2,1,0:T(1,128)S(1)}, u32[]{:S(2)}, u32[]{:S(2)}) async-start(s32[128,1,32]{2,1,0:T(1,128)} %bitcast.26), calls=%async_computation | async-start | bytes 131072 | tf_op jit(solution)/shard_map/all_to_all | solution.py:472
  28.2 22.6 %all-to-all-start.1 = ((bf16[128,8,512]{2,1,0:T(8,128)(2,1)}), bf16[128,8,512]{2,1,0:T(8,128)(2,1)S(1)}, u32[]{:S(2)}, u32[]{:S(2)}) async-start(bf16[128,8,512]{2,1,0:T(8,128)(2,1)} %bitcast.10), calls=%async_computation.1 | async-start | bytes 2097152 | tf_op jit(solution)/shard_map/all_to_all | solution.py:474
  32.8 18.0 %copy-start.1 = (f32[128,128]{1,0:T(8,128)S(1)}, f32[128,128]{1,0:T(8,128)}, u32[]{:S(2)}) copy-start(f32[128,128]{1,0:T(8,128)} %get-tuple-element.22.cols) | copy-start | bytes 196612
  32.8 18.0 %copy-start.2 = (f32[2048]{0:T(1024)S(1)}, f32[2048]{0:T(1024)}, u32[]{:S(2)}) copy-start(f32[2048]{0:T(1024)} %param.16) | copy-start | bytes 24580
  32.8 18.0 %copy-start.3 = (f32[2048]{0:T(1024)S(1)}, f32[2048]{0:T(1024)}, u32[]{:S(2)}) copy-start(f32[2048]{0:T(1024)} %param.17) | copy-start | bytes 24580
  56.0 10.6 %copy-start.4 = (s32[4,128]{1,0:T(4,128)S(1)}, s32[4,128]{1,0:T(4,128)}, u32[]{:S(2)}) copy-start(s32[4,128]{1,0:T(4,128)} %get-tuple-element.34.tgt_r) | copy-start | bytes 6148
  56.0 2.4 %collective-permute-start = (bf16[6,128,512]{2,1,0:T(8,128)(2,1)S(1)}, bf16[6,128,512]{2,1,0:T(8,128)(2,1)S(1)}, u32[]{:S(2)}, u32[]{:S(2)}) collective-permute-start(bf16[6,128,512]{2,1,0:T(8,128)(2,1)S(1)} %get-tuple-element.24), channel_id=1, source_target_pairs={{0,64},{64,0},{1,65},{65,1},{2,66},{66,2},{3,67},{67,3},{4,68},{68... | collective-permute-start | bytes 2359304 | tf_op jit(solution)/shard_map/ppermute | solution.py:482
  60.5 21.2 %collective-permute-start.1 = (bf16[2,3,128,512]{3,2,1,0:T(8,128)(2,1)}, bf16[2,3,128,512]{3,2,1,0:T(8,128)(2,1)S(1)}, u32[]{:S(2)}, u32[]{:S(2)}) collective-permute-start(bf16[2,3,128,512]{3,2,1,0:T(8,128)(2,1)} %get-tuple-element.26), channel_id=1, source_target_pairs={{0,16},{1,17},{2,18},{3,19},{4,20},{5,21},{6,22},{7,23},{8,24},{9,... | collective-permute-start | bytes 2359304 | tf_op jit(solution)/shard_map/ppermute | solution.py:345
  60.6 21.9 %collective-permute-start.2 = (bf16[2,3,128,512]{3,2,1,0:T(8,128)(2,1)}, bf16[2,3,128,512]{3,2,1,0:T(8,128)(2,1)}, u32[]{:S(2)}, u32[]{:S(2)}) collective-permute-start(bf16[2,3,128,512]{3,2,1,0:T(8,128)(2,1)} %get-tuple-element.27), channel_id=1, source_target_pairs={{0,32},{1,33},{2,34},{3,35},{4,36},{5,37},{6,38},{7,39},{8,40},{9,... | collective-permute-start | bytes 2359304 | tf_op jit(solution)/shard_map/ppermute | solution.py:345
  63.8 19.9 %collective-permute-start.3 = (bf16[2,3,128,512]{3,2,1,0:T(8,128)(2,1)}, bf16[2,3,128,512]{3,2,1,0:T(8,128)(2,1)}, u32[]{:S(2)}, u32[]{:S(2)}) collective-permute-start(bf16[2,3,128,512]{3,2,1,0:T(8,128)(2,1)} %get-tuple-element.28), channel_id=1, source_target_pairs={{0,48},{1,49},{2,50},{3,51},{4,52},{5,53},{6,54},{7,55},{8,56},{9,... | collective-permute-start | bytes 2359304 | tf_op jit(solution)/shard_map/ppermute | solution.py:345
  66.6 8.8 %copy-start = (bf16[2048,1024]{1,0:T(8,128)(2,1)}, bf16[2048,1024]{1,0:T(8,128)(2,1)S(1)}, u32[]{:S(2)}) copy-start(bf16[2048,1024]{1,0:T(8,128)(2,1)S(1)} %shard_map.110.early.count) | copy-start | bytes 12582916
  75.4 23.9 %all-to-all-start.2 = ((bf16[128,8,512]{2,1,0:T(8,128)(2,1)}), bf16[128,8,512]{2,1,0:T(8,128)(2,1)}, u32[]{:S(2)}, u32[]{:S(2)}) async-start(bf16[128,8,512]{2,1,0:T(8,128)(2,1)} %bitcast.16), calls=%async_computation.2 | async-start | bytes 2097152 | tf_op jit(solution)/shard_map/all_to_all | solution.py:487
  87.4 20.2 %collective-permute-start.4 = (f32[128,1024]{1,0:T(8,128)}, f32[128,1024]{1,0:T(8,128)S(1)}, u32[]{:S(2)}, u32[]{:S(2)}) collective-permute-start(f32[128,1024]{1,0:T(8,128)} %get-tuple-element.30), channel_id=1, source_target_pairs={{0,4},{1,5},{2,6},{3,7},{4,8},{5,9},{6,10},{7,11},{8,12},{9,13},{1... | collective-permute-start | bytes 1572872 | tf_op jit(solution)/shard_map/ppermute | solution.py:345
  87.4 20.2 %collective-permute-start.5 = (f32[128,1024]{1,0:T(8,128)}, f32[128,1024]{1,0:T(8,128)S(1)}, u32[]{:S(2)}, u32[]{:S(2)}) collective-permute-start(f32[128,1024]{1,0:T(8,128)} %get-tuple-element.31), channel_id=1, source_target_pairs={{0,8},{1,9},{2,10},{3,11},{4,12},{5,13},{6,14},{7,15},{8,0},{9,1},... | collective-permute-start | bytes 1572872 | tf_op jit(solution)/shard_map/ppermute | solution.py:345
  89.5 18.1 %collective-permute-start.6 = (f32[128,1024]{1,0:T(8,128)S(1)}, f32[128,1024]{1,0:T(8,128)S(1)}, u32[]{:S(2)}, u32[]{:S(2)}) collective-permute-start(f32[128,1024]{1,0:T(8,128)S(1)} %get-tuple-element.32), channel_id=1, source_target_pairs={{0,12},{1,13},{2,14},{3,15},{4,0},{5,1},{6,2},{7,3},{8,4},{9,5},{1... | collective-permute-start | bytes 1572872 | tf_op jit(solution)/shard_map/ppermute | solution.py:345

commit v8 on v7

--- a/solution.py
+++ b/solution.py
@@ -427,7 +427,7 @@
 def update(count, grads, table, accum):
     rows, wide = table.shape
     slots = grads.shape[0]
-    block = 512
+    block = 256
     return pl.pallas_call(
         update_kernel,
         grid=(rows // block,),

time: 122 us -> 122 us (level)
  Pallas kernels: 37.7 us -> 39.4 us
    pallas_call x1, Pallas kernels: 8.27 us -> 9.96 us  [update(): pl.pallas_call(update_kernel, grid=(rows // block,), in_specs=[pl.BlockSp...]
  transfers between devices with their start and end apart: 10 -> 10, of which waited for: 6 -> 6; matrix products, arithmetic and copies ran while one was open for 2% -> 2% of each run, Pallas kernels for 19% -> 20%
where the time goes in v8:
time: 122 us
  Pallas kernels  39.4 us (32%)
  waiting for transfers between devices  36.3 us (30%)
  starting transfers between devices  30.7 us (25%)
  blocking collectives  11.7 us (10%)
  other arithmetic  2.53 us (2%)
    all_to_all x1, waiting for transfers between devices, per_device(): lax.all_to_all(found.reshape(devices, cap, width), AXES, split_axis=0, co...  17.7 us
    all_to_all x1, blocking collectives, per_device(): lax.all_to_all(middle(parts), AXES, split_axis=0, concat_axis=0, tiled=Tr...  11.7 us
    all_to_all x1, starting transfers between devices, per_device(): lax.all_to_all(outgoing, AXES, split_axis=0, concat_axis=0, tiled=True)  11.1 us
    pallas_call x1, Pallas kernels, update(): pl.pallas_call(update_kernel, grid=(rows // block,), in_specs=[pl.BlockSp...  9.96 us
    pallas_call x1, Pallas kernels, backward(): pl.pallas_call(backward_kernel, in_specs=[VMEM] * 2 + [ANY, HBM], out_spe...  8.8 us
    ppermute x6, starting transfers between devices, along(): return lax.ppermute(value, AXES, pairs)  8.55 us
    all_to_all x1, waiting for transfers between devices, per_device(): lax.all_to_all(sending.reshape(devices, cap, width), AXES, split_axis=0,...  7.83 us
    all_to_all x1, waiting for transfers between devices, per_device(): lax.all_to_all(outgoing, AXES, split_axis=0, concat_axis=0, tiled=True)  6.5 us
  transfers between devices with their start and end apart: 10, of which 6 were waited for; matrix products, arithmetic and copies ran while one was open for 2% of the time, Pallas kernels for 20%

profile of v8, /device:TPU:0, one launch (start us, length us, event | category | flops | bytes accessed | tf_op | source)
XLA Modules:
  0.0 121.8 jit_solution(9890848165326169918)
XLA Ops:
  0.6 1.9 %shard_map.104 = (s32[128,32]{1,0:T(8,128)}, f32[128,128]{1,0:T(8,128)}, s32[4,128]{1,0:T(4,128)}) custom-call(s32[4,1,128]{2,1,0:T(1,128)} %bitcast.28, s32[4,4,128]{2,1,0:T(4,128)} %bitcast.27, s32[4,128]{1,0:T(4,128)} %bitcast.29, s32[1,128]{1,0:T(1,128)} %bitcast.30), custom_call_target="tpu_custom_call" | custom-call | tf_op jit(solution)/shard_map/pallas_call | solution.py:93
  2.5 11.1 %all-to-all-start = ((s32[128,1,32]{2,1,0:T(1,128)}), s32[128,1,32]{2,1,0:T(1,128)S(1)}, u32[]{:S(2)}, u32[]{:S(2)}) async-start(s32[128,1,32]{2,1,0:T(1,128)} %bitcast.26), calls=%async_computation | async-start | bytes 131072 | tf_op jit(solution)/shard_map/all_to_all | solution.py:472
  13.7 2.5 %convert_element_type.3.table = bf16[2048,512]{1,0:T(8,128)(2,1)S(1)} convert(f32[2048,512]{1,0:T(8,128)} %table.1) | non-fusion elementwise | flops 1048576 | bytes 6291456 | tf_op jit(solution)/shard_map/convert_element_type | solution.py:471
  16.2 6.5 %all-to-all-done = s32[128,1,32]{2,1,0:T(1,128)S(1)} async-done(((s32[128,1,32]{2,1,0:T(1,128)}), s32[128,1,32]{2,1,0:T(1,128)S(1)}, u32[]{:S(2)}, u32[]{:S(2)}) %all-to-all-start) | async-done | bytes 16416 | tf_op jit(solution)/shard_map/all_to_all | solution.py:472
  23.1 5.1 %shard_map.105 = bf16[1024,512]{1,0:T(8,128)(2,1)} custom-call(s32[128,32]{1,0:T(8,128)S(1)} %bitcast.22, bf16[2048,512]{1,0:T(8,128)(2,1)S(1)} %convert_element_type.3.table), custom_call_target="tpu_custom_call" | custom-call | flops 2147483648 | bytes 4194304 | tf_op jit(solution)/shard_map/pallas_call | solution.py:142
  28.2 4.6 %all-to-all-start.1 = ((bf16[128,8,512]{2,1,0:T(8,128)(2,1)}), bf16[128,8,512]{2,1,0:T(8,128)(2,1)S(1)}, u32[]{:S(2)}, u32[]{:S(2)}) async-start(bf16[128,8,512]{2,1,0:T(8,128)(2,1)} %bitcast.10), calls=%async_computation.1 | async-start | bytes 2097152 | tf_op jit(solution)/shard_map/all_to_all | solution.py:474
  33.1 17.7 %all-to-all-done.1 = bf16[128,8,512]{2,1,0:T(8,128)(2,1)S(1)} async-done(((bf16[128,8,512]{2,1,0:T(8,128)(2,1)}), bf16[128,8,512]{2,1,0:T(8,128)(2,1)S(1)}, u32[]{:S(2)}, u32[]{:S(2)}) %all-to-all-start.1) | async-done | bytes 1048608 | tf_op jit(solution)/shard_map/all_to_all | solution.py:474
  50.8 5.2 %shard_map.107 = (bf16[6,128,512]{2,1,0:T(8,128)(2,1)S(1)}, bf16[6,128,512]{2,1,0:T(8,128)(2,1)S(1)}, bf16[128,2048]{1,0:T(8,128)(2,1)S(1)}) custom-call(s32[3]{0:T(128)S(1)} %pad_add_fusion.at, bf16[1024,512]{1,0:T(8,128)(2,1)S(1)} %bitcast.21, f32[128,128]{1,0:T(8,128)S(1)} %copy-done.1, f32[1,2048]{1,0:T(1,128)S(1)} %bitcast.23, f32[1,2048]{1,0:T(1,128)S(1)} %bitcast.24, ...), custom_call_target="tpu_custom_call" | custom-call | flops 1073741824 | bytes 10485760 | tf_op jit(solution)/shard_map/pallas_call | solution.py:198
  56.1 2.3 %collective-permute-done.got = bf16[6,128,512]{2,1,0:T(8,128)(2,1)S(1)} collective-permute-done((bf16[6,128,512]{2,1,0:T(8,128)(2,1)S(1)}, bf16[6,128,512]{2,1,0:T(8,128)(2,1)S(1)}, u32[]{:S(2)}, u32[]{:S(2)}) %collective-permute-start) | collective-permute-done | bytes 786464 | tf_op jit(solution)/shard_map/ppermute | solution.py:482
  58.4 2.1 %shard_map.108 = (bf16[2,3,128,512]{3,2,1,0:T(8,128)(2,1)S(1)}, bf16[2,3,128,512]{3,2,1,0:T(8,128)(2,1)}, bf16[2,3,128,512]{3,2,1,0:T(8,128)(2,1)}, bf16[2,3,128,512]{3,2,1,0:T(8,128)(2,1)}) custom-call(s32[3]{0:T(128)S(1)} %pad_add_fusion.at, bf16[6,128,512]{2,1,0:T(8,128)(2,1)S(1)} %get-tuple-element.23.own, bf16[6,128,512]{2,1,0:T(8,128)(2,1)S(1)} %collective-permute-done.got), custom_call_target="tpu_custom_call" | custom-call | flops 1048576 | bytes 6291456 | tf_op jit(solution)/shard_map/pallas_call | solution.py:221
  60.6 3.2 %collective-permute-start.2 = (bf16[2,3,128,512]{3,2,1,0:T(8,128)(2,1)}, bf16[2,3,128,512]{3,2,1,0:T(8,128)(2,1)}, u32[]{:S(2)}, u32[]{:S(2)}) collective-permute-start(bf16[2,3,128,512]{3,2,1,0:T(8,128)(2,1)} %get-tuple-element.27), channel_id=1, source_target_pairs={{0,32},{1,33},{2,34},{3,35},{4,36},{5,37},{6,38},{7,39},{8,40},{9,... | collective-permute-start | bytes 2359304 | tf_op jit(solution)/shard_map/ppermute | solution.py:345
  63.8 1.2 collective-permute-start.3
  65.0 1.6 %shard_map.110.early.count = bf16[2048,1024]{1,0:T(8,128)(2,1)S(1)} custom-call(bf16[4,128,1024]{2,1,0:T(8,128)(2,1)S(1)} %shard_map.106.early.near, bf16[2,3,128,512]{3,2,1,0:T(8,128)(2,1)S(1)} %get-tuple-element.25.refs_0_.after), custom_call_target="tpu_custom_call" | custom-call | flops 16777216 | bytes 5242880 | tf_op jit(solution)/shard_map/pallas_call | solution.py:403
  66.6 8.8 %shard_map.111 = bf16[1024,512]{1,0:T(8,128)(2,1)} custom-call(bf16[128,2048]{1,0:T(8,128)(2,1)S(1)} %get-tuple-element.33.dpre, s32[4,128]{1,0:T(4,128)S(1)} %copy-done.4, bf16[2048,2048]{1,0:T(8,128)(2,1)} %w_any.3, bf16[2048,1024]{1,0:T(8,128)(2,1)S(1)} %shard_map.110.early.count), custom_call_target="tpu_custom_call" | custom-call | flops 15032385536 | bytes 10485760 | tf_op jit(solution)/shard_map/pallas_call | solution.py:249
  75.4 6.3 %all-to-all-start.2 = ((bf16[128,8,512]{2,1,0:T(8,128)(2,1)}), bf16[128,8,512]{2,1,0:T(8,128)(2,1)}, u32[]{:S(2)}, u32[]{:S(2)}) async-start(bf16[128,8,512]{2,1,0:T(8,128)(2,1)} %bitcast.16), calls=%async_computation.2 | async-start | bytes 2097152 | tf_op jit(solution)/shard_map/all_to_all | solution.py:487
  81.7 0.8 collective-permute-done.2.refs_2_
  82.5 1.2 collective-permute-done.3.refs_3_
  83.7 3.7 %shard_map.109 = (f32[128,1024]{1,0:T(8,128)S(1)}, f32[128,1024]{1,0:T(8,128)}, f32[128,1024]{1,0:T(8,128)}, f32[128,1024]{1,0:T(8,128)S(1)}) custom-call(s32[3]{0:T(128)S(1)} %pad_add_fusion.at, bf16[2,3,128,512]{3,2,1,0:T(8,128)(2,1)S(1)} %get-tuple-element.25.refs_0_.after, bf16[2,3,128,512]{3,2,1,0:T(8,128)(2,1)S(1)} %collective-permute-done.1.refs_1_, ...), custom_call_target="tpu_custom_call" | custom-call | flops 40000000000 | bytes 8388608 | tf_op jit(solution)/shard_map/pallas_call | solution.py:284
  87.4 2.1 %collective-permute-start.5 = (f32[128,1024]{1,0:T(8,128)}, f32[128,1024]{1,0:T(8,128)S(1)}, u32[]{:S(2)}, u32[]{:S(2)}) collective-permute-start(f32[128,1024]{1,0:T(8,128)} %get-tuple-element.31), channel_id=1, source_target_pairs={{0,8},{1,9},{2,10},{3,11},{4,12},{5,13},{6,14},{7,15},{8,0},{9,1},... | collective-permute-start | bytes 1572872 | tf_op jit(solution)/shard_map/ppermute | solution.py:345
  89.5 2.0 %collective-permute-start.6 = (f32[128,1024]{1,0:T(8,128)S(1)}, f32[128,1024]{1,0:T(8,128)S(1)}, u32[]{:S(2)}, u32[]{:S(2)}) collective-permute-start(f32[128,1024]{1,0:T(8,128)S(1)} %get-tuple-element.32), channel_id=1, source_target_pairs={{0,12},{1,13},{2,14},{3,15},{4,0},{5,1},{6,2},{7,3},{8,4},{9,5},{1... | collective-permute-start | bytes 1572872 | tf_op jit(solution)/shard_map/ppermute | solution.py:345
  91.5 7.8 %all-to-all-done.2 = bf16[128,8,512]{2,1,0:T(8,128)(2,1)} async-done(((bf16[128,8,512]{2,1,0:T(8,128)(2,1)}), bf16[128,8,512]{2,1,0:T(8,128)(2,1)}, u32[]{:S(2)}, u32[]{:S(2)}) %all-to-all-start.2) | async-done | bytes 1048608 | tf_op jit(solution)/shard_map/all_to_all | solution.py:487
  99.3 10.0 %shard_map.112 = f32[2048,512]{1,0:T(8,128)} custom-call(bf16[2048,1024]{1,0:T(8,128)(2,1)} %copy-done, bf16[1024,512]{1,0:T(8,128)(2,1)} %bitcast.17.grads, f32[2048,512]{1,0:T(8,128)} %table.1, f32[16,128]{1,0:T(8,128)} %bitcast.31), custom_call_target="tpu_custom_call" | custom-call | flops 4294967296 | bytes 9437184 | tf_op jit(solution)/shard_map/pallas_call | solution.py:431
  109.4 11.7 %all_to_all.26.parts = f32[8,16,1024]{2,1,0:T(8,128)S(1)} all-to-all(f32[8,16,1024]{2,1,0:T(8,128)S(1)} %shard_map.113), channel_id=1, replica_groups={{0,1,2,3,16,17,18,19},{64,80,96,112,68,84,100,116},{4,5,6,7,20,21,22,23..., dimensions={0} | all-to-all | bytes 1048576 | tf_op jit(solution)/shard_map/all_to_all | solution.py:495
  121.1 0.7 shard_map.114
  (23 shorter events, 1.0 us)
Async XLA Ops:
  2.5 20.2 %all-to-all-start = ((s32[128,1,32]{2,1,0:T(1,128)}), s32[128,1,32]{2,1,0:T(1,128)S(1)}, u32[]{:S(2)}, u32[]{:S(2)}) async-start(s32[128,1,32]{2,1,0:T(1,128)} %bitcast.26), calls=%async_computation | async-start | bytes 131072 | tf_op jit(solution)/shard_map/all_to_all | solution.py:472
  28.2 22.6 %all-to-all-start.1 = ((bf16[128,8,512]{2,1,0:T(8,128)(2,1)}), bf16[128,8,512]{2,1,0:T(8,128)(2,1)S(1)}, u32[]{:S(2)}, u32[]{:S(2)}) async-start(bf16[128,8,512]{2,1,0:T(8,128)(2,1)} %bitcast.10), calls=%async_computation.1 | async-start | bytes 2097152 | tf_op jit(solution)/shard_map/all_to_all | solution.py:474
  32.8 18.0 %copy-start.1 = (f32[128,128]{1,0:T(8,128)S(1)}, f32[128,128]{1,0:T(8,128)}, u32[]{:S(2)}) copy-start(f32[128,128]{1,0:T(8,128)} %get-tuple-element.22.cols) | copy-start | bytes 196612
  32.8 18.0 %copy-start.2 = (f32[2048]{0:T(1024)S(1)}, f32[2048]{0:T(1024)}, u32[]{:S(2)}) copy-start(f32[2048]{0:T(1024)} %param.16) | copy-start | bytes 24580
  32.8 18.0 %copy-start.3 = (f32[2048]{0:T(1024)S(1)}, f32[2048]{0:T(1024)}, u32[]{:S(2)}) copy-start(f32[2048]{0:T(1024)} %param.17) | copy-start | bytes 24580
  56.0 10.6 %copy-start.4 = (s32[4,128]{1,0:T(4,128)S(1)}, s32[4,128]{1,0:T(4,128)}, u32[]{:S(2)}) copy-start(s32[4,128]{1,0:T(4,128)} %get-tuple-element.34.tgt_r) | copy-start | bytes 6148
  56.0 2.4 %collective-permute-start = (bf16[6,128,512]{2,1,0:T(8,128)(2,1)S(1)}, bf16[6,128,512]{2,1,0:T(8,128)(2,1)S(1)}, u32[]{:S(2)}, u32[]{:S(2)}) collective-permute-start(bf16[6,128,512]{2,1,0:T(8,128)(2,1)S(1)} %get-tuple-element.24), channel_id=1, source_target_pairs={{0,64},{64,0},{1,65},{65,1},{2,66},{66,2},{3,67},{67,3},{4,68},{68... | collective-permute-start | bytes 2359304 | tf_op jit(solution)/shard_map/ppermute | solution.py:482
  60.5 21.2 %collective-permute-start.1 = (bf16[2,3,128,512]{3,2,1,0:T(8,128)(2,1)}, bf16[2,3,128,512]{3,2,1,0:T(8,128)(2,1)S(1)}, u32[]{:S(2)}, u32[]{:S(2)}) collective-permute-start(bf16[2,3,128,512]{3,2,1,0:T(8,128)(2,1)} %get-tuple-element.26), channel_id=1, source_target_pairs={{0,16},{1,17},{2,18},{3,19},{4,20},{5,21},{6,22},{7,23},{8,24},{9,... | collective-permute-start | bytes 2359304 | tf_op jit(solution)/shard_map/ppermute | solution.py:345
  60.6 21.9 %collective-permute-start.2 = (bf16[2,3,128,512]{3,2,1,0:T(8,128)(2,1)}, bf16[2,3,128,512]{3,2,1,0:T(8,128)(2,1)}, u32[]{:S(2)}, u32[]{:S(2)}) collective-permute-start(bf16[2,3,128,512]{3,2,1,0:T(8,128)(2,1)} %get-tuple-element.27), channel_id=1, source_target_pairs={{0,32},{1,33},{2,34},{3,35},{4,36},{5,37},{6,38},{7,39},{8,40},{9,... | collective-permute-start | bytes 2359304 | tf_op jit(solution)/shard_map/ppermute | solution.py:345
  63.8 19.9 %collective-permute-start.3 = (bf16[2,3,128,512]{3,2,1,0:T(8,128)(2,1)}, bf16[2,3,128,512]{3,2,1,0:T(8,128)(2,1)}, u32[]{:S(2)}, u32[]{:S(2)}) collective-permute-start(bf16[2,3,128,512]{3,2,1,0:T(8,128)(2,1)} %get-tuple-element.28), channel_id=1, source_target_pairs={{0,48},{1,49},{2,50},{3,51},{4,52},{5,53},{6,54},{7,55},{8,56},{9,... | collective-permute-start | bytes 2359304 | tf_op jit(solution)/shard_map/ppermute | solution.py:345
  66.6 8.8 %copy-start = (bf16[2048,1024]{1,0:T(8,128)(2,1)}, bf16[2048,1024]{1,0:T(8,128)(2,1)S(1)}, u32[]{:S(2)}) copy-start(bf16[2048,1024]{1,0:T(8,128)(2,1)S(1)} %shard_map.110.early.count) | copy-start | bytes 12582916
  75.4 23.9 %all-to-all-start.2 = ((bf16[128,8,512]{2,1,0:T(8,128)(2,1)}), bf16[128,8,512]{2,1,0:T(8,128)(2,1)}, u32[]{:S(2)}, u32[]{:S(2)}) async-start(bf16[128,8,512]{2,1,0:T(8,128)(2,1)} %bitcast.16), calls=%async_computation.2 | async-start | bytes 2097152 | tf_op jit(solution)/shard_map/all_to_all | solution.py:487
  87.4 21.8 %collective-permute-start.4 = (f32[128,1024]{1,0:T(8,128)}, f32[128,1024]{1,0:T(8,128)S(1)}, u32[]{:S(2)}, u32[]{:S(2)}) collective-permute-start(f32[128,1024]{1,0:T(8,128)} %get-tuple-element.30), channel_id=1, source_target_pairs={{0,4},{1,5},{2,6},{3,7},{4,8},{5,9},{6,10},{7,11},{8,12},{9,13},{1... | collective-permute-start | bytes 1572872 | tf_op jit(solution)/shard_map/ppermute | solution.py:345
  87.4 21.8 %collective-permute-start.5 = (f32[128,1024]{1,0:T(8,128)}, f32[128,1024]{1,0:T(8,128)S(1)}, u32[]{:S(2)}, u32[]{:S(2)}) collective-permute-start(f32[128,1024]{1,0:T(8,128)} %get-tuple-element.31), channel_id=1, source_target_pairs={{0,8},{1,9},{2,10},{3,11},{4,12},{5,13},{6,14},{7,15},{8,0},{9,1},... | collective-permute-start | bytes 1572872 | tf_op jit(solution)/shard_map/ppermute | solution.py:345
  89.5 19.8 %collective-permute-start.6 = (f32[128,1024]{1,0:T(8,128)S(1)}, f32[128,1024]{1,0:T(8,128)S(1)}, u32[]{:S(2)}, u32[]{:S(2)}) collective-permute-start(f32[128,1024]{1,0:T(8,128)S(1)} %get-tuple-element.32), channel_id=1, source_target_pairs={{0,12},{1,13},{2,14},{3,15},{4,0},{5,1},{6,2},{7,3},{8,4},{9,5},{1... | collective-permute-start | bytes 1572872 | tf_op jit(solution)/shard_map/ppermute | solution.py:345
